TPU v7x, 128 devices: a whole 4x4x4 slice. The times are simulated.
128 devices in a mesh: blk: 64 (over x_lo, y, z, core), rep: 2 (over x_hi).
Axes of the slice: x: 4 (x_hi: 2, x_lo: 2; x = x_hi * 2 + x_lo), y: 4, z: 4, core: 2. Of those that a mesh axis runs over, the one named last changes fastest.
Arguments:
- user_factors: float32 [65536, 256], P('blk'), may hold values from -4 to 4
- item_factors: float32 [32768, 256], P(('blk', 'rep')), may hold values from -4 to 4
- user_accum: float32 [65536, 256], P('blk'), may hold values from 0.05 to 0.5
- item_accum: float32 [32768, 256], P(('blk', 'rep')), may hold values from 0.05 to 0.5
- ratings: bfloat16 [64, 512, 128, 128], P('blk', 'rep'), may hold values from -16 to 16
- masks: bfloat16 [64, 512, 128, 128], P('blk', 'rep'), may hold values from -1 to 1
- tile_users: int32 [64, 512], P('blk', 'rep'), may hold values from 0 to 7
- tile_items: int32 [64, 512], P('blk', 'rep'), may hold values from 0 to 255, as said below
- tile_counts: int32 [64, 128], P('blk', 'rep'), may hold values from 1 to 4, as said below
Outputs:
- new_users: float32 [65536, 256], P('blk')
- new_items: float32 [32768, 256], P(('blk', 'rep'))
Inputs may be any that keep to these rules, and one draw needn't show every extreme that they name: Slots q with q // 4 = g name item blocks of owner (g % 64) * 2 + g // 64 of the 2-block owners, i.e. tile_items[s, q] // 2 equals that owner; the first slot of each group names the owner's last block. `tile_counts`: each slab has some group with all 4 slots live.
All inputs are finite; a program needn't handle non-finite values.
Results may differ from a plain program's by a relative error of at most 0.0053.
Values may be sent and summed in bfloat16 or wider, within the bound.
No kernel may reach another device: no remote copies, remote signals or barrier semaphores. Data moves between devices by JAX's collectives and lax.ppermute only.
A program may use at most 128 MiB of HBM per device.

v0:
```python
import jax
import jax.numpy as jnp
from jax import lax
from jax.sharding import PartitionSpec as P

learn_rate = 0.5
weight_decay = 0.1


def passed_along(block, axis, distance):
    devices = range(lax.axis_size(axis))
    route = [((i - distance) % len(devices), i) for i in devices]
    return lax.ppermute(block, axis, route)


def adagrad(param, squares, grad, num_slabs):
    step_grad = grad / num_slabs + weight_decay * param
    total = squares + step_grad * step_grad
    return param - learn_rate * step_grad / jnp.sqrt(total)


def body(
    user_factors,
    item_factors,
    user_accum,
    item_accum,
    ratings,
    masks,
    tile_users,
    tile_items,
    tile_counts,
):
    num_slabs = lax.axis_size("blk")
    position = lax.axis_index("blk")
    slot_count = tile_users.shape[1] // num_slabs
    tile_side = ratings.shape[-1]
    columns = user_factors.shape[1]
    item_blocks = item_factors.shape[0] // tile_side
    user_low = user_factors.astype(jnp.bfloat16).reshape(-1, tile_side, columns)
    user_blocks = user_low.shape[0]
    item_block = item_factors.astype(jnp.bfloat16).reshape(item_blocks, tile_side, columns)

    def tile_terms(item_rows, owner_index):
        first = owner_index * slot_count
        live_count = tile_counts[0, owner_index]
        rating_tile = lax.dynamic_slice_in_dim(ratings[0], first, slot_count, 0)
        weight_tile = lax.dynamic_slice_in_dim(masks[0], first, slot_count, 0)
        user_index = lax.dynamic_slice_in_dim(tile_users[0], first, slot_count, 0)
        item_index = lax.dynamic_slice_in_dim(tile_items[0], first, slot_count, 0) % item_blocks
        user_sel = user_low[user_index]
        item_sel = item_rows[item_index]
        predicted = jnp.einsum(
            "sur,sir->sui", user_sel, item_sel, preferred_element_type=jnp.float32
        )
        active = (jnp.arange(slot_count) < live_count).astype(jnp.float32)
        observed = jnp.maximum(weight_tile.astype(jnp.float32), 0.0)
        residual = (
            active[:, None, None] * observed * (predicted - rating_tile.astype(jnp.float32))
        ).astype(jnp.bfloat16)
        user_part = jnp.einsum(
            "sui,sir->sur", residual, item_sel, preferred_element_type=jnp.float32
        )
        item_part = jnp.einsum(
            "sui,sur->sir", residual, user_sel, preferred_element_type=jnp.float32
        )
        user_onehot = (user_index[:, None] == jnp.arange(user_blocks)[None, :]).astype(jnp.float32)
        item_onehot = (item_index[:, None] == jnp.arange(item_blocks)[None, :]).astype(jnp.float32)
        user_add = jnp.einsum(
            "sb,sur->bur", user_onehot, user_part, precision=lax.Precision.HIGHEST
        )
        item_add = jnp.einsum(
            "sk,sir->kir", item_onehot, item_part, precision=lax.Precision.HIGHEST
        )
        return (user_add, item_add)

    user_zero = jnp.zeros((user_blocks, tile_side, columns), jnp.float32)
    gathered_zero = jnp.zeros((num_slabs, item_blocks, tile_side, columns), jnp.float32)

    def visit(step, carry):
        item_rows, user_grad, gathered = carry
        owner_index = (position - step) % num_slabs
        user_add, item_add = tile_terms(item_rows, owner_index)
        gathered = lax.dynamic_update_slice(gathered, item_add[None], (owner_index, 0, 0, 0))
        item_rows = passed_along(item_rows, "blk", 1)
        return (item_rows, user_grad + user_add, gathered)

    item_rows, user_grad, gathered = lax.fori_loop(
        0, num_slabs, visit, (item_block, user_zero, gathered_zero)
    )
    item_grad = lax.psum_scatter(gathered, "blk", scatter_dimension=0, tiled=True)[0]
    user_grad = lax.psum(user_grad, "rep")
    new_users = adagrad(user_factors, user_accum, user_grad.reshape(user_factors.shape), num_slabs)
    new_items = adagrad(item_factors, item_accum, item_grad.reshape(item_factors.shape), num_slabs)
    return (new_users, new_items)


def solution(mesh):
    in_specs = (
        P("blk", None),
        P(("blk", "rep"), None),
        P("blk", None),
        P(("blk", "rep"), None),
        P("blk", "rep", None, None),
        P("blk", "rep", None, None),
        P("blk", "rep"),
        P("blk", "rep"),
        P("blk", "rep"),
    )
    out_specs = (P("blk", None), P(("blk", "rep"), None))
    return jax.shard_map(body, mesh=mesh, in_specs=in_specs, out_specs=out_specs, check_vma=False)
```

profile of v0, /device:TPU:2, one launch (start us, length us, event | category | flops | bytes accessed | tf_op | source)
XLA Modules:
  0.0 916.6 jit_solution(15803797107315170275)
XLA Ops:
  10.3 7.9 broadcast_in_dim.39.clone
  18.2 556.5 %while.21 = (s32[]{:T(128)}, bf16[2,128,256]{2,1,0:T(8,128)(2,1)S(1)}, f32[8,128,256]{2,0,1:T(8,128)S(1)}, f32[64,2,128,256]{3,2,1,0:T(8,128)}, s32[]{:T(128)}, ...) while((s32[]{:T(128)}, ...), condition=%wide.region_1.2_spmd.clone, body=%wide.region_0.1_spmd.clone.sunk | while | flops 117377208 | bytes 8528572 | solution.py:87
  42.9 1.4 collective-permute-done
  51.6 1.4 collective-permute-done
  60.3 1.4 collective-permute-done
  69.0 1.4 collective-permute-done
  77.7 1.4 collective-permute-done
  95.1 1.4 collective-permute-done
  103.8 1.4 collective-permute-done
  138.6 1.4 collective-permute-done
  147.3 1.4 collective-permute-done
  164.7 1.4 collective-permute-done
  173.3 1.4 collective-permute-done
  190.7 1.4 collective-permute-done
  199.4 1.4 collective-permute-done
  208.1 1.4 collective-permute-done
  216.8 1.4 collective-permute-done
  225.5 1.4 collective-permute-done
  234.2 1.4 collective-permute-done
  251.6 1.4 collective-permute-done
  269.0 1.4 collective-permute-done
  277.7 1.4 collective-permute-done
  286.4 1.4 collective-permute-done
  295.1 1.4 collective-permute-done
  312.5 1.4 collective-permute-done
  321.2 1.4 collective-permute-done
  329.9 1.4 collective-permute-done
  347.2 1.4 collective-permute-done
  364.6 1.4 collective-permute-done
  382.0 1.4 collective-permute-done
  390.7 1.4 collective-permute-done
  408.1 1.4 collective-permute-done
  416.8 1.4 collective-permute-done
  434.2 1.4 collective-permute-done
  442.9 1.4 collective-permute-done
  460.3 1.4 collective-permute-done
  469.0 1.4 collective-permute-done
  477.7 1.4 collective-permute-done
  486.4 1.4 collective-permute-done
  503.8 1.4 collective-permute-done
  512.5 1.4 collective-permute-done
  529.8 1.4 collective-permute-done
  538.5 1.4 collective-permute-done
  547.2 1.4 collective-permute-done
  555.9 1.4 collective-permute-done
  576.3 47.1 %all-reduce.2.cloned.1.call-done = f32[8,128,256]{2,0,1:T(8,128)} async-done(((f32[8,128,256]{2,0,1:T(8,128)}), f32[8,128,256]{2,0,1:T(8,128)}) %all-reduce.2.cloned.1.call-update) | async-done | bytes 1048592 | tf_op jit(solution)/shard_map/psum | solution.py:91
  626.3 280.2 %reduce-scatter.2.cloned.1.call-done = f32[1,2,128,256]{3,2,1,0:T(8,128)} async-done(((f32[64,2,128,256]{3,2,1,0:T(8,128)}), f32[1,2,128,256]{3,2,1,0:T(8,128)}) %reduce-scatter.2.cloned.1.call-update) | async-done | bytes 262160 | tf_op jit(solution)/shard_map/reduce_scatter | solution.py:90
  907.5 1.7 multiply_subtract_fusion.1
  (1134 shorter events, 497.4 us)
Async XLA Ops:
  8.0 615.3 %all-reduce.2.cloned.1.call-start = ((), (), s32[]{:S(2)}) async-start(), calls=%async_computation.1 | async-start | bytes 2097152 | tf_op jit(solution)/shard_map/psum | solution.py:91
  18.2 8.7 collective-permute-start
  26.9 8.7 collective-permute-start
  35.6 8.7 collective-permute-start
  44.3 8.7 collective-permute-start
  53.0 8.7 collective-permute-start
  61.7 8.7 collective-permute-start
  70.4 8.7 collective-permute-start
  79.1 8.7 collective-permute-start
  87.8 8.7 collective-permute-start
  96.5 8.7 collective-permute-start
  105.2 8.7 collective-permute-start
  113.9 8.7 collective-permute-start
  122.6 8.7 collective-permute-start
  131.3 8.7 collective-permute-start
  140.0 8.7 collective-permute-start
  148.7 8.7 collective-permute-start
  157.3 8.7 collective-permute-start
  183.4 8.7 collective-permute-start
  192.1 8.7 collective-permute-start
  200.8 8.7 collective-permute-start
  209.5 8.7 collective-permute-start
  235.6 8.7 collective-permute-start
  244.3 8.7 collective-permute-start
  253.0 8.7 collective-permute-start
  261.7 8.7 collective-permute-start
  287.8 8.7 collective-permute-start
  296.5 8.7 collective-permute-start
  305.2 8.7 collective-permute-start
  313.9 8.7 collective-permute-start
  348.6 8.7 collective-permute-start
  357.3 8.7 collective-permute-start
  366.0 8.7 collective-permute-start
  374.7 8.7 collective-permute-start
  400.8 8.7 collective-permute-start
  409.5 8.7 collective-permute-start
  418.2 8.7 collective-permute-start
  426.9 8.7 collective-permute-start
  453.0 8.7 collective-permute-start
  461.7 8.7 collective-permute-start
  470.4 8.7 collective-permute-start
  479.1 8.7 collective-permute-start
  513.8 8.7 collective-permute-start
  522.5 8.7 collective-permute-start
  531.2 8.7 collective-permute-start
  539.9 8.7 collective-permute-start
  566.0 8.7 collective-permute-start
  575.7 330.8 %reduce-scatter.2.cloned.1.call-start = ((), (), s32[]{:S(2)}) async-start(), calls=%async_computation.2 | async-start | bytes 17039360 | tf_op jit(solution)/shard_map/reduce_scatter | solution.py:90
  (25 other events, 621.2 us)
Sparse Core Ops, SparseCore 0:
  575.8 47.4 all-reduce.1
Sparse Core Ops, SparseCore 1:
  578.7 327.8 reduce-scatter.1
where the time goes:
time: 919 us; the launch traced here: 917 us
  waiting for transfers between devices  415 us (45%)
  matrix products  240 us (26%)
  local copies, waits for them, and re-layouts  174 us (19%)
  other arithmetic  58.4 us (6%)
  between operations  15.6 us (2%)
    reduce_scatter x1, waiting for transfers between devices, body(): lax.psum_scatter(gathered, 'blk', scatter_dimension=0, tiled=True)[0]  280 us
    ppermute x64, waiting for transfers between devices, passed_along(): return lax.ppermute(block, axis, route)  86.7 us
    dot_general x64, matrix products, tile_terms(): jnp.einsum('sur,sir->sui', user_sel, item_sel, preferred_element_type=jnp...  77 us
    dot_general x64, matrix products, tile_terms(): jnp.einsum('sb,sur->bur', user_onehot, user_part, precision=lax.Precision...  75.6 us
    dot_general x64, matrix products, tile_terms(): jnp.einsum('sk,sir->kir', item_onehot, item_part, precision=lax.Precision...  57 us
    psum x1, waiting for transfers between devices, body(): user_grad = lax.psum(user_grad, 'rep')  47.1 us
    dynamic_update_slice x64, local copies, waits for them, and re-layouts, visit(): lax.dynamic_update_slice(gathered, item_add[None], (owner_index, 0, 0, 0))  46.8 us
    dynamic_slice x64, local copies, waits for them, and re-layouts, tile_terms(): live_count = tile_counts[0, owner_index]  40.9 us
  transfers between devices with their start and end apart: 66, of which 66 were waited for; matrix products, arithmetic and copies ran while one was open for 50% of the time, Pallas kernels for 0%

commit v1 on v0

v1 whole, which is shorter than its diff:
```python
import jax
import jax.numpy as jnp
from jax import lax
from jax.experimental import pallas as pl
from jax.experimental.pallas import tpu as pltpu
from jax.sharding import PartitionSpec as P

learn_rate = 0.5
weight_decay = 0.1
TILE = 128
SLOTS = 4
CHUNK = 4


def adagrad(param, squares, grad, num_slabs):
    step_grad = grad / num_slabs + weight_decay * param
    total = squares + step_grad * step_grad
    return param - learn_rate * step_grad / jnp.sqrt(total)


def core_swap(block):
    devices = range(lax.axis_size("blk"))
    return lax.ppermute(block, "blk", [(i, i ^ 1) for i in devices])


def tile_kernel(
    core_ref,
    live_ref,
    users_ref,
    items_ref,
    own_ratings,
    own_masks,
    far_ratings,
    far_masks,
    item_rows,
    user_rows,
    user_cols,
    item_grad,
    user_grad,
    ratings,
    masks,
    sems,
):
    owners = item_rows.shape[0]
    chunks = owners // CHUNK
    core = core_ref[0]

    def copies(k):
        at = pl.ds(k * CHUNK, CHUNK)
        near, far = pl.ds(0, SLOTS), pl.ds(SLOTS, SLOTS)
        pairs = (
            (own_ratings.at[at, core], ratings.at[at, near]),
            (own_masks.at[at, core], masks.at[at, near]),
            (far_ratings.at[at], ratings.at[at, far]),
            (far_masks.at[at], masks.at[at, far]),
        )
        return [
            pltpu.make_async_copy(source, target, sems.at[k, i])
            for i, (source, target) in enumerate(pairs)
        ]

    for k in range(chunks):
        for copy in copies(k):
            copy.start()
    user_grad[...] = jnp.zeros_like(user_grad)

    def group(g, live_near, tiles):
        rows = item_rows[g]
        places = []
        for t in range(tiles):
            slot = jnp.where(t < live_near, t, t - live_near + SLOTS)
            block = users_ref[g * 2 * SLOTS + slot]
            within = items_ref[g * 2 * SLOTS + slot]
            places.append((slot, block, within))
        picked = jnp.concatenate([user_rows[block] for _, block, _ in places], 0)
        predicted = lax.dot_general(
            picked, rows, (((1,), (1,)), ((), ())), preferred_element_type=jnp.float32
        )
        wide = []
        for t, (slot, _, within) in enumerate(places):
            part = predicted[t * TILE : (t + 1) * TILE]
            second = within == 1
            chosen = jnp.where(second, part[:, TILE:], part[:, :TILE])
            observed = jnp.maximum(masks[g, slot].astype(jnp.float32), 0.0)
            residual = observed * (chosen - ratings[g, slot].astype(jnp.float32))
            wide.append(
                jnp.concatenate(
                    [jnp.where(second, 0.0, residual), jnp.where(second, residual, 0.0)], 1
                ).astype(jnp.bfloat16)
            )
        wide = jnp.concatenate(wide, 0)
        user_part = jnp.dot(wide, rows, preferred_element_type=jnp.float32)
        for t, (_, block, _) in enumerate(places):
            user_grad[block] += user_part[t * TILE : (t + 1) * TILE]
        turned = jnp.concatenate([user_cols[block] for _, block, _ in places], 1)
        item_grad[g] = jnp.dot(turned, wide, preferred_element_type=jnp.float32).astype(
            item_grad.dtype
        )

    def chunk(k, carry):
        for copy in copies(k):
            copy.wait()

        def one(i, carry):
            g = k * CHUNK + i
            live_near = live_ref[2 * g]
            live = live_near + live_ref[2 * g + 1]
            for tiles in range(2, 2 * SLOTS + 1):
                pl.when(live == tiles)(lambda tiles=tiles: group(g, live_near, tiles))
            return carry

        return lax.fori_loop(0, CHUNK, one, carry)

    lax.fori_loop(0, chunks, chunk, 0)


def tile_terms(
    core, live, users, items, ratings, masks, far_ratings, far_masks, item_rows, user_rows
):
    owners, rows, columns = item_rows.shape
    blocks = user_rows.shape[0]
    smem = pl.BlockSpec(memory_space=pltpu.SMEM)
    vmem = pl.BlockSpec(memory_space=pltpu.VMEM)
    far = pl.BlockSpec(memory_space=pl.ANY)
    return pl.pallas_call(
        tile_kernel,
        out_shape=(
            jax.ShapeDtypeStruct((owners, columns, rows), jnp.bfloat16),
            jax.ShapeDtypeStruct((blocks, TILE, columns), jnp.float32),
        ),
        in_specs=[smem] * 4 + [far] * 4 + [vmem] * 3,
        out_specs=(vmem, vmem),
        scratch_shapes=[
            pltpu.VMEM((owners, 2 * SLOTS, TILE, TILE), jnp.bfloat16),
            pltpu.VMEM((owners, 2 * SLOTS, TILE, TILE), jnp.bfloat16),
            pltpu.SemaphoreType.DMA((owners // CHUNK, 4)),
        ],
        compiler_params=pltpu.CompilerParams(vmem_limit_bytes=50 << 20),
        cost_estimate=pl.CostEstimate(
            flops=6 * owners * 5 * TILE * rows * columns,
            bytes_accessed=32 << 20,
            transcendentals=0,
        ),
    )(
        core,
        live.reshape(-1),
        users.reshape(-1),
        items.reshape(-1),
        ratings,
        masks,
        far_ratings,
        far_masks,
        item_rows,
        user_rows,
        user_rows.swapaxes(1, 2),
    )


def body(
    user_factors,
    item_factors,
    user_accum,
    item_accum,
    ratings,
    masks,
    tile_users,
    tile_items,
    tile_counts,
):
    num_slabs = lax.axis_size("blk")
    columns = user_factors.shape[1]
    owners = num_slabs // 2
    core = lax.axis_index("blk") % 2
    same_core = [[j for j in range(num_slabs) if j % 2 == c] for c in range(2)]

    item_low = item_factors.astype(jnp.bfloat16)
    user_low = user_factors.astype(jnp.bfloat16).reshape(-1, TILE, columns)
    blocks = user_low.shape[0]
    ratings = ratings.reshape(owners, 2, SLOTS, TILE, TILE)
    masks = masks.reshape(owners, 2, SLOTS, TILE, TILE)
    index = jnp.concatenate(
        [
            tile_counts.reshape(owners, 2, 1),
            tile_users.reshape(owners, 2, SLOTS),
            tile_items.reshape(owners, 2, SLOTS) % 2,
        ],
        2,
    )

    def split(array):
        return (
            lax.dynamic_index_in_dim(array, core, 1, keepdims=False),
            core_swap(lax.dynamic_index_in_dim(array, 1 - core, 1, keepdims=False)),
        )

    near, far = split(index)
    live = jnp.stack([near[:, 0], far[:, 0]], 1)
    users = jnp.concatenate([near[:, 1 : 1 + SLOTS], far[:, 1 : 1 + SLOTS] + blocks], 1)
    items = jnp.concatenate([near[:, 1 + SLOTS :], far[:, 1 + SLOTS :]], 1)
    far_ratings = split(ratings)[1]
    far_masks = split(masks)[1]
    user_rows = jnp.concatenate([user_low, core_swap(user_low)], 0)

    item_rows = lax.all_to_all(
        jnp.broadcast_to(item_low, (owners,) + item_low.shape),
        "blk",
        0,
        0,
        axis_index_groups=same_core,
        tiled=True,
    )
    item_grad, user_grad = tile_terms(
        core[None].astype(jnp.int32),
        live,
        users,
        items,
        ratings,
        masks,
        far_ratings,
        far_masks,
        item_rows,
        user_rows,
    )
    far_grad = core_swap(user_grad[blocks:].astype(jnp.bfloat16))
    half = (user_grad[:blocks] + far_grad.astype(jnp.float32)).astype(jnp.bfloat16)
    other = lax.ppermute(half, "rep", [(0, 1), (1, 0)])
    user_sum = half.astype(jnp.float32) + other.astype(jnp.float32)
    item_parts = lax.all_to_all(
        item_grad, "blk", 0, 0, axis_index_groups=same_core, tiled=True
    )
    item_sum = jnp.sum(item_parts.astype(jnp.float32), 0).T
    new_users = adagrad(user_factors, user_accum, user_sum.reshape(user_factors.shape), num_slabs)
    new_items = adagrad(item_factors, item_accum, item_sum, num_slabs)
    return (new_users, new_items)


def solution(mesh):
    in_specs = (
        P("blk", None),
        P(("blk", "rep"), None),
        P("blk", None),
        P(("blk", "rep"), None),
        P("blk", "rep", None, None),
        P("blk", "rep", None, None),
        P("blk", "rep"),
        P("blk", "rep"),
        P("blk", "rep"),
    )
    out_specs = (P("blk", None), P(("blk", "rep"), None))
    return jax.shard_map(body, mesh=mesh, in_specs=in_specs, out_specs=out_specs, check_vma=False)
```

time: 919 us -> 194 us (0.21)
  waiting for transfers between devices: 415 us -> 115 us
  matrix products: 240 us -> 0 us
  local copies, waits for them, and re-layouts: 174 us -> 16.8 us
  other arithmetic: 58.4 us -> 9.99 us
  Pallas kernels: 0 us -> 29.1 us
  between operations: 15.6 us -> 0.9 us
  starting transfers between devices: 5.48 us -> 18.5 us
    reduce_scatter x1 -> x0, waiting for transfers between devices: 280 us -> none  [body(): lax.psum_scatter(gathered, 'blk', scatter_dimension=0, tiled=True)[0]]
    dot_general x320 -> x0, matrix products: 240 us -> none  [the longest x64 77 us: tile_terms(): jnp.einsum('sur,sir->sui', user_sel, item_sel, preferred_element_type=jnp...]
    gather x128 -> x0, local copies, waits for them, and re-layouts: 72.2 us -> none  [the longest x64 36.1 us: tile_terms(): item_sel = item_rows[item_index]]
    all_to_all x0 -> x2, waiting for transfers between devices: none -> 55.6 us  [the longest x1 55.5 us: body(): lax.all_to_all(jnp.broadcast_to(item_low, (owners,) + item_low.shape), 'b...]
    psum x1 -> x0, waiting for transfers between devices: 47.1 us -> none  [body(): user_grad = lax.psum(user_grad, 'rep')]
    dynamic_update_slice x64 -> x0, local copies, waits for them, and re-layouts: 46.8 us -> none  [visit(): lax.dynamic_update_slice(gathered, item_add[None], (owner_index, 0, 0, 0))]
    dynamic_slice x64 -> x1, local copies, waits for them, and re-layouts: 40.9 us -> 0.02 us  [split(): lax.dynamic_index_in_dim(array, core, 1, keepdims=False)]
    convert_element_type x66 -> x3, other arithmetic: 42.1 us -> 1.42 us  [the longest x1 1.35 us: body(): (user_grad[:blocks] + far_grad.astype(jnp.float32)).astype(jnp.bfloat16)]
  transfers between devices with their start and end apart: 66 -> 8, of which waited for: 66 -> 5; matrix products, arithmetic and copies ran while one was open for 50% -> 9% of each run, Pallas kernels for 0% -> 0%
where the time goes in v1:
time: 194 us; the launch traced here: 190 us
  waiting for transfers between devices  115 us (59%)
  Pallas kernels  29.1 us (15%)
  starting transfers between devices  18.5 us (10%)
  local copies, waits for them, and re-layouts  16.8 us (9%)
  other arithmetic  9.99 us (5%)
    ppermute x1, waiting for transfers between devices, body(): other = lax.ppermute(half, 'rep', [(0, 1), (1, 0)])  56.7 us
    all_to_all x1, waiting for transfers between devices, body(): lax.all_to_all(jnp.broadcast_to(item_low, (owners,) + item_low.shape), 'b...  55.5 us
    pallas_call x1, Pallas kernels, tile_terms(): pl.pallas_call(tile_kernel, out_shape=(jax.ShapeDtypeStruct((owners, colu...  29.1 us
    all_to_all x1, starting transfers between devices, body(): lax.all_to_all(jnp.broadcast_to(item_low, (owners,) + item_low.shape), 'b...  9.77 us
    squeeze x2, local copies, waits for them, and re-layouts, split(): lax.dynamic_index_in_dim(array, 1 - core, 1, keepdims=False)  7.32 us
    all_to_all x1, starting transfers between devices, body(): lax.all_to_all(item_grad, 'blk', 0, 0, axis_index_groups=same_core, tiled...  4.65 us
  transfers between devices with their start and end apart: 8, of which 5 were waited for; matrix products, arithmetic and copies ran while one was open for 9% of the time, Pallas kernels for 0%

profile of v1, /device:TPU:2, one launch (start us, length us, event | category | flops | bytes accessed | tf_op | source)
XLA Modules:
  0.0 190.5 jit_solution(13796519829657404627)
XLA Ops:
  0.7 5.1 %dynamic-slice_bitcast_fusion.1 = bf16[32,4,128,128]{3,2,1,0:T(8,128)(2,1)} fusion(bf16[32,2,4,128,128]{4,3,2,1,0:T(8,128)(2,1)} %bitcast.24, s32[]{:T(128)S(6)} %select_n.26), kind=kLoop, calls=%fused_computation.2 | loop fusion | bytes 8388612 | tf_op jit(solution)/shard_map/jit(dynamic_index_in_dim)/squeeze | solution.py:193
  5.7 1.1 copy-done
  6.8 2.3 %dynamic-slice_bitcast_fusion = bf16[32,4,128,128]{3,2,1,0:T(8,128)(2,1)} fusion(bf16[32,2,4,128,128]{4,3,2,1,0:T(8,128)(2,1)S(1)} %bitcast.27, s32[]{:T(128)S(6)} %select_n.26), kind=kLoop, calls=%fused_computation.1 | loop fusion | bytes 8388612 | tf_op jit(solution)/shard_map/jit(dynamic_index_in_dim)/squeeze | solution.py:193
  9.1 2.4 %broadcast_in_dim.7 = bf16[32,256,256]{2,1,0:T(8,128)(2,1)} broadcast(bf16[256,256]{1,0:T(8,128)(2,1)S(1)} %convert_element_type.22), dimensions={1,2} | broadcast | bytes 4325376 | tf_op jit(solution)/shard_map/broadcast_in_dim | solution.py:205
  11.5 9.8 %all-to-all-start = ((bf16[32,256,256]{2,1,0:T(8,128)(2,1)}), bf16[32,256,256]{2,1,0:T(8,128)(2,1)}, u32[]{:S(2)}, u32[]{:S(2)}) async-start(bf16[32,256,256]{2,1,0:T(8,128)(2,1)} %broadcast_in_dim.7), calls=%async_computation | async-start | bytes 8388608 | tf_op jit(solution)/shard_map/all_to_all | solution.py:204
  21.3 0.5 broadcast.24
  21.8 0.7 reduce.9
  22.5 0.1 reshape.36
  22.6 0.1 and_select_fusion
  22.7 0.1 copy.19
  22.8 0.7 reduce.10
  23.4 0.1 reshape.35
  23.6 0.1 copy.18
  23.7 0.7 reduce.11
  24.3 0.1 reshape.34
  24.4 0.1 copy.17
  24.6 0.1 collective-permute-start
  24.7 0.1 convert_element_type.23
  24.7 0.3 copy.24
  25.0 0.6 collective-permute-start.3
  25.6 0.2 collective-permute-done
  25.8 0.1 copy.21
  25.9 0.1 reshape.38.users_ref
  26.0 0.1 copy.22
  26.1 0.1 reshape.39.items_ref
  26.2 0.1 copy.20
  26.3 0.1 reshape.37.live_ref
  26.4 0.8 collective-permute-done.3
  27.2 1.2 fusion.1
  28.4 0.5 copy.25.user_rows
  29.0 55.5 %all-to-all-done.item_rows = bf16[32,256,256]{2,1,0:T(8,128)(2,1)} async-done(((bf16[32,256,256]{2,1,0:T(8,128)(2,1)}), bf16[32,256,256]{2,1,0:T(8,128)(2,1)}, u32[]{:S(2)}, u32[]{:S(2)}) %all-to-all-start) | async-done | bytes 4194336 | tf_op jit(solution)/shard_map/all_to_all | solution.py:204
  84.5 29.1 %shard_map.104 = (bf16[32,256,256]{2,1,0:T(8,128)(2,1)}, f32[16,128,256]{2,1,0:T(8,128)}) custom-call(s32[1]{0:T(128)} %bitcast.core_ref, s32[64]{0:T(128)S(1)} %reshape.37.live_ref, s32[256]{0:T(256)S(1)} %reshape.38.users_ref, s32[256]{0:T(256)S(1)} %reshape.39.items_ref, bf16[32,2,4,128,128]{4,3,2,1,0:T(8,128)(2,1)} %bitcast.25, ...), custom_call_target="tpu_custom_call" | custom-call | flops 8053063680 | bytes 33554432 | tf_op jit(solution)/shard_map/pallas_call | solution.py:125
  113.6 4.7 %all-to-all-start.1 = ((bf16[32,256,256]{2,1,0:T(8,128)(2,1)}), bf16[32,256,256]{2,1,0:T(8,128)(2,1)}, u32[]{:S(2)}, u32[]{:S(2)}) async-start(bf16[32,256,256]{2,1,0:T(8,128)(2,1)} %get-tuple-element.5), calls=%async_computation.1 | async-start | bytes 8388608 | tf_op jit(solution)/shard_map/all_to_all | solution.py:228
  118.3 0.0 copy-start.2
  118.3 0.0 copy-start.4
  118.3 1.4 slice.43
  119.8 0.1 collective-permute-start.4
  119.9 1.9 collective-permute-done.4
  121.8 1.3 add_convert_fusion
  123.1 3.3 %collective-permute-start.5 = (bf16[8,128,256]{2,1,0:T(8,128)(2,1)S(1)}, bf16[8,128,256]{2,1,0:T(8,128)(2,1)}, u32[]{:S(2)}, u32[]{:S(2)}) collective-permute-start(bf16[8,128,256]{2,1,0:T(8,128)(2,1)S(1)} %add_convert_fusion), channel_id=1, source_target_pairs={{0,1},{1,0},{2,3},{3,2},{4,5},{5,4},{6,7},{7,6},{8,9},{9,8},{10,11... | collective-permute-start | bytes 1572872 | tf_op jit(solution)/shard_map/ppermute | solution.py:226
  126.4 0.1 copy.28
  126.5 1.1 copy.27
  127.6 56.7 %collective-permute-done.5 = bf16[8,128,256]{2,1,0:T(8,128)(2,1)} collective-permute-done((bf16[8,128,256]{2,1,0:T(8,128)(2,1)S(1)}, bf16[8,128,256]{2,1,0:T(8,128)(2,1)}, u32[]{:S(2)}, u32[]{:S(2)}) %collective-permute-start.5) | collective-permute-done | bytes 524320 | tf_op jit(solution)/shard_map/ppermute | solution.py:226
  184.3 1.2 add_multiply_fusion
  185.5 1.2 multiply_subtract_fusion
  186.8 2.8 %convert_reduce_fusion = f32[256,256]{1,0:T(8,128)S(1)} fusion(bf16[32,256,256]{2,1,0:T(8,128)(2,1)} %all-to-all-done.1), kind=kLoop, calls=%fused_computation | loop fusion | flops 4128768 | bytes 4456448 | tf_op jit(solution)/shard_map/reduce_sum | solution.py:231
  189.6 0.1 multiply_subtract_fusion.1
  189.7 0.8 copy.29
  (29 shorter events, 0.1 us)
Async XLA Ops:
  0.6 6.2 %copy-start = (bf16[1,256,128,128]{3,2,1,0:T(8,128)(2,1)S(1)}, bf16[1,256,128,128]{3,2,1,0:T(8,128)(2,1)}, u32[]{:S(2)}) copy-start(bf16[1,256,128,128]{3,2,1,0:T(8,128)(2,1)} %param.14) | copy-start | bytes 25165828
  5.7 78.8 %collective-permute-start.1 = (bf16[32,4,128,128]{3,2,1,0:T(8,128)(2,1)}, bf16[32,4,128,128]{3,2,1,0:T(8,128)(2,1)}, u32[]{:S(2)}, u32[]{:S(2)}) collective-permute-start(bf16[32,4,128,128]{3,2,1,0:T(8,128)(2,1)} %dynamic-slice_bitcast_fusion.1), channel_id=1, source_target_pairs={{0,2},{2,0},{4,6},{6,4},{8,10},{10,8},{12,14},{14,12},{16,18},{18,... | collective-permute-start | bytes 12582920 | tf_op jit(solution)/shard_map/ppermute | solution.py:23
  6.8 2.3 %copy-start.3 = (f32[256,256]{1,0:T(8,128)S(1)}, f32[256,256]{1,0:T(8,128)}, u32[]{:S(2)}) copy-start(f32[256,256]{1,0:T(8,128)} %param.10) | copy-start | bytes 786436
  9.1 75.5 %collective-permute-start.2 = (bf16[32,4,128,128]{3,2,1,0:T(8,128)(2,1)}, bf16[32,4,128,128]{3,2,1,0:T(8,128)(2,1)}, u32[]{:S(2)}, u32[]{:S(2)}) collective-permute-start(bf16[32,4,128,128]{3,2,1,0:T(8,128)(2,1)} %dynamic-slice_bitcast_fusion), channel_id=1, source_target_pairs={{0,2},{2,0},{4,6},{6,4},{8,10},{10,8},{12,14},{14,12},{16,18},{18,... | collective-permute-start | bytes 12582920 | tf_op jit(solution)/shard_map/ppermute | solution.py:23
  11.5 10.3 %copy-start.5 = (s32[1,256]{1,0:T(1,128)S(1)}, s32[1,256]{1,0:T(1,128)}, u32[]{:S(2)}) copy-start(s32[1,256]{1,0:T(1,128)} %param.16) | copy-start | bytes 3076
  11.5 11.2 %copy-start.6 = (s32[1,256]{1,0:T(1,128)S(1)}, s32[1,256]{1,0:T(1,128)}, u32[]{:S(2)}) copy-start(s32[1,256]{1,0:T(1,128)} %param.15) | copy-start | bytes 3076
  11.5 12.1 %copy-start.7 = (s32[1,64]{1,0:T(1,128)S(1)}, s32[1,64]{1,0:T(1,128)}, u32[]{:S(2)}) copy-start(s32[1,64]{1,0:T(1,128)} %param.17) | copy-start | bytes 772
  11.5 13.1 %copy-start.1 = (f32[1024,256]{1,0:T(8,128)S(1)}, f32[1024,256]{1,0:T(8,128)}, u32[]{:S(2)}) copy-start(f32[1024,256]{1,0:T(8,128)} %param.9) | copy-start | bytes 3145732
  11.5 73.0 %all-to-all-start = ((bf16[32,256,256]{2,1,0:T(8,128)(2,1)}), bf16[32,256,256]{2,1,0:T(8,128)(2,1)}, u32[]{:S(2)}, u32[]{:S(2)}) async-start(bf16[32,256,256]{2,1,0:T(8,128)(2,1)} %broadcast_in_dim.7), calls=%async_computation | async-start | bytes 8388608 | tf_op jit(solution)/shard_map/all_to_all | solution.py:204
  24.6 1.3 collective-permute-start
  25.0 2.2 %collective-permute-start.3 = (bf16[8,128,256]{1,2,0:T(8,128)(2,1)S(1)}, bf16[8,128,256]{1,2,0:T(8,128)(2,1)}, u32[]{:S(2)}, u32[]{:S(2)}) collective-permute-start(bf16[8,128,256]{1,2,0:T(8,128)(2,1)S(1)} %copy.24), channel_id=1, source_target_pairs={{0,2},{2,0},{4,6},{6,4},{8,10},{10,8},{12,14},{14,12},{16,18},{18,... | collective-permute-start | bytes 1572872 | tf_op jit(solution)/shard_map/ppermute | solution.py:23
  113.6 73.1 %all-to-all-start.1 = ((bf16[32,256,256]{2,1,0:T(8,128)(2,1)}), bf16[32,256,256]{2,1,0:T(8,128)(2,1)}, u32[]{:S(2)}, u32[]{:S(2)}) async-start(bf16[32,256,256]{2,1,0:T(8,128)(2,1)} %get-tuple-element.5), calls=%async_computation.1 | async-start | bytes 8388608 | tf_op jit(solution)/shard_map/all_to_all | solution.py:228
  118.3 67.2 %copy-start.2 = (f32[1024,256]{1,0:T(8,128)S(1)}, f32[1024,256]{1,0:T(8,128)}, u32[]{:S(2)}) copy-start(f32[1024,256]{1,0:T(8,128)} %param.9) | copy-start | bytes 3145732
  118.3 67.2 %copy-start.4 = (f32[1024,256]{1,0:T(8,128)S(1)}, f32[1024,256]{1,0:T(8,128)}, u32[]{:S(2)}) copy-start(f32[1024,256]{1,0:T(8,128)} %param.11) | copy-start | bytes 3145732
  119.8 2.0 %collective-permute-start.4 = (bf16[8,128,256]{2,1,0:T(8,128)(2,1)S(1)}, bf16[8,128,256]{2,1,0:T(8,128)(2,1)S(1)}, u32[]{:S(2)}, u32[]{:S(2)}) collective-permute-start(bf16[8,128,256]{2,1,0:T(8,128)(2,1)S(1)} %slice.43), channel_id=1, source_target_pairs={{0,2},{2,0},{4,6},{6,4},{8,10},{10,8},{12,14},{14,12},{16,18},{18,... | collective-permute-start | bytes 1572872 | tf_op jit(solution)/shard_map/ppermute | solution.py:23
  123.1 61.2 %collective-permute-start.5 = (bf16[8,128,256]{2,1,0:T(8,128)(2,1)S(1)}, bf16[8,128,256]{2,1,0:T(8,128)(2,1)}, u32[]{:S(2)}, u32[]{:S(2)}) collective-permute-start(bf16[8,128,256]{2,1,0:T(8,128)(2,1)S(1)} %add_convert_fusion), channel_id=1, source_target_pairs={{0,1},{1,0},{2,3},{3,2},{4,5},{5,4},{6,7},{7,6},{8,9},{9,8},{10,11... | collective-permute-start | bytes 1572872 | tf_op jit(solution)/shard_map/ppermute | solution.py:226

commit v2 on v0

v2 whole, which is shorter than its diff:
```python
import jax
import jax.numpy as jnp
from jax import lax
from jax.experimental import pallas as pl
from jax.experimental.pallas import tpu as pltpu
from jax.sharding import PartitionSpec as P

learn_rate = 0.5
weight_decay = 0.1
TILE = 128
SLOTS = 4
XS, YS, ZS, CORES = 2, 4, 4, 2
RING = 4
HALF = RING // 2
PAIR = 2


def place(index):
    return (
        index // (YS * ZS * CORES),
        index // (ZS * CORES) % YS,
        index // CORES % ZS,
        index % CORES,
    )


def moved(index, way):
    at = [(a + d) % n for a, d, n in zip(place(index), way, (XS, YS, ZS, CORES))]
    return ((at[0] * YS + at[1]) * ZS + at[2]) * CORES + at[3]


def fetch(block, x=0, y=0, z=0, core=0):
    count = XS * YS * ZS * CORES
    route = [(moved(i, (x, y, z, core)), i) for i in range(count)]
    return lax.ppermute(block, "blk", route)


def adagrad(param, squares, grad, num_slabs):
    step_grad = grad / num_slabs + weight_decay * param
    total = squares + step_grad * step_grad
    return param - learn_rate * step_grad / jnp.sqrt(total)


def owner_at(here, part, step, lane):
    x, y, z, _ = here
    if part == 0:
        return (x * YS + (y + lane) % YS) * ZS + (z + step) % ZS
    return ((1 - x) * YS + (y + step) % YS) * ZS + (z + lane) % ZS


def tile_kernel(pieces, outs, *refs):
    size = len(pieces)
    device_ref, near_ref, far_ref, own_ratings, own_masks = refs[:5]
    far_tiles = refs[5]
    item_rows = refs[6 : 6 + size]
    user_rows, user_cols = refs[6 + size : 8 + size]
    item_out = refs[8 + size : 8 + size + len(outs)]
    user_grad = refs[8 + size + len(outs)]
    owners_ref, rows_ref, grads_ref, ratings, masks, tile_sems, row_sems, out_sems = refs[
        9 + size + len(outs) :
    ]
    here = place(device_ref[0])
    core = here[3]
    blocks = user_rows.shape[0] // 2
    item_at = own_ratings.shape[0] * CORES * SLOTS
    count_at = 2 * item_at
    plane_size = YS * ZS
    total = rows_ref.shape[0]

    def tile_copies(n, far_of):
        owner = owners_ref[n]
        near, far = pl.ds(0, SLOTS), pl.ds(SLOTS, SLOTS)
        pairs = (
            (own_ratings.at[owner, core], ratings.at[n, near]),
            (own_masks.at[owner, core], masks.at[n, near]),
            (far_tiles.at[far_of, 0, owner % plane_size], ratings.at[n, far]),
            (far_tiles.at[far_of, 1, owner % plane_size], masks.at[n, far]),
        )
        return [
            pltpu.make_async_copy(source, target, tile_sems.at[n, i])
            for i, (source, target) in enumerate(pairs)
        ]

    row_copies, at = [], 0
    for a, (part, step, first, lanes) in enumerate(pieces):
        row_copies.append(
            pltpu.make_async_copy(item_rows[a], rows_ref.at[pl.ds(at, lanes)], row_sems.at[a])
        )
        row_copies[-1].start()
        for lane in range(lanes):
            owners_ref[at + lane] = owner_at(here, part, step, first + lane)
            for copy in tile_copies(at + lane, part):
                copy.start()
        at += lanes
    out_copies = [
        pltpu.make_async_copy(grads_ref.at[pl.ds(b * RING, RING)], item_out[b], out_sems.at[b])
        for b in range(len(outs))
    ]
    user_grad[...] = jnp.zeros_like(user_grad)
    for copy in row_copies:
        copy.wait()

    def predict(n, live, tiles):
        rows = rows_ref[n]
        first = (owners_ref[n] * CORES + core) * SLOTS
        places = []
        for t in range(tiles):
            far = t >= live[0]
            slot = jnp.where(far, jnp.minimum(t - live[0], SLOTS - 1), t)
            at = first + slot
            block = jnp.where(far, far_ref[0, at] + blocks, near_ref[0, at])
            within = jnp.where(far, far_ref[0, item_at + at], near_ref[0, item_at + at]) % 2
            alive = t < live[0] + live[1]
            places.append((jnp.where(far, slot + SLOTS, slot), block, within, alive))
        picked = jnp.concatenate([user_rows[block] for _, block, _, _ in places], 0)
        predicted = lax.dot_general(
            picked, rows, (((1,), (1,)), ((), ())), preferred_element_type=jnp.float32
        )
        return places, rows, predicted

    def residuals(n, places, predicted):
        wide = []
        for t, (slot, _, within, alive) in enumerate(places):
            part = predicted[t * TILE : (t + 1) * TILE]
            second = within == 1
            chosen = jnp.where(second, part[:, TILE:], part[:, :TILE])
            observed = jnp.maximum(masks[n, slot].astype(jnp.float32), 0.0)
            residual = observed * (chosen - ratings[n, slot].astype(jnp.float32))
            residual = residual.astype(jnp.bfloat16)
            none = jnp.zeros_like(residual)
            low = jnp.where(jnp.logical_and(alive, within == 0), residual, none)
            high = jnp.where(jnp.logical_and(alive, second), residual, none)
            wide.append(jnp.concatenate([low, high], 1))
        return jnp.concatenate(wide, 0)

    def together(entries, lives, tiles):
        firsts = [predict(n, live, tiles) for n, live in zip(entries, lives)]
        wides = [
            residuals(n, places, predicted)
            for n, (places, _, predicted) in zip(entries, firsts)
        ]
        user_parts = []
        for n, (places, rows, _), wide in zip(entries, firsts, wides):
            user_parts.append(jnp.dot(wide, rows, preferred_element_type=jnp.float32))
            turned = jnp.concatenate([user_cols[block] for _, block, _, _ in places], 1)
            grads_ref[n] = jnp.dot(turned, wide, preferred_element_type=jnp.float32).astype(
                jnp.bfloat16
            )
        for (places, _, _), user_part in zip(firsts, user_parts):
            for t, (_, block, _, _) in enumerate(places):
                user_grad[block] += user_part[t * TILE : (t + 1) * TILE]

    def some(i, carry):
        entries = [i * PAIR + k for k in range(PAIR)]
        lives = []
        for n in entries:
            for copy in tile_copies(n, 0):
                copy.wait()
            at = count_at + owners_ref[n] * CORES + core
            lives.append((near_ref[0, at], far_ref[0, at]))
        most = jnp.maximum(*[live[0] + live[1] for live in lives])
        for tiles in range(2, 2 * SLOTS + 1):
            pl.when(most == tiles)(lambda tiles=tiles: together(entries, lives, tiles))
        for b, copy in enumerate(out_copies):
            pl.when(i == (b + 1) * (RING // PAIR) - 1)(copy.start)
        return carry

    lax.fori_loop(0, total // PAIR, some, 0)
    for copy in out_copies:
        copy.wait()


def tile_terms(pieces, outs, device, near, far, own_tiles, far_tiles, item_rows, user_rows, user_cols):
    _, rows, columns = item_rows[0].shape
    blocks = user_rows.shape[0]
    total = sum(piece[3] for piece in pieces)
    smem = pl.BlockSpec(memory_space=pltpu.SMEM)
    vmem = pl.BlockSpec(memory_space=pltpu.VMEM)
    hbm = pl.BlockSpec(memory_space=pltpu.HBM)
    anywhere = pl.BlockSpec(memory_space=pl.ANY)

    def kernel(*refs):
        tile_kernel(pieces, outs, *refs)

    result = pl.pallas_call(
        kernel,
        out_shape=[jax.ShapeDtypeStruct((RING, columns, rows), jnp.bfloat16)] * len(outs)
        + [jax.ShapeDtypeStruct((blocks, TILE, columns), jnp.float32)],
        in_specs=[smem] * 3 + [hbm] * 2 + [anywhere] * (1 + len(pieces)) + [vmem] * 2,
        out_specs=[anywhere] * len(outs) + [vmem],
        scratch_shapes=[
            pltpu.SMEM((total,), jnp.int32),
            pltpu.VMEM((total, rows, columns), jnp.bfloat16),
            pltpu.VMEM((total, columns, rows), jnp.bfloat16),
            pltpu.VMEM((total, 2 * SLOTS, TILE, TILE), jnp.bfloat16),
            pltpu.VMEM((total, 2 * SLOTS, TILE, TILE), jnp.bfloat16),
            pltpu.SemaphoreType.DMA((total, 4)),
            pltpu.SemaphoreType.DMA((len(pieces),)),
            pltpu.SemaphoreType.DMA((len(outs),)),
        ],
        compiler_params=pltpu.CompilerParams(vmem_limit_bytes=32 << 20),
        cost_estimate=pl.CostEstimate(
            flops=total * (3 << 28), bytes_accessed=total << 20, transcendentals=0
        ),
    )(device, near, far, *own_tiles, far_tiles, *item_rows, user_rows, user_cols)
    return result[: len(outs)], result[len(outs)]


def in_hbm(array):
    return pltpu.with_memory_space_constraint(array, pltpu.HBM)


def pack_kernel(device_ref, ratings, masks, out, sems):
    x, _, _, core = place(device_ref[0])
    copies = [
        pltpu.make_async_copy(
            array.at[plane, :, 1 - core], out.at[part, kind], sems.at[part, kind]
        )
        for part, plane in enumerate((x, 1 - x))
        for kind, array in enumerate((ratings, masks))
    ]
    for copy in copies:
        copy.start()
    for copy in copies:
        copy.wait()


def packed_tiles(device, ratings, masks):
    lanes = YS * ZS
    shape = (XS, lanes, CORES, SLOTS, TILE, TILE)
    hbm = pl.BlockSpec(memory_space=pltpu.HBM)
    return pl.pallas_call(
        pack_kernel,
        out_shape=jax.ShapeDtypeStruct((2, 2, lanes, SLOTS, TILE, TILE), jnp.bfloat16),
        in_specs=[pl.BlockSpec(memory_space=pltpu.SMEM), hbm, hbm],
        out_specs=pl.BlockSpec(memory_space=pltpu.VMEM),
        scratch_shapes=[pltpu.SemaphoreType.DMA((2, 2))],
        compiler_params=pltpu.CompilerParams(vmem_limit_bytes=16 << 20),
        cost_estimate=pl.CostEstimate(flops=0, bytes_accessed=16 << 20, transcendentals=0),
    )(device, *[in_hbm(array.reshape(shape)) for array in (ratings, masks)])


def added(*terms):
    return sum(term.astype(jnp.float32) for term in terms)


def body(
    user_factors,
    item_factors,
    user_accum,
    item_accum,
    ratings,
    masks,
    tile_users,
    tile_items,
    tile_counts,
):
    low = jnp.bfloat16
    num_slabs = lax.axis_size("blk")
    columns = user_factors.shape[1]
    owners = num_slabs // CORES
    device = lax.axis_index("blk")

    item_low = item_factors.astype(low)
    own_line = [item_low] + [fetch(item_low, y=d) for d in range(1, RING)]
    far_line = [fetch(item_low, x=1, z=d) for d in range(RING)]

    near = jnp.concatenate([tile_users, tile_items, tile_counts], 1)
    far = fetch(near, core=1)
    user_low = user_factors.astype(low).reshape(-1, TILE, columns)
    blocks = user_low.shape[0]
    far_rows = fetch(user_low, core=1)
    start, far, far_rows = lax.optimization_barrier((device[None], far, far_rows))
    packed = packed_tiles(start, ratings, masks)
    user_rows = jnp.concatenate([user_low, far_rows], 0)

    far_tiles = fetch(packed, core=1)
    own_line, far_line, user_rows = lax.optimization_barrier((own_line, far_line, user_rows))
    user_cols = user_rows.swapaxes(1, 2)
    rows = [jnp.stack(own_line), jnp.stack(far_line)]
    ahead = [fetch(rows[0], z=1), fetch(rows[1], y=1)]
    behind = [fetch(rows[0], z=-1), fetch(rows[1], y=-1)]

    def terms(pieces, outs, item_rows):
        return tile_terms(
            pieces,
            outs,
            device[None],
            near,
            far,
            [in_hbm(a.reshape(owners, CORES, SLOTS, TILE, TILE)) for a in (ratings, masks)],
            far_tiles,
            item_rows,
            user_rows,
            user_cols,
        )

    here_terms, user_first = terms(
        ((0, 0, 0, RING), (1, 0, 0, RING)), ((0, 0), (1, 0)), rows
    )
    ahead, behind, here_terms, user_first = lax.optimization_barrier(
        (ahead, behind, here_terms, user_first)
    )
    across = [
        [fetch(ahead[0][:HALF], z=1), fetch(behind[0][HALF:], z=-1)],
        [fetch(ahead[1][:HALF], y=1), fetch(behind[1][HALF:], y=-1)],
    ]
    near_terms, user_second = terms(
        ((0, 1, 0, RING), (1, 1, 0, RING), (0, 3, 0, RING), (1, 3, 0, RING)),
        ((0, 1), (1, 1), (0, 3), (1, 3)),
        [ahead[0], ahead[1], behind[0], behind[1]],
    )
    across_terms, user_third = terms(
        ((0, 2, 0, HALF), (0, 2, HALF, HALF), (1, 2, 0, HALF), (1, 2, HALF, HALF)),
        ((0, 2), (1, 2)),
        across[0] + across[1],
    )

    arrived = [
        [fetch(near_terms[0], z=-1), fetch(near_terms[2], z=1)],
        [fetch(near_terms[1], y=-1), fetch(near_terms[3], y=1)],
    ]
    arrived, across_terms = lax.optimization_barrier((arrived, across_terms))

    def user_part(begin):
        return added(*[g[begin : begin + blocks] for g in (user_first, user_second, user_third)])

    far_grad = fetch(user_part(blocks).astype(low), core=1)
    half = (user_part(0) + far_grad.astype(jnp.float32)).astype(low)

    def lines(mine, arrived):
        return [added(mine[k], *[a[k] for a in arrived]).astype(low) for k in range(RING)]

    own_sum = lines(here_terms[0], arrived[0] + [fetch(across_terms[0], z=2)])
    far_sum = lines(here_terms[1], arrived[1] + [fetch(across_terms[1], y=2)])
    other = lax.ppermute(half, "rep", [(0, 1), (1, 0)])
    own_sum, far_sum, other = lax.optimization_barrier((own_sum, far_sum, other))
    user_sum = added(half, other)
    item_sum = added(
        own_sum[0],
        *[fetch(own_sum[d], y=-d) for d in range(1, RING)],
        *[fetch(far_sum[d], x=1, z=-d) for d in range(RING)],
    ).T
    new_users = adagrad(user_factors, user_accum, user_sum.reshape(user_factors.shape), num_slabs)
    new_items = adagrad(item_factors, item_accum, item_sum, num_slabs)
    return (new_users, new_items)


def solution(mesh):
    in_specs = (
        P("blk", None),
        P(("blk", "rep"), None),
        P("blk", None),
        P(("blk", "rep"), None),
        P("blk", "rep", None, None),
        P("blk", "rep", None, None),
        P("blk", "rep"),
        P("blk", "rep"),
        P("blk", "rep"),
    )
    out_specs = (P("blk", None), P(("blk", "rep"), None))
    return jax.shard_map(body, mesh=mesh, in_specs=in_specs, out_specs=out_specs, check_vma=False)
```

time: 919 us -> 127 us (0.14)
  waiting for transfers between devices: 415 us -> 34.7 us
  matrix products: 240 us -> 0 us
  local copies, waits for them, and re-layouts: 174 us -> 6.57 us
  other arithmetic: 58.4 us -> 7.95 us
  starting transfers between devices: 5.48 us -> 44.1 us
  Pallas kernels: 0 us -> 32 us
  between operations: 15.6 us -> 1.07 us
    reduce_scatter x1 -> x0, waiting for transfers between devices: 280 us -> none  [body(): lax.psum_scatter(gathered, 'blk', scatter_dimension=0, tiled=True)[0]]
    dot_general x320 -> x0, matrix products: 240 us -> none  [the longest x64 77 us: tile_terms(): jnp.einsum('sur,sir->sui', user_sel, item_sel, preferred_element_type=jnp...]
    gather x128 -> x0, local copies, waits for them, and re-layouts: 72.2 us -> none  [the longest x64 36.1 us: tile_terms(): item_sel = item_rows[item_index]]
    ppermute x64 -> x33, waiting for transfers between devices: 86.7 us -> 34.7 us  [the longest x32 34.7 us: fetch(): return lax.ppermute(block, 'blk', route)]
    psum x1 -> x0, waiting for transfers between devices: 47.1 us -> none  [body(): user_grad = lax.psum(user_grad, 'rep')]
    dynamic_update_slice x64 -> x0, local copies, waits for them, and re-layouts: 46.8 us -> none  [visit(): lax.dynamic_update_slice(gathered, item_add[None], (owner_index, 0, 0, 0))]
    dynamic_slice x64 -> x0, local copies, waits for them, and re-layouts: 40.9 us -> none  [tile_terms(): live_count = tile_counts[0, owner_index]]
    convert_element_type x66 -> x4, other arithmetic: 42.1 us -> 1.89 us  [the longest x1 1.29 us: body(): user_low = user_factors.astype(low).reshape(-1, TILE, columns)]
  transfers between devices with their start and end apart: 66 -> 33, of which waited for: 66 -> 14; matrix products, arithmetic and copies ran while one was open for 50% -> 9% of each run, Pallas kernels for 0% -> 20%
where the time goes in v2:
time: 127 us; the launch traced here: 126 us
  starting transfers between devices  44.1 us (35%)
  waiting for transfers between devices  34.7 us (27%)
  Pallas kernels  32 us (25%)
  other arithmetic  7.95 us (6%)
  local copies, waits for them, and re-layouts  6.57 us (5%)
    ppermute x32, starting transfers between devices, fetch(): return lax.ppermute(block, 'blk', route)  41.7 us
    ppermute x32, waiting for transfers between devices, fetch(): return lax.ppermute(block, 'blk', route)  34.7 us
    pallas_call x3, Pallas kernels, tile_terms(): pl.pallas_call(kernel, out_shape=[jax.ShapeDtypeStruct((RING, columns, ro...  25.2 us
    pallas_call x1, Pallas kernels, packed_tiles(): pl.pallas_call(pack_kernel, out_shape=jax.ShapeDtypeStruct((2, 2, lanes,...  6.82 us
    add x2, other arithmetic, added(): return sum((term.astype(jnp.float32) for term in terms))  3.19 us
  transfers between devices with their start and end apart: 33, of which 14 were waited for; matrix products, arithmetic and copies ran while one was open for 9% of the time, Pallas kernels for 20%

profile of v2, /device:TPU:2, one launch (start us, length us, event | category | flops | bytes accessed | tf_op | source)
XLA Modules:
  0.0 126.4 jit_solution(5004622464823302191)
XLA Ops:
  0.7 1.3 %convert_element_type.182 = bf16[1024,256]{1,0:T(8,128)(2,1)S(1)} convert(f32[1024,256]{1,0:T(8,128)} %param.9) | non-fusion elementwise | flops 262144 | bytes 1572864 | tf_op jit(solution)/shard_map/convert_element_type | solution.py:270
  2.4 0.5 collective-permute-start.7
  2.9 1.3 %collective-permute-done.7.refs_2_ = s32[1,576]{1,0:T(1,128)S(1)} collective-permute-done((s32[1,576]{1,0:T(1,128)S(1)}, s32[1,576]{1,0:T(1,128)S(1)}, u32[]{:S(2)}, u32[]{:S(2)}) %collective-permute-start.7) | collective-permute-done | bytes 2336 | tf_op jit(solution)/shard_map/ppermute | solution.py:35
  4.2 6.8 %shard_map.104 = bf16[2,2,16,4,128,128]{5,4,3,2,1,0:T(8,128)(2,1)} custom-call(s32[1]{0:T(128)} %bitcast.1.device_ref.refs_0_, bf16[2,16,2,4,128,128]{5,4,3,2,1,0:T(8,128)(2,1)} %bitcast.42, bf16[2,16,2,4,128,128]{5,4,3,2,1,0:T(8,128)(2,1)} %bitcast.46), custom_call_target="tpu_custom_call" | custom-call | bytes 16777216 | tf_op jit(solution)/shard_map/pallas_call | solution.py:232
  11.3 3.1 %collective-permute-start = (bf16[256,256]{1,0:T(8,128)(2,1)S(1)}, bf16[256,256]{1,0:T(8,128)(2,1)S(1)}, u32[]{:S(2)}, u32[]{:S(2)}) collective-permute-start(bf16[256,256]{1,0:T(8,128)(2,1)S(1)} %convert_element_type.181), channel_id=1, source_target_pairs={{16,0},{18,2},{20,4},{22,6},{24,8},{26,10},{28,12},{30,14},{32,16}... | collective-permute-start | bytes 393224 | tf_op jit(solution)/shard_map/ppermute | solution.py:35
  14.4 0.6 collective-permute-start.1
  15.0 1.0 collective-permute-start.2
  16.5 3.9 %collective-permute-done = bf16[256,256]{1,0:T(8,128)(2,1)S(1)} collective-permute-done((bf16[256,256]{1,0:T(8,128)(2,1)S(1)}, bf16[256,256]{1,0:T(8,128)(2,1)S(1)}, u32[]{:S(2)}, u32[]{:S(2)}) %collective-permute-start) | collective-permute-done | bytes 131104 | tf_op jit(solution)/shard_map/ppermute | solution.py:35
  20.5 4.0 %collective-permute-start.4 = (bf16[256,256]{1,0:T(8,128)(2,1)S(1)}, bf16[256,256]{1,0:T(8,128)(2,1)S(1)}, u32[]{:S(2)}, u32[]{:S(2)}) collective-permute-start(bf16[256,256]{1,0:T(8,128)(2,1)S(1)} %convert_element_type.181), channel_id=1, source_target_pairs={{68,0},{70,2},{72,4},{74,6},{76,8},{78,10},{64,12},{66,14},{84,16}... | collective-permute-start | bytes 393224 | tf_op jit(solution)/shard_map/ppermute | solution.py:35
  24.5 1.6 %collective-permute-start.5 = (bf16[256,256]{1,0:T(8,128)(2,1)S(1)}, bf16[256,256]{1,0:T(8,128)(2,1)S(1)}, u32[]{:S(2)}, u32[]{:S(2)}) collective-permute-start(bf16[256,256]{1,0:T(8,128)(2,1)S(1)} %convert_element_type.181), channel_id=1, source_target_pairs={{72,0},{74,2},{76,4},{78,6},{64,8},{66,10},{68,12},{70,14},{88,16}... | collective-permute-start | bytes 393224 | tf_op jit(solution)/shard_map/ppermute | solution.py:35
  26.2 1.9 %collective-permute-start.6 = (bf16[256,256]{1,0:T(8,128)(2,1)S(1)}, bf16[256,256]{1,0:T(8,128)(2,1)S(1)}, u32[]{:S(2)}, u32[]{:S(2)}) collective-permute-start(bf16[256,256]{1,0:T(8,128)(2,1)S(1)} %convert_element_type.181), channel_id=1, source_target_pairs={{76,0},{78,2},{64,4},{66,6},{68,8},{70,10},{72,12},{74,14},{92,16}... | collective-permute-start | bytes 393224 | tf_op jit(solution)/shard_map/ppermute | solution.py:35
  28.5 4.5 %collective-permute-done.5 = bf16[256,256]{1,0:T(8,128)(2,1)S(1)} collective-permute-done((bf16[256,256]{1,0:T(8,128)(2,1)S(1)}, bf16[256,256]{1,0:T(8,128)(2,1)S(1)}, u32[]{:S(2)}, u32[]{:S(2)}) %collective-permute-start.5) | collective-permute-done | bytes 131104 | tf_op jit(solution)/shard_map/ppermute | solution.py:35
  32.9 1.4 %collective-permute-done.6 = bf16[256,256]{1,0:T(8,128)(2,1)S(1)} collective-permute-done((bf16[256,256]{1,0:T(8,128)(2,1)S(1)}, bf16[256,256]{1,0:T(8,128)(2,1)S(1)}, u32[]{:S(2)}, u32[]{:S(2)}) %collective-permute-start.6) | collective-permute-done | bytes 131104 | tf_op jit(solution)/shard_map/ppermute | solution.py:35
  34.4 1.0 collective-permute-start.9
  35.4 1.1 collective-permute-start.11
  36.6 3.9 %collective-permute-start.10 = (bf16[4,256,256]{2,1,0:T(8,128)(2,1)S(1)}, bf16[4,256,256]{2,1,0:T(8,128)(2,1)}, u32[]{:S(2)}, u32[]{:S(2)}) collective-permute-start(bf16[4,256,256]{2,1,0:T(8,128)(2,1)S(1)} %pad_maximum_fusion.2.refs_7_), channel_id=1, source_target_pairs={{16,0},{18,2},{20,4},{22,6},{24,8},{26,10},{28,12},{30,14},{32,16}... | collective-permute-start | bytes 1572872 | tf_op jit(solution)/shard_map/ppermute | solution.py:35
  41.1 6.0 %shard_map.105 = (bf16[4,256,256]{2,1,0:T(8,128)(2,1)S(1)}, bf16[4,256,256]{2,1,0:T(8,128)(2,1)S(1)}, f32[16,128,256]{2,1,0:T(8,128)S(1)}) custom-call(s32[1]{0:T(128)} %bitcast.1.device_ref.refs_0_, s32[1,576]{1,0:T(1,128)S(1)} %constant_dynamic-update-slice_fusion.refs_1_, s32[1,576]{1,0:T(1,128)S(1)} %collective-permute-done.7.refs_2_, ...), custom_call_target="tpu_custom_call" | custom-call | flops 6442450944 | bytes 8388608 | tf_op jit(solution)/shard_map/pallas_call | solution.py:185
  47.1 2.7 %collective-permute-done.10.refs_7_ = bf16[4,256,256]{2,1,0:T(8,128)(2,1)} collective-permute-done((bf16[4,256,256]{2,1,0:T(8,128)(2,1)S(1)}, bf16[4,256,256]{2,1,0:T(8,128)(2,1)}, u32[]{:S(2)}, u32[]{:S(2)}) %collective-permute-start.10) | collective-permute-done | bytes 524320 | tf_op jit(solution)/shard_map/ppermute | solution.py:35
  49.8 3.5 %collective-permute-done.12.refs_9_ = bf16[4,256,256]{2,1,0:T(8,128)(2,1)} collective-permute-done((bf16[4,256,256]{2,1,0:T(8,128)(2,1)S(1)}, bf16[4,256,256]{2,1,0:T(8,128)(2,1)}, u32[]{:S(2)}, u32[]{:S(2)}) %collective-permute-start.12) | collective-permute-done | bytes 524320 | tf_op jit(solution)/shard_map/ppermute | solution.py:35
  53.3 1.0 slice.128
  54.3 1.6 %collective-permute-start.14 = (bf16[2,256,256]{2,1,0:T(8,128)(2,1)S(1)}, bf16[2,256,256]{2,1,0:T(8,128)(2,1)S(1)}, u32[]{:S(2)}, u32[]{:S(2)}) collective-permute-start(bf16[2,256,256]{2,1,0:T(8,128)(2,1)S(1)} %slice.128), channel_id=1, source_target_pairs={{4,0},{6,2},{8,4},{10,6},{12,8},{14,10},{0,12},{2,14},{20,16},{22,... | collective-permute-start | bytes 786440 | tf_op jit(solution)/shard_map/ppermute | solution.py:35
  55.9 1.0 slice.129
  57.4 1.0 slice.130
  58.9 1.0 slice.131
  59.9 1.8 %collective-permute-start.17 = (bf16[2,256,256]{2,1,0:T(8,128)(2,1)S(1)}, bf16[2,256,256]{2,1,0:T(8,128)(2,1)S(1)}, u32[]{:S(2)}, u32[]{:S(2)}) collective-permute-start(bf16[2,256,256]{2,1,0:T(8,128)(2,1)S(1)} %slice.131), channel_id=1, source_target_pairs={{48,0},{50,2},{52,4},{54,6},{56,8},{58,10},{60,12},{62,14},{0,16},... | collective-permute-start | bytes 786440 | tf_op jit(solution)/shard_map/ppermute | solution.py:35
  61.7 12.7 %shard_map.106 = (bf16[4,256,256]{2,1,0:T(8,128)(2,1)S(1)}, bf16[4,256,256]{2,1,0:T(8,128)(2,1)S(1)}, bf16[4,256,256]{2,1,0:T(8,128)(2,1)S(1)}, bf16[4,256,256]{2,1,0:T(8,128)(2,1)S(1)}, f32[16,128,256]{2,1,0:T(8,128)S(1)}) custom-call(s32[1]{0:T(128)} %bitcast.1.device_ref.refs_0_, s32[1,576]{1,0:T(1,128)S(1)} %constant_dynamic-update-slice_fusion.refs_1_, ...), custom_call_target="tpu_custom_call" | custom-call | flops 12884901888 | bytes 16777216 | tf_op jit(solution)/shard_map/pallas_call | solution.py:185
  74.5 2.2 %collective-permute-start.19 = (bf16[4,256,256]{2,1,0:T(8,128)(2,1)S(1)}, bf16[4,256,256]{2,1,0:T(8,128)(2,1)S(1)}, u32[]{:S(2)}, u32[]{:S(2)}) collective-permute-start(bf16[4,256,256]{2,1,0:T(8,128)(2,1)S(1)} %get-tuple-element.70), channel_id=1, source_target_pairs={{12,0},{14,2},{0,4},{2,6},{4,8},{6,10},{8,12},{10,14},{28,16},{30,... | collective-permute-start | bytes 1572872 | tf_op jit(solution)/shard_map/ppermute | solution.py:35
  76.7 1.4 %collective-permute-start.20 = (bf16[4,256,256]{2,1,0:T(8,128)(2,1)S(1)}, bf16[4,256,256]{2,1,0:T(8,128)(2,1)S(1)}, u32[]{:S(2)}, u32[]{:S(2)}) collective-permute-start(bf16[4,256,256]{2,1,0:T(8,128)(2,1)S(1)} %get-tuple-element.71), channel_id=1, source_target_pairs={{4,0},{6,2},{8,4},{10,6},{12,8},{14,10},{0,12},{2,14},{20,16},{22,... | collective-permute-start | bytes 1572872 | tf_op jit(solution)/shard_map/ppermute | solution.py:35
  78.3 3.0 %collective-permute-start.22 = (bf16[4,256,256]{2,1,0:T(8,128)(2,1)S(1)}, bf16[4,256,256]{2,1,0:T(8,128)(2,1)S(1)}, u32[]{:S(2)}, u32[]{:S(2)}) collective-permute-start(bf16[4,256,256]{2,1,0:T(8,128)(2,1)S(1)} %get-tuple-element.73), channel_id=1, source_target_pairs={{16,0},{18,2},{20,4},{22,6},{24,8},{26,10},{28,12},{30,14},{32,16}... | collective-permute-start | bytes 1572872 | tf_op jit(solution)/shard_map/ppermute | solution.py:35
  81.3 6.5 %shard_map.107 = (bf16[4,256,256]{2,1,0:T(8,128)(2,1)S(1)}, bf16[4,256,256]{2,1,0:T(8,128)(2,1)S(1)}, f32[16,128,256]{2,1,0:T(8,128)S(1)}) custom-call(s32[1]{0:T(128)} %bitcast.1.device_ref.refs_0_, s32[1,576]{1,0:T(1,128)S(1)} %constant_dynamic-update-slice_fusion.refs_1_, s32[1,576]{1,0:T(1,128)S(1)} %collective-permute-done.7.refs_2_, ...), custom_call_target="tpu_custom_call" | custom-call | flops 6442450944 | bytes 8388608 | tf_op jit(solution)/shard_map/pallas_call | solution.py:185
  88.6 1.4 %collective-permute-start.23 = (bf16[4,256,256]{2,1,0:T(8,128)(2,1)S(1)}, bf16[4,256,256]{2,1,0:T(8,128)(2,1)}, u32[]{:S(2)}, u32[]{:S(2)}) collective-permute-start(bf16[4,256,256]{2,1,0:T(8,128)(2,1)S(1)} %get-tuple-element.78), channel_id=1, source_target_pairs={{8,0},{10,2},{12,4},{14,6},{0,8},{2,10},{4,12},{6,14},{24,16},{26,... | collective-permute-start | bytes 1572872 | tf_op jit(solution)/shard_map/ppermute | solution.py:35
  90.0 1.8 %collective-permute-start.24 = (bf16[4,256,256]{2,1,0:T(8,128)(2,1)S(1)}, bf16[4,256,256]{2,1,0:T(8,128)(2,1)}, u32[]{:S(2)}, u32[]{:S(2)}) collective-permute-start(bf16[4,256,256]{2,1,0:T(8,128)(2,1)S(1)} %get-tuple-element.82), channel_id=1, source_target_pairs={{32,0},{34,2},{36,4},{38,6},{40,8},{42,10},{44,12},{46,14},{48,16}... | collective-permute-start | bytes 1572872 | tf_op jit(solution)/shard_map/ppermute | solution.py:35
  92.1 2.4 %collective-permute-start.25 = (bf16[8,128,256]{2,1,0:T(8,128)(2,1)S(1)}, bf16[8,128,256]{2,1,0:T(8,128)(2,1)}, u32[]{:S(2)}, u32[]{:S(2)}) collective-permute-start(bf16[8,128,256]{2,1,0:T(8,128)(2,1)S(1)} %add_convert_fusion), channel_id=1, source_target_pairs={{0,1},{1,0},{2,3},{3,2},{4,5},{5,4},{6,7},{7,6},{8,9},{9,8},{10,11... | collective-permute-start | bytes 1572872 | tf_op jit(solution)/shard_map/ppermute | solution.py:336
  94.6 0.8 copy.24
  95.5 8.8 %collective-permute-done.23 = bf16[4,256,256]{2,1,0:T(8,128)(2,1)} collective-permute-done((bf16[4,256,256]{2,1,0:T(8,128)(2,1)S(1)}, bf16[4,256,256]{2,1,0:T(8,128)(2,1)}, u32[]{:S(2)}, u32[]{:S(2)}) %collective-permute-start.23) | collective-permute-done | bytes 524320 | tf_op jit(solution)/shard_map/ppermute | solution.py:35
  104.3 1.7 %fusion.3 = (bf16[256,256]{1,0:T(8,128)(2,1)S(1)}, bf16[256,256]{1,0:T(8,128)(2,1)S(1)}, bf16[256,256]{1,0:T(8,128)(2,1)S(1)}, bf16[256,256]{1,0:T(8,128)(2,1)S(1)}) fusion(bf16[4,256,256]{2,1,0:T(8,128)(2,1)} %collective-permute-done.23, bf16[4,256,256]{2,1,0:T(8,128)(2,1)} %copy-done.12, bf16[4,256,256]{2,1,0:T(8,128)(2,1)} %copy-done.9, ...), kind=kLoop, calls=%fused_computation.21 | loop fusion | flops 2097152 | bytes 2621440 | tf_op jit(solution)/shard_map/add | solution.py:244
  106.1 1.5 %fusion.7 = (bf16[256,256]{1,0:T(8,128)(2,1)S(1)}, bf16[256,256]{1,0:T(8,128)(2,1)S(1)}, bf16[256,256]{1,0:T(8,128)(2,1)S(1)}, bf16[256,256]{1,0:T(8,128)(2,1)S(1)}) fusion(bf16[4,256,256]{2,1,0:T(8,128)(2,1)} %collective-permute-done.24, bf16[4,256,256]{2,1,0:T(8,128)(2,1)S(1)} %copy-done.14, bf16[4,256,256]{2,1,0:T(8,128)(2,1)S(1)} %copy-done.11, ...), kind=kLoop, calls=%fused_computation.25 | loop fusion | flops 2097152 | bytes 2621440 | tf_op jit(solution)/shard_map/add | solution.py:244
  107.6 2.8 %collective-permute-start.32 = (bf16[256,256]{1,0:T(8,128)(2,1)S(1)}, bf16[256,256]{1,0:T(8,128)(2,1)S(1)}, u32[]{:S(2)}, u32[]{:S(2)}) collective-permute-start(bf16[256,256]{1,0:T(8,128)(2,1)S(1)} %get-tuple-element.91), channel_id=1, source_target_pairs={{68,0},{70,2},{72,4},{74,6},{76,8},{78,10},{64,12},{66,14},{84,16}... | collective-permute-start | bytes 393224 | tf_op jit(solution)/shard_map/ppermute | solution.py:35
  110.4 0.8 collective-permute-start.31
  111.2 1.2 add_multiply_fusion
  112.4 1.3 %collective-permute-start.30 = (bf16[256,256]{1,0:T(8,128)(2,1)S(1)}, bf16[256,256]{1,0:T(8,128)(2,1)S(1)}, u32[]{:S(2)}, u32[]{:S(2)}) collective-permute-start(bf16[256,256]{1,0:T(8,128)(2,1)S(1)} %get-tuple-element.89), channel_id=1, source_target_pairs={{76,0},{78,2},{64,4},{66,6},{68,8},{70,10},{72,12},{74,14},{92,16}... | collective-permute-start | bytes 393224 | tf_op jit(solution)/shard_map/ppermute | solution.py:35
  114.7 1.6 %collective-permute-start.27 = (bf16[256,256]{1,0:T(8,128)(2,1)S(1)}, bf16[256,256]{1,0:T(8,128)(2,1)S(1)}, u32[]{:S(2)}, u32[]{:S(2)}) collective-permute-start(bf16[256,256]{1,0:T(8,128)(2,1)S(1)} %get-tuple-element.86), channel_id=1, source_target_pairs={{32,0},{34,2},{36,4},{38,6},{40,8},{42,10},{44,12},{46,14},{48,16}... | collective-permute-start | bytes 393224 | tf_op jit(solution)/shard_map/ppermute | solution.py:35
  116.3 2.9 %collective-permute-done.31 = bf16[256,256]{1,0:T(8,128)(2,1)S(1)} collective-permute-done((bf16[256,256]{1,0:T(8,128)(2,1)S(1)}, bf16[256,256]{1,0:T(8,128)(2,1)S(1)}, u32[]{:S(2)}, u32[]{:S(2)}) %collective-permute-start.31) | collective-permute-done | bytes 131104 | tf_op jit(solution)/shard_map/ppermute | solution.py:35
  119.2 1.2 multiply_subtract_fusion
  120.4 0.8 collective-permute-done.30
  121.2 0.8 collective-permute-done.29
  122.0 3.3 %collective-permute-done.26 = bf16[256,256]{1,0:T(8,128)(2,1)S(1)} collective-permute-done((bf16[256,256]{1,0:T(8,128)(2,1)S(1)}, bf16[256,256]{1,0:T(8,128)(2,1)S(1)}, u32[]{:S(2)}, u32[]{:S(2)}) %collective-permute-start.26) | collective-permute-done | bytes 131104 | tf_op jit(solution)/shard_map/ppermute | solution.py:35
  125.6 0.8 copy.26
  (84 shorter events, 5.9 us)
Async XLA Ops:
  2.2 2.0 %collective-permute-start.8 = (bf16[8,128,256]{1,2,0:T(8,128)(2,1)S(1)}, bf16[8,128,256]{1,2,0:T(8,128)(2,1)S(1)}, u32[]{:S(2)}, u32[]{:S(2)}) collective-permute-start(bf16[8,128,256]{1,2,0:T(8,128)(2,1)S(1)} %copy.19), channel_id=1, source_target_pairs={{2,0},{0,2},{6,4},{4,6},{10,8},{8,10},{14,12},{12,14},{18,16},{16,... | collective-permute-start | bytes 1572872 | tf_op jit(solution)/shard_map/ppermute | solution.py:35
  2.4 1.8 %collective-permute-start.7 = (s32[1,576]{1,0:T(1,128)S(1)}, s32[1,576]{1,0:T(1,128)S(1)}, u32[]{:S(2)}, u32[]{:S(2)}) collective-permute-start(s32[1,576]{1,0:T(1,128)S(1)} %constant_dynamic-update-slice_fusion.refs_1_), channel_id=1, source_target_pairs={{2,0},{0,2},{6,4},{4,6},{10,8},{8,10},{14,12},{12,14},{18,16},{16,... | collective-permute-start | bytes 6920 | tf_op jit(solution)/shard_map/ppermute | solution.py:35
  4.2 7.1 %copy-start.6 = (f32[256,256]{1,0:T(8,128)S(1)}, f32[256,256]{1,0:T(8,128)}, u32[]{:S(2)}) copy-start(f32[256,256]{1,0:T(8,128)} %param.10) | copy-start | bytes 786436
  11.1 30.0 %collective-permute-start.13 = (bf16[2,2,16,4,128,128]{5,4,3,2,1,0:T(8,128)(2,1)}, bf16[2,2,16,4,128,128]{5,4,3,2,1,0:T(8,128)(2,1)}, u32[]{:S(2)}, u32[]{:S(2)}) collective-permute-start(bf16[2,2,16,4,128,128]{5,4,3,2,1,0:T(8,128)(2,1)} %shard_map.104), channel_id=1, source_target_pairs={{2,0},{0,2},{6,4},{4,6},{10,8},{8,10},{14,12},{12,14},{18,16},{16,... | collective-permute-start | bytes 25165832 | tf_op jit(solution)/shard_map/ppermute | solution.py:35
  11.3 9.2 %collective-permute-start = (bf16[256,256]{1,0:T(8,128)(2,1)S(1)}, bf16[256,256]{1,0:T(8,128)(2,1)S(1)}, u32[]{:S(2)}, u32[]{:S(2)}) collective-permute-start(bf16[256,256]{1,0:T(8,128)(2,1)S(1)} %convert_element_type.181), channel_id=1, source_target_pairs={{16,0},{18,2},{20,4},{22,6},{24,8},{26,10},{28,12},{30,14},{32,16}... | collective-permute-start | bytes 393224 | tf_op jit(solution)/shard_map/ppermute | solution.py:35
  14.4 10.1 %collective-permute-start.1 = (bf16[256,256]{1,0:T(8,128)(2,1)S(1)}, bf16[256,256]{1,0:T(8,128)(2,1)S(1)}, u32[]{:S(2)}, u32[]{:S(2)}) collective-permute-start(bf16[256,256]{1,0:T(8,128)(2,1)S(1)} %convert_element_type.181), channel_id=1, source_target_pairs={{32,0},{34,2},{36,4},{38,6},{40,8},{42,10},{44,12},{46,14},{48,16}... | collective-permute-start | bytes 393224 | tf_op jit(solution)/shard_map/ppermute | solution.py:35
  15.0 11.1 %collective-permute-start.2 = (bf16[256,256]{1,0:T(8,128)(2,1)S(1)}, bf16[256,256]{1,0:T(8,128)(2,1)S(1)}, u32[]{:S(2)}, u32[]{:S(2)}) collective-permute-start(bf16[256,256]{1,0:T(8,128)(2,1)S(1)} %convert_element_type.181), channel_id=1, source_target_pairs={{48,0},{50,2},{52,4},{54,6},{56,8},{58,10},{60,12},{62,14},{0,16},... | collective-permute-start | bytes 393224 | tf_op jit(solution)/shard_map/ppermute | solution.py:35
  16.0 12.2 %collective-permute-start.3 = (bf16[256,256]{1,0:T(8,128)(2,1)S(1)}, bf16[256,256]{1,0:T(8,128)(2,1)S(1)}, u32[]{:S(2)}, u32[]{:S(2)}) collective-permute-start(bf16[256,256]{1,0:T(8,128)(2,1)S(1)} %convert_element_type.181), channel_id=1, source_target_pairs={{64,0},{66,2},{68,4},{70,6},{72,8},{74,10},{76,12},{78,14},{80,16}... | collective-permute-start | bytes 393224 | tf_op jit(solution)/shard_map/ppermute | solution.py:35
  20.5 8.0 %collective-permute-start.4 = (bf16[256,256]{1,0:T(8,128)(2,1)S(1)}, bf16[256,256]{1,0:T(8,128)(2,1)S(1)}, u32[]{:S(2)}, u32[]{:S(2)}) collective-permute-start(bf16[256,256]{1,0:T(8,128)(2,1)S(1)} %convert_element_type.181), channel_id=1, source_target_pairs={{68,0},{70,2},{72,4},{74,6},{76,8},{78,10},{64,12},{66,14},{84,16}... | collective-permute-start | bytes 393224 | tf_op jit(solution)/shard_map/ppermute | solution.py:35
  24.5 8.4 %collective-permute-start.5 = (bf16[256,256]{1,0:T(8,128)(2,1)S(1)}, bf16[256,256]{1,0:T(8,128)(2,1)S(1)}, u32[]{:S(2)}, u32[]{:S(2)}) collective-permute-start(bf16[256,256]{1,0:T(8,128)(2,1)S(1)} %convert_element_type.181), channel_id=1, source_target_pairs={{72,0},{74,2},{76,4},{78,6},{64,8},{66,10},{68,12},{70,14},{88,16}... | collective-permute-start | bytes 393224 | tf_op jit(solution)/shard_map/ppermute | solution.py:35
  26.2 8.2 %collective-permute-start.6 = (bf16[256,256]{1,0:T(8,128)(2,1)S(1)}, bf16[256,256]{1,0:T(8,128)(2,1)S(1)}, u32[]{:S(2)}, u32[]{:S(2)}) collective-permute-start(bf16[256,256]{1,0:T(8,128)(2,1)S(1)} %convert_element_type.181), channel_id=1, source_target_pairs={{76,0},{78,2},{64,4},{66,6},{68,8},{70,10},{72,12},{74,14},{92,16}... | collective-permute-start | bytes 393224 | tf_op jit(solution)/shard_map/ppermute | solution.py:35
  34.4 12.6 %collective-permute-start.9 = (bf16[4,256,256]{2,1,0:T(8,128)(2,1)S(1)}, bf16[4,256,256]{2,1,0:T(8,128)(2,1)}, u32[]{:S(2)}, u32[]{:S(2)}) collective-permute-start(bf16[4,256,256]{2,1,0:T(8,128)(2,1)S(1)} %pad_maximum_fusion.1.refs_6_), channel_id=1, source_target_pairs={{4,0},{6,2},{8,4},{10,6},{12,8},{14,10},{0,12},{2,14},{20,16},{22,... | collective-permute-start | bytes 1572872 | tf_op jit(solution)/shard_map/ppermute | solution.py:35
  35.4 14.4 %collective-permute-start.11 = (bf16[4,256,256]{2,1,0:T(8,128)(2,1)S(1)}, bf16[4,256,256]{2,1,0:T(8,128)(2,1)}, u32[]{:S(2)}, u32[]{:S(2)}) collective-permute-start(bf16[4,256,256]{2,1,0:T(8,128)(2,1)S(1)} %pad_maximum_fusion.1.refs_6_), channel_id=1, source_target_pairs={{12,0},{14,2},{0,4},{2,6},{4,8},{6,10},{8,12},{10,14},{28,16},{30,... | collective-permute-start | bytes 1572872 | tf_op jit(solution)/shard_map/ppermute | solution.py:35
  36.6 13.2 %collective-permute-start.10 = (bf16[4,256,256]{2,1,0:T(8,128)(2,1)S(1)}, bf16[4,256,256]{2,1,0:T(8,128)(2,1)}, u32[]{:S(2)}, u32[]{:S(2)}) collective-permute-start(bf16[4,256,256]{2,1,0:T(8,128)(2,1)S(1)} %pad_maximum_fusion.2.refs_7_), channel_id=1, source_target_pairs={{16,0},{18,2},{20,4},{22,6},{24,8},{26,10},{28,12},{30,14},{32,16}... | collective-permute-start | bytes 1572872 | tf_op jit(solution)/shard_map/ppermute | solution.py:35
  40.5 12.8 %collective-permute-start.12 = (bf16[4,256,256]{2,1,0:T(8,128)(2,1)S(1)}, bf16[4,256,256]{2,1,0:T(8,128)(2,1)}, u32[]{:S(2)}, u32[]{:S(2)}) collective-permute-start(bf16[4,256,256]{2,1,0:T(8,128)(2,1)S(1)} %pad_maximum_fusion.2.refs_7_), channel_id=1, source_target_pairs={{48,0},{50,2},{52,4},{54,6},{56,8},{58,10},{60,12},{62,14},{0,16},... | collective-permute-start | bytes 1572872 | tf_op jit(solution)/shard_map/ppermute | solution.py:35
  47.0 27.4 %copy-start = (bf16[4,256,256]{2,1,0:T(8,128)(2,1)}, bf16[4,256,256]{2,1,0:T(8,128)(2,1)S(1)}, u32[]{:S(2)}) copy-start(bf16[4,256,256]{2,1,0:T(8,128)(2,1)S(1)} %get-tuple-element.79) | copy-start | bytes 1572868
  47.1 27.4 %copy-start.2 = (bf16[4,256,256]{2,1,0:T(8,128)(2,1)}, bf16[4,256,256]{2,1,0:T(8,128)(2,1)S(1)}, u32[]{:S(2)}) copy-start(bf16[4,256,256]{2,1,0:T(8,128)(2,1)S(1)} %get-tuple-element.69) | copy-start | bytes 1572868
  54.3 22.4 %collective-permute-start.14 = (bf16[2,256,256]{2,1,0:T(8,128)(2,1)S(1)}, bf16[2,256,256]{2,1,0:T(8,128)(2,1)S(1)}, u32[]{:S(2)}, u32[]{:S(2)}) collective-permute-start(bf16[2,256,256]{2,1,0:T(8,128)(2,1)S(1)} %slice.128), channel_id=1, source_target_pairs={{4,0},{6,2},{8,4},{10,6},{12,8},{14,10},{0,12},{2,14},{20,16},{22,... | collective-permute-start | bytes 786440 | tf_op jit(solution)/shard_map/ppermute | solution.py:35
  56.9 21.2 %collective-permute-start.15 = (bf16[2,256,256]{2,1,0:T(8,128)(2,1)S(1)}, bf16[2,256,256]{2,1,0:T(8,128)(2,1)S(1)}, u32[]{:S(2)}, u32[]{:S(2)}) collective-permute-start(bf16[2,256,256]{2,1,0:T(8,128)(2,1)S(1)} %slice.129), channel_id=1, source_target_pairs={{12,0},{14,2},{0,4},{2,6},{4,8},{6,10},{8,12},{10,14},{28,16},{30,... | collective-permute-start | bytes 786440 | tf_op jit(solution)/shard_map/ppermute | solution.py:35
  58.4 19.9 %collective-permute-start.16 = (bf16[2,256,256]{2,1,0:T(8,128)(2,1)S(1)}, bf16[2,256,256]{2,1,0:T(8,128)(2,1)S(1)}, u32[]{:S(2)}, u32[]{:S(2)}) collective-permute-start(bf16[2,256,256]{2,1,0:T(8,128)(2,1)S(1)} %slice.130), channel_id=1, source_target_pairs={{16,0},{18,2},{20,4},{22,6},{24,8},{26,10},{28,12},{30,14},{32,16}... | collective-permute-start | bytes 786440 | tf_op jit(solution)/shard_map/ppermute | solution.py:35
  59.9 21.4 %collective-permute-start.17 = (bf16[2,256,256]{2,1,0:T(8,128)(2,1)S(1)}, bf16[2,256,256]{2,1,0:T(8,128)(2,1)S(1)}, u32[]{:S(2)}, u32[]{:S(2)}) collective-permute-start(bf16[2,256,256]{2,1,0:T(8,128)(2,1)S(1)} %slice.131), channel_id=1, source_target_pairs={{48,0},{50,2},{52,4},{54,6},{56,8},{58,10},{60,12},{62,14},{0,16},... | collective-permute-start | bytes 786440 | tf_op jit(solution)/shard_map/ppermute | solution.py:35
  74.5 13.8 %collective-permute-start.19 = (bf16[4,256,256]{2,1,0:T(8,128)(2,1)S(1)}, bf16[4,256,256]{2,1,0:T(8,128)(2,1)S(1)}, u32[]{:S(2)}, u32[]{:S(2)}) collective-permute-start(bf16[4,256,256]{2,1,0:T(8,128)(2,1)S(1)} %get-tuple-element.70), channel_id=1, source_target_pairs={{12,0},{14,2},{0,4},{2,6},{4,8},{6,10},{8,12},{10,14},{28,16},{30,... | collective-permute-start | bytes 1572872 | tf_op jit(solution)/shard_map/ppermute | solution.py:35
  76.7 11.5 %collective-permute-start.20 = (bf16[4,256,256]{2,1,0:T(8,128)(2,1)S(1)}, bf16[4,256,256]{2,1,0:T(8,128)(2,1)S(1)}, u32[]{:S(2)}, u32[]{:S(2)}) collective-permute-start(bf16[4,256,256]{2,1,0:T(8,128)(2,1)S(1)} %get-tuple-element.71), channel_id=1, source_target_pairs={{4,0},{6,2},{8,4},{10,6},{12,8},{14,10},{0,12},{2,14},{20,16},{22,... | collective-permute-start | bytes 1572872 | tf_op jit(solution)/shard_map/ppermute | solution.py:35
  78.1 10.5 %collective-permute-start.21 = (bf16[4,256,256]{2,1,0:T(8,128)(2,1)S(1)}, bf16[4,256,256]{2,1,0:T(8,128)(2,1)S(1)}, u32[]{:S(2)}, u32[]{:S(2)}) collective-permute-start(bf16[4,256,256]{2,1,0:T(8,128)(2,1)S(1)} %get-tuple-element.72), channel_id=1, source_target_pairs={{48,0},{50,2},{52,4},{54,6},{56,8},{58,10},{60,12},{62,14},{0,16},... | collective-permute-start | bytes 1572872 | tf_op jit(solution)/shard_map/ppermute | solution.py:35
  78.3 10.3 %collective-permute-start.22 = (bf16[4,256,256]{2,1,0:T(8,128)(2,1)S(1)}, bf16[4,256,256]{2,1,0:T(8,128)(2,1)S(1)}, u32[]{:S(2)}, u32[]{:S(2)}) collective-permute-start(bf16[4,256,256]{2,1,0:T(8,128)(2,1)S(1)} %get-tuple-element.73), channel_id=1, source_target_pairs={{16,0},{18,2},{20,4},{22,6},{24,8},{26,10},{28,12},{30,14},{32,16}... | collective-permute-start | bytes 1572872 | tf_op jit(solution)/shard_map/ppermute | solution.py:35
  88.1 3.7 %collective-permute-start.18 = (bf16[8,128,256]{2,1,0:T(8,128)(2,1)S(1)}, bf16[8,128,256]{2,1,0:T(8,128)(2,1)S(1)}, u32[]{:S(2)}, u32[]{:S(2)}) collective-permute-start(bf16[8,128,256]{2,1,0:T(8,128)(2,1)S(1)} %add_convert_fusion.1), channel_id=1, source_target_pairs={{2,0},{0,2},{6,4},{4,6},{10,8},{8,10},{14,12},{12,14},{18,16},{16,... | collective-permute-start | bytes 1572872 | tf_op jit(solution)/shard_map/ppermute | solution.py:35
  88.2 3.9 %copy-start.9 = (bf16[4,256,256]{2,1,0:T(8,128)(2,1)}, bf16[4,256,256]{2,1,0:T(8,128)(2,1)S(1)}, u32[]{:S(2)}) copy-start(bf16[4,256,256]{2,1,0:T(8,128)(2,1)S(1)} %collective-permute-done.19) | copy-start | bytes 1572868
  88.2 3.9 %copy-start.12 = (bf16[4,256,256]{2,1,0:T(8,128)(2,1)}, bf16[4,256,256]{2,1,0:T(8,128)(2,1)S(1)}, u32[]{:S(2)}) copy-start(bf16[4,256,256]{2,1,0:T(8,128)(2,1)S(1)} %collective-permute-done.20) | copy-start | bytes 1572868
  88.6 3.5 %copy-start.13 = (bf16[4,256,256]{2,1,0:T(8,128)(2,1)}, bf16[4,256,256]{2,1,0:T(8,128)(2,1)S(1)}, u32[]{:S(2)}) copy-start(bf16[4,256,256]{2,1,0:T(8,128)(2,1)S(1)} %collective-permute-done.22) | copy-start | bytes 1572868
  88.6 5.9 %copy-start.7 = (f32[256,256]{1,0:T(8,128)S(1)}, f32[256,256]{1,0:T(8,128)}, u32[]{:S(2)}) copy-start(f32[256,256]{1,0:T(8,128)} %param.10) | copy-start | bytes 786436
  88.6 6.0 %copy-start.15 = (f32[256,256]{1,0:T(8,128)S(1)}, f32[256,256]{1,0:T(8,128)}, u32[]{:S(2)}) copy-start(f32[256,256]{1,0:T(8,128)} %param.12) | copy-start | bytes 786436
  88.6 15.7 %copy-start.3 = (bf16[4,256,256]{2,1,0:T(8,128)(2,1)S(1)}, bf16[4,256,256]{2,1,0:T(8,128)(2,1)}, u32[]{:S(2)}) copy-start(bf16[4,256,256]{2,1,0:T(8,128)(2,1)} %copy-done.2) | copy-start | bytes 1572868
  88.6 15.7 %collective-permute-start.23 = (bf16[4,256,256]{2,1,0:T(8,128)(2,1)S(1)}, bf16[4,256,256]{2,1,0:T(8,128)(2,1)}, u32[]{:S(2)}, u32[]{:S(2)}) collective-permute-start(bf16[4,256,256]{2,1,0:T(8,128)(2,1)S(1)} %get-tuple-element.78), channel_id=1, source_target_pairs={{8,0},{10,2},{12,4},{14,6},{0,8},{2,10},{4,12},{6,14},{24,16},{26,... | collective-permute-start | bytes 1572872 | tf_op jit(solution)/shard_map/ppermute | solution.py:35
  90.0 16.0 %collective-permute-start.24 = (bf16[4,256,256]{2,1,0:T(8,128)(2,1)S(1)}, bf16[4,256,256]{2,1,0:T(8,128)(2,1)}, u32[]{:S(2)}, u32[]{:S(2)}) collective-permute-start(bf16[4,256,256]{2,1,0:T(8,128)(2,1)S(1)} %get-tuple-element.82), channel_id=1, source_target_pairs={{32,0},{34,2},{36,4},{38,6},{40,8},{42,10},{44,12},{46,14},{48,16}... | collective-permute-start | bytes 1572872 | tf_op jit(solution)/shard_map/ppermute | solution.py:35
  92.1 13.9 %copy-start.1 = (bf16[4,256,256]{2,1,0:T(8,128)(2,1)S(1)}, bf16[4,256,256]{2,1,0:T(8,128)(2,1)}, u32[]{:S(2)}) copy-start(bf16[4,256,256]{2,1,0:T(8,128)(2,1)} %copy-done) | copy-start | bytes 1572868
  92.1 15.4 %collective-permute-start.25 = (bf16[8,128,256]{2,1,0:T(8,128)(2,1)S(1)}, bf16[8,128,256]{2,1,0:T(8,128)(2,1)}, u32[]{:S(2)}, u32[]{:S(2)}) collective-permute-start(bf16[8,128,256]{2,1,0:T(8,128)(2,1)S(1)} %add_convert_fusion), channel_id=1, source_target_pairs={{0,1},{1,0},{2,3},{3,2},{4,5},{5,4},{6,7},{7,6},{8,9},{9,8},{10,11... | collective-permute-start | bytes 1572872 | tf_op jit(solution)/shard_map/ppermute | solution.py:336
  95.5 10.6 %copy-start.11 = (bf16[4,256,256]{2,1,0:T(8,128)(2,1)S(1)}, bf16[4,256,256]{2,1,0:T(8,128)(2,1)}, u32[]{:S(2)}) copy-start(bf16[4,256,256]{2,1,0:T(8,128)(2,1)} %copy-done.10) | copy-start | bytes 1572868
  95.5 10.6 %copy-start.14 = (bf16[4,256,256]{2,1,0:T(8,128)(2,1)S(1)}, bf16[4,256,256]{2,1,0:T(8,128)(2,1)}, u32[]{:S(2)}) copy-start(bf16[4,256,256]{2,1,0:T(8,128)(2,1)} %copy-done.13) | copy-start | bytes 1572868
  106.0 13.2 %copy-start.4 = (f32[1024,256]{1,0:T(8,128)S(1)}, f32[1024,256]{1,0:T(8,128)}, u32[]{:S(2)}) copy-start(f32[1024,256]{1,0:T(8,128)} %param.9) | copy-start | bytes 3145732
  106.0 13.2 %copy-start.8 = (f32[1024,256]{1,0:T(8,128)S(1)}, f32[1024,256]{1,0:T(8,128)}, u32[]{:S(2)}) copy-start(f32[1024,256]{1,0:T(8,128)} %param.11) | copy-start | bytes 3145732
  107.6 7.1 %collective-permute-start.32 = (bf16[256,256]{1,0:T(8,128)(2,1)S(1)}, bf16[256,256]{1,0:T(8,128)(2,1)S(1)}, u32[]{:S(2)}, u32[]{:S(2)}) collective-permute-start(bf16[256,256]{1,0:T(8,128)(2,1)S(1)} %get-tuple-element.91), channel_id=1, source_target_pairs={{68,0},{70,2},{72,4},{74,6},{76,8},{78,10},{64,12},{66,14},{84,16}... | collective-permute-start | bytes 393224 | tf_op jit(solution)/shard_map/ppermute | solution.py:35
  110.4 8.8 %collective-permute-start.31 = (bf16[256,256]{1,0:T(8,128)(2,1)S(1)}, bf16[256,256]{1,0:T(8,128)(2,1)S(1)}, u32[]{:S(2)}, u32[]{:S(2)}) collective-permute-start(bf16[256,256]{1,0:T(8,128)(2,1)S(1)} %get-tuple-element.90), channel_id=1, source_target_pairs={{72,0},{74,2},{76,4},{78,6},{64,8},{66,10},{68,12},{70,14},{88,16}... | collective-permute-start | bytes 393224 | tf_op jit(solution)/shard_map/ppermute | solution.py:35
  112.4 13.0 %copy-start.5 = (f32[256,256]{0,1:T(8,128)S(1)}, f32[256,256]{0,1:T(8,128)}, u32[]{:S(2)}) copy-start(f32[256,256]{0,1:T(8,128)} %copy.24) | copy-start | bytes 786436
  112.4 8.8 %collective-permute-start.30 = (bf16[256,256]{1,0:T(8,128)(2,1)S(1)}, bf16[256,256]{1,0:T(8,128)(2,1)S(1)}, u32[]{:S(2)}, u32[]{:S(2)}) collective-permute-start(bf16[256,256]{1,0:T(8,128)(2,1)S(1)} %get-tuple-element.89), channel_id=1, source_target_pairs={{76,0},{78,2},{64,4},{66,6},{68,8},{70,10},{72,12},{74,14},{92,16}... | collective-permute-start | bytes 393224 | tf_op jit(solution)/shard_map/ppermute | solution.py:35
  113.7 8.3 %collective-permute-start.29 = (bf16[256,256]{1,0:T(8,128)(2,1)S(1)}, bf16[256,256]{1,0:T(8,128)(2,1)S(1)}, u32[]{:S(2)}, u32[]{:S(2)}) collective-permute-start(bf16[256,256]{1,0:T(8,128)(2,1)S(1)} %get-tuple-element.88), channel_id=1, source_target_pairs={{64,0},{66,2},{68,4},{70,6},{72,8},{74,10},{76,12},{78,14},{80,16}... | collective-permute-start | bytes 393224 | tf_op jit(solution)/shard_map/ppermute | solution.py:35
  114.2 7.8 %collective-permute-start.28 = (bf16[256,256]{1,0:T(8,128)(2,1)S(1)}, bf16[256,256]{1,0:T(8,128)(2,1)S(1)}, u32[]{:S(2)}, u32[]{:S(2)}) collective-permute-start(bf16[256,256]{1,0:T(8,128)(2,1)S(1)} %get-tuple-element.87), channel_id=1, source_target_pairs={{16,0},{18,2},{20,4},{22,6},{24,8},{26,10},{28,12},{30,14},{32,16}... | collective-permute-start | bytes 393224 | tf_op jit(solution)/shard_map/ppermute | solution.py:35
  114.7 7.3 %collective-permute-start.27 = (bf16[256,256]{1,0:T(8,128)(2,1)S(1)}, bf16[256,256]{1,0:T(8,128)(2,1)S(1)}, u32[]{:S(2)}, u32[]{:S(2)}) collective-permute-start(bf16[256,256]{1,0:T(8,128)(2,1)S(1)} %get-tuple-element.86), channel_id=1, source_target_pairs={{32,0},{34,2},{36,4},{38,6},{40,8},{42,10},{44,12},{46,14},{48,16}... | collective-permute-start | bytes 393224 | tf_op jit(solution)/shard_map/ppermute | solution.py:35
  119.2 6.2 %collective-permute-start.26 = (bf16[256,256]{1,0:T(8,128)(2,1)S(1)}, bf16[256,256]{1,0:T(8,128)(2,1)S(1)}, u32[]{:S(2)}, u32[]{:S(2)}) collective-permute-start(bf16[256,256]{1,0:T(8,128)(2,1)S(1)} %get-tuple-element.85), channel_id=1, source_target_pairs={{48,0},{50,2},{52,4},{54,6},{56,8},{58,10},{60,12},{62,14},{0,16},... | collective-permute-start | bytes 393224 | tf_op jit(solution)/shard_map/ppermute | solution.py:35
  (4 other events, 8.6 us)

commit v3 on v2

v3 whole, which is shorter than its diff:
```python
import jax
import jax.numpy as jnp
from jax import lax
from jax.experimental import pallas as pl
from jax.experimental.pallas import tpu as pltpu
from jax.sharding import PartitionSpec as P

learn_rate = 0.5
weight_decay = 0.1
TILE = 128
SLOTS = 4
XS, YS, ZS, CORES = 2, 4, 4, 2
RING = 4
PAIR = 2


def place(index):
    return (
        index // (YS * ZS * CORES),
        index // (ZS * CORES) % YS,
        index // CORES % ZS,
        index % CORES,
    )


def moved(index, way):
    at = [(a + d) % n for a, d, n in zip(place(index), way, (XS, YS, ZS, CORES))]
    return ((at[0] * YS + at[1]) * ZS + at[2]) * CORES + at[3]


def fetch(block, x=0, y=0, z=0, core=0):
    count = XS * YS * ZS * CORES
    route = [(moved(i, (x, y, z, core)), i) for i in range(count)]
    return lax.ppermute(block, "blk", route)


def exchange_along_y(blocks):
    lines = [
        [((x * YS + y) * ZS + z) * CORES + core for y in range(YS)]
        for x in range(XS)
        for z in range(ZS)
        for core in range(CORES)
    ]
    return lax.all_to_all(blocks, "blk", 0, 0, axis_index_groups=lines, tiled=True)


def adagrad(param, squares, grad, num_slabs):
    step_grad = grad / num_slabs + weight_decay * param
    total = squares + step_grad * step_grad
    return param - learn_rate * step_grad / jnp.sqrt(total)


def owner_at(here, part, step, lane):
    x, y, z, _ = here
    if part == 0:
        return (x * YS + lane) * ZS + (z + step) % ZS
    return ((1 - x) * YS + (y + step) % YS) * ZS + (z + lane) % ZS


def tile_kernel(pieces, outs, *refs):
    size = len(pieces)
    device_ref, near_ref, far_ref, near_live, far_live, own_ratings, own_masks = refs[:7]
    far_ratings, far_masks = refs[7:9]
    item_rows = refs[9 : 9 + size]
    user_rows, user_cols, user_before = refs[9 + size : 12 + size]
    item_out = refs[12 + size : 12 + size + len(outs)]
    user_grad = refs[12 + size + len(outs)]
    owners_ref, rows_ref, grads_ref, ratings, masks, tile_sems, row_sems, out_sems = refs[
        13 + size + len(outs) :
    ]
    here = place(device_ref[0])
    core = here[3]
    blocks = user_rows.shape[0] // 2
    total = rows_ref.shape[0]

    def tile_copies(n):
        owner = owners_ref[n]
        near, far = pl.ds(0, SLOTS), pl.ds(SLOTS, SLOTS)
        pairs = (
            (own_ratings.at[owner, core], ratings.at[n, near]),
            (own_masks.at[owner, core], masks.at[n, near]),
            (far_ratings.at[owner, core], ratings.at[n, far]),
            (far_masks.at[owner, core], masks.at[n, far]),
        )
        return [
            pltpu.make_async_copy(source, target, tile_sems.at[n, i])
            for i, (source, target) in enumerate(pairs)
        ]

    row_copies, at = [], 0
    for a, (part, step, first, lanes) in enumerate(pieces):
        row_copies.append(
            pltpu.make_async_copy(item_rows[a], rows_ref.at[pl.ds(at, lanes)], row_sems.at[a])
        )
        row_copies[-1].start()
        for lane in range(lanes):
            owners_ref[at + lane] = owner_at(here, part, step, first + lane)
            for copy in tile_copies(at + lane):
                copy.start()
        at += lanes
    out_copies = [
        pltpu.make_async_copy(grads_ref.at[pl.ds(b * RING, RING)], item_out[b], out_sems.at[b])
        for b in range(len(outs))
    ]
    if user_before is None:
        user_grad[...] = jnp.zeros_like(user_grad)
    else:
        row_copies.append(pltpu.make_async_copy(user_before, user_grad, row_sems.at[size]))
        row_copies[-1].start()
    for copy in row_copies:
        copy.wait()

    def predict(n, live, tiles):
        rows = rows_ref[n]
        first = (owners_ref[n] * CORES + core) * SLOTS
        places = []
        for t in range(tiles):
            far = t >= live[0]
            slot = jnp.where(far, jnp.minimum(t - live[0], SLOTS - 1), t)
            at = first + slot
            code = jnp.where(far, far_ref[0, at] + 2 * blocks, near_ref[0, at])
            block, within = code // 2, code % 2
            alive = t < live[0] + live[1]
            places.append((jnp.where(far, slot + SLOTS, slot), block, within, alive))
        picked = jnp.concatenate([user_rows[block] for _, block, _, _ in places], 0)
        predicted = lax.dot_general(
            picked, rows, (((1,), (1,)), ((), ())), preferred_element_type=jnp.float32
        )
        return places, rows, predicted

    def residuals(n, places, predicted):
        wide = []
        for t, (slot, _, within, alive) in enumerate(places):
            part = predicted[t * TILE : (t + 1) * TILE]
            second = within == 1
            chosen = jnp.where(second, part[:, TILE:], part[:, :TILE])
            observed = jnp.maximum(masks[n, slot].astype(jnp.float32), 0.0)
            residual = observed * (chosen - ratings[n, slot].astype(jnp.float32))
            residual = residual.astype(jnp.bfloat16)
            none = jnp.zeros_like(residual)
            low = jnp.where(jnp.logical_and(alive, within == 0), residual, none)
            high = jnp.where(jnp.logical_and(alive, second), residual, none)
            wide.append(jnp.concatenate([low, high], 1))
        return jnp.concatenate(wide, 0)

    def together(entries, lives, tiles):
        firsts = [predict(n, live, tiles) for n, live in zip(entries, lives)]
        wides = [
            residuals(n, places, predicted)
            for n, (places, _, predicted) in zip(entries, firsts)
        ]
        user_parts = []
        for n, (places, rows, _), wide in zip(entries, firsts, wides):
            user_parts.append(jnp.dot(wide, rows, preferred_element_type=jnp.float32))
            turned = jnp.concatenate([user_cols[block] for _, block, _, _ in places], 1)
            grads_ref[n] = jnp.dot(turned, wide, preferred_element_type=jnp.float32).astype(
                jnp.bfloat16
            )
        for (places, _, _), user_part in zip(firsts, user_parts):
            for t, (_, block, _, _) in enumerate(places):
                user_grad[block] += user_part[t * TILE : (t + 1) * TILE]

    def some(i, carry):
        entries = [i * PAIR + k for k in range(PAIR)]
        lives = []
        for n in entries:
            for copy in tile_copies(n):
                copy.wait()
            at = owners_ref[n] * CORES + core
            lives.append((near_live[0, at], far_live[0, at]))
        most = jnp.maximum(*[live[0] + live[1] for live in lives])
        for tiles in range(2, 2 * SLOTS + 1):
            pl.when(most == tiles)(lambda tiles=tiles: together(entries, lives, tiles))
        for b, copy in enumerate(out_copies):
            pl.when(i == (b + 1) * (RING // PAIR) - 1)(copy.start)
        return carry

    lax.fori_loop(0, total // PAIR, some, 0)
    for copy in out_copies:
        copy.wait()


def tile_terms(pieces, outs, device, indices, own_tiles, far_tiles, item_rows, user_rows, user_cols, user_before):
    _, rows, columns = item_rows[0].shape
    blocks = user_rows.shape[0]
    total = sum(piece[3] for piece in pieces)
    smem = pl.BlockSpec(memory_space=pltpu.SMEM)
    vmem = pl.BlockSpec(memory_space=pltpu.VMEM)
    hbm = pl.BlockSpec(memory_space=pltpu.HBM)
    anywhere = pl.BlockSpec(memory_space=pl.ANY)

    first = user_before is None

    def kernel(*refs):
        cut = 11 + len(pieces)
        tile_kernel(pieces, outs, *refs[:cut], *((None,) if first else ()), *refs[cut:])

    result = pl.pallas_call(
        kernel,
        out_shape=[jax.ShapeDtypeStruct((RING, columns, rows), jnp.bfloat16)] * len(outs)
        + [jax.ShapeDtypeStruct((blocks, TILE, columns), jnp.float32)],
        in_specs=[smem] * 5 + [hbm] * 4 + [anywhere] * len(pieces) + [vmem] * 2
        + [anywhere] * (not first),
        out_specs=[anywhere] * len(outs) + [vmem],
        scratch_shapes=[
            pltpu.SMEM((total,), jnp.int32),
            pltpu.VMEM((total, rows, columns), jnp.bfloat16),
            pltpu.VMEM((total, columns, rows), jnp.bfloat16),
            pltpu.VMEM((total, 2 * SLOTS, TILE, TILE), jnp.bfloat16),
            pltpu.VMEM((total, 2 * SLOTS, TILE, TILE), jnp.bfloat16),
            pltpu.SemaphoreType.DMA((total, 4)),
            pltpu.SemaphoreType.DMA((len(pieces) + 1,)),
            pltpu.SemaphoreType.DMA((len(outs),)),
        ],
        compiler_params=pltpu.CompilerParams(vmem_limit_bytes=32 << 20),
        cost_estimate=pl.CostEstimate(
            flops=total * (3 << 28), bytes_accessed=total << 20, transcendentals=0
        ),
    )(device, *indices, *own_tiles, *far_tiles, *item_rows, user_rows, user_cols, *(() if first else (user_before,)))
    return result[: len(outs)], result[len(outs)]


def in_hbm(array):
    return pltpu.with_memory_space_constraint(array, pltpu.HBM)


def added(*terms):
    return sum(term.astype(jnp.float32) for term in terms)


def body(
    user_factors,
    item_factors,
    user_accum,
    item_accum,
    ratings,
    masks,
    tile_users,
    tile_items,
    tile_counts,
):
    low = jnp.bfloat16
    num_slabs = lax.axis_size("blk")
    columns = user_factors.shape[1]
    owners = num_slabs // CORES
    device = lax.axis_index("blk")

    near = tile_users * 2 + tile_items % 2
    far, far_live = fetch(near, core=1), fetch(tile_counts, core=1)
    user_low = user_factors.astype(low).reshape(-1, TILE, columns)
    blocks = user_low.shape[0]
    far_rows = fetch(user_low, core=1)
    item_low = item_factors.astype(low)
    cross = fetch(item_low, x=1)
    shape = (owners, CORES, SLOTS, TILE, TILE)
    own_tiles = [ratings.reshape(shape), masks.reshape(shape)]
    first, second, cross, far, far_live, far_rows = lax.optimization_barrier(
        (*own_tiles, cross, far, far_live, far_rows)
    )
    far_tiles = [fetch(first, core=1), fetch(second, core=1)]
    user_rows = jnp.concatenate([user_low, far_rows], 0)

    own_line = exchange_along_y(jnp.broadcast_to(item_low, (YS,) + item_low.shape))
    far_line = [cross] + [fetch(cross, z=d) for d in range(1, RING)]
    own_line, far_line, user_rows, far_tiles[0] = lax.optimization_barrier(
        (own_line, far_line, user_rows, far_tiles[0])
    )
    user_cols = user_rows.swapaxes(1, 2)
    rows = [own_line, jnp.stack(far_line)]
    ahead = [fetch(rows[0], z=1), fetch(rows[1], y=1)]
    behind = [fetch(rows[0], z=-1), fetch(rows[1], y=-1)]

    def terms(pieces, outs, item_rows, user_before):
        return tile_terms(
            pieces,
            outs,
            device[None],
            (near, far, tile_counts, far_live),
            [in_hbm(array) for array in own_tiles],
            [in_hbm(array) for array in far_tiles],
            item_rows,
            user_rows,
            user_cols,
            user_before,
        )

    here_terms, user_first = terms(
        ((0, 0, 0, RING), (1, 0, 0, RING)), ((0, 0), (1, 0)), rows, None
    )
    rows, ahead, behind, here_terms, user_first = lax.optimization_barrier(
        (rows, ahead, behind, here_terms, user_first)
    )
    across = [fetch(rows[0], z=2), fetch(rows[1], y=2)]
    near_terms, user_second = terms(
        ((0, 1, 0, RING), (1, 1, 0, RING), (0, 3, 0, RING), (1, 3, 0, RING)),
        ((0, 1), (1, 1), (0, 3), (1, 3)),
        [ahead[0], ahead[1], behind[0], behind[1]],
        user_first,
    )
    across_terms, user_grad = terms(
        ((0, 2, 0, RING), (1, 2, 0, RING)), ((0, 2), (1, 2)), across, user_second
    )
    arrived = [
        [fetch(near_terms[0], z=-1), fetch(near_terms[2], z=1)],
        [fetch(near_terms[1], y=-1), fetch(near_terms[3], y=1)],
    ]
    arrived, across_terms = lax.optimization_barrier((arrived, across_terms))

    far_grad = fetch(user_grad[blocks:].astype(low), core=1)
    half = (user_grad[:blocks] + far_grad.astype(jnp.float32)).astype(low)
    own_last, far_last = fetch(across_terms[0], z=2), fetch(across_terms[1], y=2)
    half, own_last, far_last = lax.optimization_barrier((half, own_last, far_last))
    other = lax.ppermute(half, "rep", [(0, 1), (1, 0)])
    user_sum = added(half, other)
    own_sum = added(here_terms[0], *arrived[0], own_last).astype(low)
    far_sum = [
        added(here_terms[1][k], *[a[k] for a in arrived[1]], far_last[k]).astype(low)
        for k in range(RING)
    ]
    own_sum, far_sum = lax.optimization_barrier((own_sum, far_sum))
    cross_sum = added(far_sum[0], *[fetch(far_sum[d], z=-d) for d in range(1, RING)]).astype(low)
    cross_sum, other = lax.optimization_barrier((cross_sum, other))
    user_sum = added(half, other)
    item_sum = added(
        jnp.sum(exchange_along_y(own_sum).astype(jnp.float32), 0),
        fetch(cross_sum, x=1),
    ).T
    new_users = adagrad(user_factors, user_accum, user_sum.reshape(user_factors.shape), num_slabs)
    new_items = adagrad(item_factors, item_accum, item_sum, num_slabs)
    return (new_users, new_items)


def solution(mesh):
    in_specs = (
        P("blk", None),
        P(("blk", "rep"), None),
        P("blk", None),
        P(("blk", "rep"), None),
        P("blk", "rep", None, None),
        P("blk", "rep", None, None),
        P("blk", "rep"),
        P("blk", "rep"),
        P("blk", "rep"),
    )
    out_specs = (P("blk", None), P(("blk", "rep"), None))
    return jax.shard_map(body, mesh=mesh, in_specs=in_specs, out_specs=out_specs, check_vma=False)
```

time: 127 us -> 118 us (0.929)
  Pallas kernels: 32 us -> 25.5 us
  waiting for transfers between devices: 34.7 us -> 39.7 us
  local copies, waits for them, and re-layouts: 6.57 us -> 2.81 us
  starting transfers between devices: 44.1 us -> 40.4 us
  other arithmetic: 7.95 us -> 9.24 us
    ppermute x32 -> x26, starting transfers between devices: 41.7 us -> 30.6 us  [fetch(): return lax.ppermute(block, 'blk', route)]
    all_to_all x0 -> x2, starting transfers between devices: none -> 7.93 us  [exchange_along_y(): lax.all_to_all(blocks, 'blk', 0, 0, axis_index_groups=lines, tiled=True)]
    pallas_call x1 -> x0, Pallas kernels: 6.82 us -> none  [packed_tiles(): pl.pallas_call(pack_kernel, out_shape=jax.ShapeDtypeStruct((2, 2, lanes,...]
    all_to_all x0 -> x2, waiting for transfers between devices: none -> 4.25 us  [exchange_along_y(): lax.all_to_all(blocks, 'blk', 0, 0, axis_index_groups=lines, tiled=True)]
    slice x4 -> x1, local copies, waits for them, and re-layouts: 3.87 us -> 0.05 us  [body(): far_grad = fetch(user_grad[blocks:].astype(low), core=1)]
    add x2 -> x1, other arithmetic: 3.19 us -> 0.96 us  [added(): return sum((term.astype(jnp.float32) for term in terms))]
    ppermute x1, waiting for transfers between devices: 0.01 us -> 1.8 us  [body(): other = lax.ppermute(half, 'rep', [(0, 1), (1, 0)])]
    convert_element_type x2 -> x3, other arithmetic: 0.58 us -> 2.31 us  [the longest x1 1.1 us: body(): added(far_sum[0], *[fetch(far_sum[d], z=-d) for d in range(1, RING)])]
  transfers between devices with their start and end apart: 33 -> 29, of which waited for: 14 -> 16; matrix products, arithmetic and copies ran while one was open for 9% -> 6% of each run, Pallas kernels for 20% -> 21%
where the time goes in v3:
time: 118 us; the launch traced here: 119 us
  starting transfers between devices  40.4 us (34%)
  waiting for transfers between devices  39.7 us (34%)
  Pallas kernels  25.5 us (22%)
  other arithmetic  9.24 us (8%)
  local copies, waits for them, and re-layouts  2.81 us (2%)
    ppermute x26, waiting for transfers between devices, fetch(): return lax.ppermute(block, 'blk', route)  33.7 us
    ppermute x26, starting transfers between devices, fetch(): return lax.ppermute(block, 'blk', route)  30.6 us
    pallas_call x3, Pallas kernels, tile_terms(): pl.pallas_call(kernel, out_shape=[jax.ShapeDtypeStruct((RING, columns, ro...  25.5 us
    all_to_all x2, starting transfers between devices, exchange_along_y(): lax.all_to_all(blocks, 'blk', 0, 0, axis_index_groups=lines, tiled=True)  7.93 us
    all_to_all x2, waiting for transfers between devices, exchange_along_y(): lax.all_to_all(blocks, 'blk', 0, 0, axis_index_groups=lines, tiled=True)  4.25 us
    sub x2, other arithmetic, adagrad(): return param - learn_rate * step_grad / jnp.sqrt(total)  2.64 us
  transfers between devices with their start and end apart: 29, of which 16 were waited for; matrix products, arithmetic and copies ran while one was open for 6% of the time, Pallas kernels for 21%

profile of v3, /device:TPU:2, one launch (start us, length us, event | category | flops | bytes accessed | tf_op | source)
XLA Modules:
  0.0 118.5 jit_solution(9857826643154461479)
XLA Ops:
  0.6 1.3 %convert_element_type.124 = bf16[1024,256]{1,0:T(8,128)(2,1)S(1)} convert(f32[1024,256]{1,0:T(8,128)} %param.9) | non-fusion elementwise | flops 262144 | bytes 1572864 | tf_op jit(solution)/shard_map/convert_element_type | solution.py:250
  2.3 1.0 convert_element_type.123
  3.3 0.5 collective-permute-start
  3.8 0.7 fusion.4.refs_1_
  5.1 1.0 collective-permute-done.2.refs_4_
  6.1 3.2 %collective-permute-done = bf16[256,256]{1,0:T(8,128)(2,1)S(1)} collective-permute-done((bf16[256,256]{1,0:T(8,128)(2,1)S(1)}, bf16[256,256]{1,0:T(8,128)(2,1)S(1)}, u32[]{:S(2)}, u32[]{:S(2)}) %collective-permute-start) | collective-permute-done | bytes 131104 | tf_op jit(solution)/shard_map/ppermute | solution.py:34
  9.3 0.5 collective-permute-start.8
  9.8 0.8 broadcast_in_dim.9
  10.6 4.5 %all-to-all-start = ((bf16[4,256,256]{2,1,0:T(8,128)(2,1)}), bf16[4,256,256]{2,1,0:T(8,128)(2,1)S(1)}, u32[]{:S(2)}, u32[]{:S(2)}) async-start(bf16[4,256,256]{2,1,0:T(8,128)(2,1)} %broadcast_in_dim.9), calls=%async_computation | async-start | bytes 1048576 | tf_op jit(solution)/shard_map/all_to_all | solution.py:44
  15.1 4.0 %collective-permute-start.4 = (bf16[256,256]{1,0:T(8,128)(2,1)S(1)}, bf16[256,256]{1,0:T(8,128)(2,1)S(1)}, u32[]{:S(2)}, u32[]{:S(2)}) collective-permute-start(bf16[256,256]{1,0:T(8,128)(2,1)S(1)} %collective-permute-done), channel_id=1, source_target_pairs={{4,0},{6,2},{8,4},{10,6},{12,8},{14,10},{0,12},{2,14},{20,16},{22,... | collective-permute-start | bytes 393224 | tf_op jit(solution)/shard_map/ppermute | solution.py:34
  19.1 1.3 %collective-permute-start.6 = (bf16[256,256]{1,0:T(8,128)(2,1)S(1)}, bf16[256,256]{1,0:T(8,128)(2,1)S(1)}, u32[]{:S(2)}, u32[]{:S(2)}) collective-permute-start(bf16[256,256]{1,0:T(8,128)(2,1)S(1)} %collective-permute-done), channel_id=1, source_target_pairs={{12,0},{14,2},{0,4},{2,6},{4,8},{6,10},{8,12},{10,14},{28,16},{30,... | collective-permute-start | bytes 393224 | tf_op jit(solution)/shard_map/ppermute | solution.py:34
  20.5 4.3 %all-to-all-done.refs_9_ = bf16[4,256,256]{2,1,0:T(8,128)(2,1)S(1)} async-done(((bf16[4,256,256]{2,1,0:T(8,128)(2,1)}), bf16[4,256,256]{2,1,0:T(8,128)(2,1)S(1)}, u32[]{:S(2)}, u32[]{:S(2)}) %all-to-all-start) | async-done | bytes 524320 | tf_op jit(solution)/shard_map/all_to_all | solution.py:44
  24.7 2.2 %collective-permute-done.5 = bf16[256,256]{1,0:T(8,128)(2,1)S(1)} collective-permute-done((bf16[256,256]{1,0:T(8,128)(2,1)S(1)}, bf16[256,256]{1,0:T(8,128)(2,1)S(1)}, u32[]{:S(2)}, u32[]{:S(2)}) %collective-permute-start.5) | collective-permute-done | bytes 131104 | tf_op jit(solution)/shard_map/ppermute | solution.py:34
  26.9 1.1 collective-permute-done.6
  28.1 3.0 %collective-permute-start.10 = (bf16[4,256,256]{2,1,0:T(8,128)(2,1)S(1)}, bf16[4,256,256]{2,1,0:T(8,128)(2,1)}, u32[]{:S(2)}, u32[]{:S(2)}) collective-permute-start(bf16[4,256,256]{2,1,0:T(8,128)(2,1)S(1)} %pad_maximum_fusion.1.refs_10_), channel_id=1, source_target_pairs={{16,0},{18,2},{20,4},{22,6},{24,8},{26,10},{28,12},{30,14},{32,16}... | collective-permute-start | bytes 1572872 | tf_op jit(solution)/shard_map/ppermute | solution.py:34
  31.1 3.2 %collective-permute-start.9 = (bf16[4,256,256]{2,1,0:T(8,128)(2,1)S(1)}, bf16[4,256,256]{2,1,0:T(8,128)(2,1)}, u32[]{:S(2)}, u32[]{:S(2)}) collective-permute-start(bf16[4,256,256]{2,1,0:T(8,128)(2,1)S(1)} %all-to-all-done.refs_9_), channel_id=1, source_target_pairs={{4,0},{6,2},{8,4},{10,6},{12,8},{14,10},{0,12},{2,14},{20,16},{22,... | collective-permute-start | bytes 1572872 | tf_op jit(solution)/shard_map/ppermute | solution.py:34
  34.3 0.5 copy.20.refs_11_.refs_13_
  34.9 5.9 %shard_map.104 = (bf16[4,256,256]{2,1,0:T(8,128)(2,1)S(1)}, bf16[4,256,256]{2,1,0:T(8,128)(2,1)S(1)}, f32[16,128,256]{2,1,0:T(8,128)S(1)}) custom-call(s32[1]{0:T(128)} %bitcast.refs_0_, s32[1,256]{1,0:T(1,128)S(1)} %fusion.4.refs_1_, s32[1,256]{1,0:T(1,128)S(1)} %collective-permute-done.1.refs_2_, s32[1,64]{1,0:T(1,128)S(1)} %copy-done, ...), custom_call_target="tpu_custom_call" | custom-call | flops 6442450944 | bytes 8388608 | tf_op jit(solution)/shard_map/pallas_call | solution.py:198
  40.7 1.3 %collective-permute-done.10.refs_10_ = bf16[4,256,256]{2,1,0:T(8,128)(2,1)} collective-permute-done((bf16[4,256,256]{2,1,0:T(8,128)(2,1)S(1)}, bf16[4,256,256]{2,1,0:T(8,128)(2,1)}, u32[]{:S(2)}, u32[]{:S(2)}) %collective-permute-start.10) | collective-permute-done | bytes 524320 | tf_op jit(solution)/shard_map/ppermute | solution.py:34
  42.1 3.5 %collective-permute-done.12.refs_12_ = bf16[4,256,256]{2,1,0:T(8,128)(2,1)} collective-permute-done((bf16[4,256,256]{2,1,0:T(8,128)(2,1)S(1)}, bf16[4,256,256]{2,1,0:T(8,128)(2,1)}, u32[]{:S(2)}, u32[]{:S(2)}) %collective-permute-start.12) | collective-permute-done | bytes 524320 | tf_op jit(solution)/shard_map/ppermute | solution.py:34
  45.6 1.5 %collective-permute-start.13 = (bf16[4,256,256]{2,1,0:T(8,128)(2,1)S(1)}, bf16[4,256,256]{2,1,0:T(8,128)(2,1)S(1)}, u32[]{:S(2)}, u32[]{:S(2)}) collective-permute-start(bf16[4,256,256]{2,1,0:T(8,128)(2,1)S(1)} %all-to-all-done.refs_9_), channel_id=1, source_target_pairs={{8,0},{10,2},{12,4},{14,6},{0,8},{2,10},{4,12},{6,14},{24,16},{26,... | collective-permute-start | bytes 1572872 | tf_op jit(solution)/shard_map/ppermute | solution.py:34
  47.1 2.0 %collective-permute-start.14 = (bf16[4,256,256]{2,1,0:T(8,128)(2,1)S(1)}, bf16[4,256,256]{2,1,0:T(8,128)(2,1)S(1)}, u32[]{:S(2)}, u32[]{:S(2)}) collective-permute-start(bf16[4,256,256]{2,1,0:T(8,128)(2,1)S(1)} %pad_maximum_fusion.1.refs_10_), channel_id=1, source_target_pairs={{32,0},{34,2},{36,4},{38,6},{40,8},{42,10},{44,12},{46,14},{48,16}... | collective-permute-start | bytes 1572872 | tf_op jit(solution)/shard_map/ppermute | solution.py:34
  49.1 13.3 %shard_map.105 = (bf16[4,256,256]{2,1,0:T(8,128)(2,1)S(1)}, bf16[4,256,256]{2,1,0:T(8,128)(2,1)S(1)}, bf16[4,256,256]{2,1,0:T(8,128)(2,1)S(1)}, bf16[4,256,256]{2,1,0:T(8,128)(2,1)S(1)}, f32[16,128,256]{2,1,0:T(8,128)S(1)}) custom-call(s32[1]{0:T(128)} %bitcast.refs_0_, s32[1,256]{1,0:T(1,128)S(1)} %fusion.4.refs_1_, ...), custom_call_target="tpu_custom_call" | custom-call | flops 12884901888 | bytes 16777216 | tf_op jit(solution)/shard_map/pallas_call | solution.py:198
  62.4 2.9 %collective-permute-start.16 = (bf16[4,256,256]{2,1,0:T(8,128)(2,1)S(1)}, bf16[4,256,256]{2,1,0:T(8,128)(2,1)S(1)}, u32[]{:S(2)}, u32[]{:S(2)}) collective-permute-start(bf16[4,256,256]{2,1,0:T(8,128)(2,1)S(1)} %get-tuple-element.76), channel_id=1, source_target_pairs={{12,0},{14,2},{0,4},{2,6},{4,8},{6,10},{8,12},{10,14},{28,16},{30,... | collective-permute-start | bytes 1572872 | tf_op jit(solution)/shard_map/ppermute | solution.py:34
  65.7 1.4 %collective-permute-start.18 = (bf16[4,256,256]{2,1,0:T(8,128)(2,1)S(1)}, bf16[4,256,256]{2,1,0:T(8,128)(2,1)S(1)}, u32[]{:S(2)}, u32[]{:S(2)}) collective-permute-start(bf16[4,256,256]{2,1,0:T(8,128)(2,1)S(1)} %get-tuple-element.78), channel_id=1, source_target_pairs={{48,0},{50,2},{52,4},{54,6},{56,8},{58,10},{60,12},{62,14},{0,16},... | collective-permute-start | bytes 1572872 | tf_op jit(solution)/shard_map/ppermute | solution.py:34
  67.1 1.9 %collective-permute-start.19 = (bf16[4,256,256]{2,1,0:T(8,128)(2,1)S(1)}, bf16[4,256,256]{2,1,0:T(8,128)(2,1)S(1)}, u32[]{:S(2)}, u32[]{:S(2)}) collective-permute-start(bf16[4,256,256]{2,1,0:T(8,128)(2,1)S(1)} %get-tuple-element.79), channel_id=1, source_target_pairs={{16,0},{18,2},{20,4},{22,6},{24,8},{26,10},{28,12},{30,14},{32,16}... | collective-permute-start | bytes 1572872 | tf_op jit(solution)/shard_map/ppermute | solution.py:34
  69.0 6.3 %shard_map.106 = (bf16[4,256,256]{2,1,0:T(8,128)(2,1)S(1)}, bf16[4,256,256]{2,1,0:T(8,128)(2,1)S(1)}, f32[16,128,256]{2,1,0:T(8,128)S(1)}) custom-call(s32[1]{0:T(128)} %bitcast.refs_0_, s32[1,256]{1,0:T(1,128)S(1)} %fusion.4.refs_1_, s32[1,256]{1,0:T(1,128)S(1)} %collective-permute-done.1.refs_2_, s32[1,64]{1,0:T(1,128)S(1)} %copy-done, ...), custom_call_target="tpu_custom_call" | custom-call | flops 6442450944 | bytes 8388608 | tf_op jit(solution)/shard_map/pallas_call | solution.py:198
  75.4 0.7 collective-permute-done.16
  76.2 2.7 %collective-permute-done.18 = bf16[4,256,256]{2,1,0:T(8,128)(2,1)S(1)} collective-permute-done((bf16[4,256,256]{2,1,0:T(8,128)(2,1)S(1)}, bf16[4,256,256]{2,1,0:T(8,128)(2,1)S(1)}, u32[]{:S(2)}, u32[]{:S(2)}) %collective-permute-start.18) | collective-permute-done | bytes 524320 | tf_op jit(solution)/shard_map/ppermute | solution.py:34
  78.8 0.4 collective-permute-start.20
  79.3 1.1 collective-permute-start.21
  80.5 10.9 %collective-permute-done.20 = bf16[4,256,256]{2,1,0:T(8,128)(2,1)S(1)} collective-permute-done((bf16[4,256,256]{2,1,0:T(8,128)(2,1)S(1)}, bf16[4,256,256]{2,1,0:T(8,128)(2,1)S(1)}, u32[]{:S(2)}, u32[]{:S(2)}) %collective-permute-start.20) | collective-permute-done | bytes 524320 | tf_op jit(solution)/shard_map/ppermute | solution.py:34
  91.4 1.6 %collective-permute-done.21 = bf16[4,256,256]{2,1,0:T(8,128)(2,1)S(1)} collective-permute-done((bf16[4,256,256]{2,1,0:T(8,128)(2,1)S(1)}, bf16[4,256,256]{2,1,0:T(8,128)(2,1)S(1)}, u32[]{:S(2)}, u32[]{:S(2)}) %collective-permute-start.21) | collective-permute-done | bytes 524320 | tf_op jit(solution)/shard_map/ppermute | solution.py:34
  93.0 1.0 fusion.3
  93.9 1.1 add_convert_fusion
  95.0 3.5 %all-to-all-start.1 = ((bf16[4,256,256]{2,1,0:T(8,128)(2,1)}), bf16[4,256,256]{2,1,0:T(8,128)(2,1)S(1)}, u32[]{:S(2)}, u32[]{:S(2)}) async-start(bf16[4,256,256]{2,1,0:T(8,128)(2,1)} %add_convert_fusion), calls=%async_computation.1 | async-start | bytes 1048576 | tf_op jit(solution)/shard_map/all_to_all | solution.py:44
  98.5 1.9 %collective-permute-start.25 = (bf16[8,128,256]{2,1,0:T(8,128)(2,1)S(1)}, bf16[8,128,256]{2,1,0:T(8,128)(2,1)S(1)}, u32[]{:S(2)}, u32[]{:S(2)}) collective-permute-start(bf16[8,128,256]{2,1,0:T(8,128)(2,1)S(1)} %add_convert_fusion.1), channel_id=1, source_target_pairs={{0,1},{1,0},{2,3},{3,2},{4,5},{5,4},{6,7},{7,6},{8,9},{9,8},{10,11... | collective-permute-start | bytes 1572872 | tf_op jit(solution)/shard_map/ppermute | solution.py:313
  100.3 0.7 collective-permute-start.22
  101.0 3.3 %collective-permute-start.23 = (bf16[256,256]{1,0:T(8,128)(2,1)}, bf16[256,256]{1,0:T(8,128)(2,1)}, u32[]{:S(2)}, u32[]{:S(2)}) collective-permute-start(bf16[256,256]{1,0:T(8,128)(2,1)} %get-tuple-element.95), channel_id=1, source_target_pairs={{8,0},{10,2},{12,4},{14,6},{0,8},{2,10},{4,12},{6,14},{24,16},{26,... | collective-permute-start | bytes 393224 | tf_op jit(solution)/shard_map/ppermute | solution.py:34
  104.3 1.7 %collective-permute-start.24 = (bf16[256,256]{1,0:T(8,128)(2,1)}, bf16[256,256]{1,0:T(8,128)(2,1)}, u32[]{:S(2)}, u32[]{:S(2)}) collective-permute-start(bf16[256,256]{1,0:T(8,128)(2,1)} %get-tuple-element.96), channel_id=1, source_target_pairs={{4,0},{6,2},{8,4},{10,6},{12,8},{14,10},{0,12},{2,14},{20,16},{22,... | collective-permute-start | bytes 393224 | tf_op jit(solution)/shard_map/ppermute | solution.py:34
  106.3 0.5 collective-permute-done.22
  106.8 2.2 %collective-permute-done.23 = bf16[256,256]{1,0:T(8,128)(2,1)} collective-permute-done((bf16[256,256]{1,0:T(8,128)(2,1)}, bf16[256,256]{1,0:T(8,128)(2,1)}, u32[]{:S(2)}, u32[]{:S(2)}) %collective-permute-start.23) | collective-permute-done | bytes 131104 | tf_op jit(solution)/shard_map/ppermute | solution.py:34
  109.0 0.6 collective-permute-done.24
  109.6 1.1 add_convert_fusion.2
  110.8 1.8 %collective-permute-done.25 = bf16[8,128,256]{2,1,0:T(8,128)(2,1)S(1)} collective-permute-done((bf16[8,128,256]{2,1,0:T(8,128)(2,1)S(1)}, bf16[8,128,256]{2,1,0:T(8,128)(2,1)S(1)}, u32[]{:S(2)}, u32[]{:S(2)}) %collective-permute-start.25) | collective-permute-done | bytes 524320 | tf_op jit(solution)/shard_map/ppermute | solution.py:313
  112.8 2.5 %multiply_subtract_fusion = f32[1024,256]{1,0:T(8,128)} fusion(f32[1024,256]{1,0:T(8,128)S(1)} %copy-done.1, f32[1024,256]{1,0:T(8,128)} %param.11, f32[8,128,256]{2,1,0:T(8,128)S(1)} %add_multiply_fusion), kind=kLoop, calls=%fused_computation.4 | loop fusion | flops 1835008 | bytes 4194304 | tf_op jit(solution)/shard_map/sub | solution.py:50
  115.3 2.3 %collective-permute-done.26 = bf16[256,256]{1,0:T(8,128)(2,1)S(1)} collective-permute-done((bf16[256,256]{1,0:T(8,128)(2,1)S(1)}, bf16[256,256]{1,0:T(8,128)(2,1)S(1)}, u32[]{:S(2)}, u32[]{:S(2)}) %collective-permute-start.26) | collective-permute-done | bytes 131104 | tf_op jit(solution)/shard_map/ppermute | solution.py:34
  117.7 0.8 copy.26
  (41 shorter events, 2.4 us)
Async XLA Ops:
  0.6 34.2 %copy-start = (s32[1,64]{1,0:T(1,128)S(1)}, s32[1,64]{1,0:T(1,128)}, u32[]{:S(2)}) copy-start(s32[1,64]{1,0:T(1,128)} %refs_3_.5) | copy-start | bytes 772
  2.2 7.0 %collective-permute-start.3 = (bf16[8,128,256]{1,2,0:T(8,128)(2,1)S(1)}, bf16[8,128,256]{1,2,0:T(8,128)(2,1)S(1)}, u32[]{:S(2)}, u32[]{:S(2)}) collective-permute-start(bf16[8,128,256]{1,2,0:T(8,128)(2,1)S(1)} %copy.18), channel_id=1, source_target_pairs={{2,0},{0,2},{6,4},{4,6},{10,8},{8,10},{14,12},{12,14},{18,16},{16,... | collective-permute-start | bytes 1572872 | tf_op jit(solution)/shard_map/ppermute | solution.py:34
  3.3 6.0 %collective-permute-start = (bf16[256,256]{1,0:T(8,128)(2,1)S(1)}, bf16[256,256]{1,0:T(8,128)(2,1)S(1)}, u32[]{:S(2)}, u32[]{:S(2)}) collective-permute-start(bf16[256,256]{1,0:T(8,128)(2,1)S(1)} %convert_element_type.123), channel_id=1, source_target_pairs={{64,0},{66,2},{68,4},{70,6},{72,8},{74,10},{76,12},{78,14},{80,16}... | collective-permute-start | bytes 393224 | tf_op jit(solution)/shard_map/ppermute | solution.py:34
  4.5 1.5 %collective-permute-start.1 = (s32[1,256]{1,0:T(1,128)S(1)}, s32[1,256]{1,0:T(1,128)S(1)}, u32[]{:S(2)}, u32[]{:S(2)}) collective-permute-start(s32[1,256]{1,0:T(1,128)S(1)} %fusion.4.refs_1_), channel_id=1, source_target_pairs={{2,0},{0,2},{6,4},{4,6},{10,8},{8,10},{14,12},{12,14},{18,16},{16,... | collective-permute-start | bytes 3080 | tf_op jit(solution)/shard_map/ppermute | solution.py:34
  4.8 1.3 %collective-permute-start.2 = (s32[1,64]{1,0:T(1,128)}, s32[1,64]{1,0:T(1,128)S(1)}, u32[]{:S(2)}, u32[]{:S(2)}) collective-permute-start(s32[1,64]{1,0:T(1,128)} %refs_3_.5), channel_id=1, source_target_pairs={{2,0},{0,2},{6,4},{4,6},{10,8},{8,10},{14,12},{12,14},{18,16},{16,... | collective-permute-start | bytes 776 | tf_op jit(solution)/shard_map/ppermute | solution.py:34
  9.3 18.7 %collective-permute-start.7 = (bf16[32,2,4,128,128]{4,3,2,1,0:T(8,128)(2,1)}, bf16[32,2,4,128,128]{4,3,2,1,0:T(8,128)(2,1)}, u32[]{:S(2)}, u32[]{:S(2)}) collective-permute-start(bf16[32,2,4,128,128]{4,3,2,1,0:T(8,128)(2,1)} %bitcast.28), channel_id=1, source_target_pairs={{2,0},{0,2},{6,4},{4,6},{10,8},{8,10},{14,12},{12,14},{18,16},{16,... | collective-permute-start | bytes 25165832 | tf_op jit(solution)/shard_map/ppermute | solution.py:34
  9.3 25.6 %collective-permute-start.8 = (bf16[32,2,4,128,128]{4,3,2,1,0:T(8,128)(2,1)}, bf16[32,2,4,128,128]{4,3,2,1,0:T(8,128)(2,1)}, u32[]{:S(2)}, u32[]{:S(2)}) collective-permute-start(bf16[32,2,4,128,128]{4,3,2,1,0:T(8,128)(2,1)} %bitcast.32), channel_id=1, source_target_pairs={{2,0},{0,2},{6,4},{4,6},{10,8},{8,10},{14,12},{12,14},{18,16},{16,... | collective-permute-start | bytes 25165832 | tf_op jit(solution)/shard_map/ppermute | solution.py:34
  10.6 14.1 %all-to-all-start = ((bf16[4,256,256]{2,1,0:T(8,128)(2,1)}), bf16[4,256,256]{2,1,0:T(8,128)(2,1)S(1)}, u32[]{:S(2)}, u32[]{:S(2)}) async-start(bf16[4,256,256]{2,1,0:T(8,128)(2,1)} %broadcast_in_dim.9), calls=%async_computation | async-start | bytes 1048576 | tf_op jit(solution)/shard_map/all_to_all | solution.py:44
  15.1 9.6 %collective-permute-start.4 = (bf16[256,256]{1,0:T(8,128)(2,1)S(1)}, bf16[256,256]{1,0:T(8,128)(2,1)S(1)}, u32[]{:S(2)}, u32[]{:S(2)}) collective-permute-start(bf16[256,256]{1,0:T(8,128)(2,1)S(1)} %collective-permute-done), channel_id=1, source_target_pairs={{4,0},{6,2},{8,4},{10,6},{12,8},{14,10},{0,12},{2,14},{20,16},{22,... | collective-permute-start | bytes 393224 | tf_op jit(solution)/shard_map/ppermute | solution.py:34
  19.1 7.8 %collective-permute-start.5 = (bf16[256,256]{1,0:T(8,128)(2,1)S(1)}, bf16[256,256]{1,0:T(8,128)(2,1)S(1)}, u32[]{:S(2)}, u32[]{:S(2)}) collective-permute-start(bf16[256,256]{1,0:T(8,128)(2,1)S(1)} %collective-permute-done), channel_id=1, source_target_pairs={{8,0},{10,2},{12,4},{14,6},{0,8},{2,10},{4,12},{6,14},{24,16},{26,... | collective-permute-start | bytes 393224 | tf_op jit(solution)/shard_map/ppermute | solution.py:34
  19.1 8.9 %collective-permute-start.6 = (bf16[256,256]{1,0:T(8,128)(2,1)S(1)}, bf16[256,256]{1,0:T(8,128)(2,1)S(1)}, u32[]{:S(2)}, u32[]{:S(2)}) collective-permute-start(bf16[256,256]{1,0:T(8,128)(2,1)S(1)} %collective-permute-done), channel_id=1, source_target_pairs={{12,0},{14,2},{0,4},{2,6},{4,8},{6,10},{8,12},{10,14},{28,16},{30,... | collective-permute-start | bytes 393224 | tf_op jit(solution)/shard_map/ppermute | solution.py:34
  28.1 14.0 %collective-permute-start.10 = (bf16[4,256,256]{2,1,0:T(8,128)(2,1)S(1)}, bf16[4,256,256]{2,1,0:T(8,128)(2,1)}, u32[]{:S(2)}, u32[]{:S(2)}) collective-permute-start(bf16[4,256,256]{2,1,0:T(8,128)(2,1)S(1)} %pad_maximum_fusion.1.refs_10_), channel_id=1, source_target_pairs={{16,0},{18,2},{20,4},{22,6},{24,8},{26,10},{28,12},{30,14},{32,16}... | collective-permute-start | bytes 1572872 | tf_op jit(solution)/shard_map/ppermute | solution.py:34
  31.1 14.5 %collective-permute-start.12 = (bf16[4,256,256]{2,1,0:T(8,128)(2,1)S(1)}, bf16[4,256,256]{2,1,0:T(8,128)(2,1)}, u32[]{:S(2)}, u32[]{:S(2)}) collective-permute-start(bf16[4,256,256]{2,1,0:T(8,128)(2,1)S(1)} %pad_maximum_fusion.1.refs_10_), channel_id=1, source_target_pairs={{48,0},{50,2},{52,4},{54,6},{56,8},{58,10},{60,12},{62,14},{0,16},... | collective-permute-start | bytes 1572872 | tf_op jit(solution)/shard_map/ppermute | solution.py:34
  31.1 14.5 %collective-permute-start.11 = (bf16[4,256,256]{2,1,0:T(8,128)(2,1)S(1)}, bf16[4,256,256]{2,1,0:T(8,128)(2,1)}, u32[]{:S(2)}, u32[]{:S(2)}) collective-permute-start(bf16[4,256,256]{2,1,0:T(8,128)(2,1)S(1)} %all-to-all-done.refs_9_), channel_id=1, source_target_pairs={{12,0},{14,2},{0,4},{2,6},{4,8},{6,10},{8,12},{10,14},{28,16},{30,... | collective-permute-start | bytes 1572872 | tf_op jit(solution)/shard_map/ppermute | solution.py:34
  31.1 14.5 %collective-permute-start.9 = (bf16[4,256,256]{2,1,0:T(8,128)(2,1)S(1)}, bf16[4,256,256]{2,1,0:T(8,128)(2,1)}, u32[]{:S(2)}, u32[]{:S(2)}) collective-permute-start(bf16[4,256,256]{2,1,0:T(8,128)(2,1)S(1)} %all-to-all-done.refs_9_), channel_id=1, source_target_pairs={{4,0},{6,2},{8,4},{10,6},{12,8},{14,10},{0,12},{2,14},{20,16},{22,... | collective-permute-start | bytes 1572872 | tf_op jit(solution)/shard_map/ppermute | solution.py:34
  45.6 21.5 %collective-permute-start.13 = (bf16[4,256,256]{2,1,0:T(8,128)(2,1)S(1)}, bf16[4,256,256]{2,1,0:T(8,128)(2,1)S(1)}, u32[]{:S(2)}, u32[]{:S(2)}) collective-permute-start(bf16[4,256,256]{2,1,0:T(8,128)(2,1)S(1)} %all-to-all-done.refs_9_), channel_id=1, source_target_pairs={{8,0},{10,2},{12,4},{14,6},{0,8},{2,10},{4,12},{6,14},{24,16},{26,... | collective-permute-start | bytes 1572872 | tf_op jit(solution)/shard_map/ppermute | solution.py:34
  47.1 21.9 %collective-permute-start.14 = (bf16[4,256,256]{2,1,0:T(8,128)(2,1)S(1)}, bf16[4,256,256]{2,1,0:T(8,128)(2,1)S(1)}, u32[]{:S(2)}, u32[]{:S(2)}) collective-permute-start(bf16[4,256,256]{2,1,0:T(8,128)(2,1)S(1)} %pad_maximum_fusion.1.refs_10_), channel_id=1, source_target_pairs={{32,0},{34,2},{36,4},{38,6},{40,8},{42,10},{44,12},{46,14},{48,16}... | collective-permute-start | bytes 1572872 | tf_op jit(solution)/shard_map/ppermute | solution.py:34
  62.4 13.7 %collective-permute-start.16 = (bf16[4,256,256]{2,1,0:T(8,128)(2,1)S(1)}, bf16[4,256,256]{2,1,0:T(8,128)(2,1)S(1)}, u32[]{:S(2)}, u32[]{:S(2)}) collective-permute-start(bf16[4,256,256]{2,1,0:T(8,128)(2,1)S(1)} %get-tuple-element.76), channel_id=1, source_target_pairs={{12,0},{14,2},{0,4},{2,6},{4,8},{6,10},{8,12},{10,14},{28,16},{30,... | collective-permute-start | bytes 1572872 | tf_op jit(solution)/shard_map/ppermute | solution.py:34
  65.4 10.8 %collective-permute-start.17 = (bf16[4,256,256]{2,1,0:T(8,128)(2,1)S(1)}, bf16[4,256,256]{2,1,0:T(8,128)(2,1)S(1)}, u32[]{:S(2)}, u32[]{:S(2)}) collective-permute-start(bf16[4,256,256]{2,1,0:T(8,128)(2,1)S(1)} %get-tuple-element.77), channel_id=1, source_target_pairs={{4,0},{6,2},{8,4},{10,6},{12,8},{14,10},{0,12},{2,14},{20,16},{22,... | collective-permute-start | bytes 1572872 | tf_op jit(solution)/shard_map/ppermute | solution.py:34
  65.7 13.1 %collective-permute-start.18 = (bf16[4,256,256]{2,1,0:T(8,128)(2,1)S(1)}, bf16[4,256,256]{2,1,0:T(8,128)(2,1)S(1)}, u32[]{:S(2)}, u32[]{:S(2)}) collective-permute-start(bf16[4,256,256]{2,1,0:T(8,128)(2,1)S(1)} %get-tuple-element.78), channel_id=1, source_target_pairs={{48,0},{50,2},{52,4},{54,6},{56,8},{58,10},{60,12},{62,14},{0,16},... | collective-permute-start | bytes 1572872 | tf_op jit(solution)/shard_map/ppermute | solution.py:34
  67.1 11.7 %collective-permute-start.19 = (bf16[4,256,256]{2,1,0:T(8,128)(2,1)S(1)}, bf16[4,256,256]{2,1,0:T(8,128)(2,1)S(1)}, u32[]{:S(2)}, u32[]{:S(2)}) collective-permute-start(bf16[4,256,256]{2,1,0:T(8,128)(2,1)S(1)} %get-tuple-element.79), channel_id=1, source_target_pairs={{16,0},{18,2},{20,4},{22,6},{24,8},{26,10},{28,12},{30,14},{32,16}... | collective-permute-start | bytes 1572872 | tf_op jit(solution)/shard_map/ppermute | solution.py:34
  75.3 30.8 %copy-start.2 = (f32[256,256]{1,0:T(8,128)S(1)}, f32[256,256]{1,0:T(8,128)}, u32[]{:S(2)}) copy-start(f32[256,256]{1,0:T(8,128)} %param.10) | copy-start | bytes 786436
  75.3 30.9 %copy-start.3 = (f32[256,256]{1,0:T(8,128)S(1)}, f32[256,256]{1,0:T(8,128)}, u32[]{:S(2)}) copy-start(f32[256,256]{1,0:T(8,128)} %param.12) | copy-start | bytes 786436
  75.3 37.5 %copy-start.1 = (f32[1024,256]{1,0:T(8,128)S(1)}, f32[1024,256]{1,0:T(8,128)}, u32[]{:S(2)}) copy-start(f32[1024,256]{1,0:T(8,128)} %param.9) | copy-start | bytes 3145732
  75.4 5.0 %collective-permute-start.15 = (bf16[8,128,256]{2,1,0:T(8,128)(2,1)S(1)}, bf16[8,128,256]{2,1,0:T(8,128)(2,1)S(1)}, u32[]{:S(2)}, u32[]{:S(2)}) collective-permute-start(bf16[8,128,256]{2,1,0:T(8,128)(2,1)S(1)} %slice.92), channel_id=1, source_target_pairs={{2,0},{0,2},{6,4},{4,6},{10,8},{8,10},{14,12},{12,14},{18,16},{16,... | collective-permute-start | bytes 1572872 | tf_op jit(solution)/shard_map/ppermute | solution.py:34
  78.8 12.5 %collective-permute-start.20 = (bf16[4,256,256]{2,1,0:T(8,128)(2,1)S(1)}, bf16[4,256,256]{2,1,0:T(8,128)(2,1)S(1)}, u32[]{:S(2)}, u32[]{:S(2)}) collective-permute-start(bf16[4,256,256]{2,1,0:T(8,128)(2,1)S(1)} %get-tuple-element.82), channel_id=1, source_target_pairs={{8,0},{10,2},{12,4},{14,6},{0,8},{2,10},{4,12},{6,14},{24,16},{26,... | collective-permute-start | bytes 1572872 | tf_op jit(solution)/shard_map/ppermute | solution.py:34
  79.3 13.7 %collective-permute-start.21 = (bf16[4,256,256]{2,1,0:T(8,128)(2,1)S(1)}, bf16[4,256,256]{2,1,0:T(8,128)(2,1)S(1)}, u32[]{:S(2)}, u32[]{:S(2)}) collective-permute-start(bf16[4,256,256]{2,1,0:T(8,128)(2,1)S(1)} %get-tuple-element.83), channel_id=1, source_target_pairs={{32,0},{34,2},{36,4},{38,6},{40,8},{42,10},{44,12},{46,14},{48,16}... | collective-permute-start | bytes 1572872 | tf_op jit(solution)/shard_map/ppermute | solution.py:34
  95.0 15.7 %all-to-all-start.1 = ((bf16[4,256,256]{2,1,0:T(8,128)(2,1)}), bf16[4,256,256]{2,1,0:T(8,128)(2,1)S(1)}, u32[]{:S(2)}, u32[]{:S(2)}) async-start(bf16[4,256,256]{2,1,0:T(8,128)(2,1)} %add_convert_fusion), calls=%async_computation.1 | async-start | bytes 1048576 | tf_op jit(solution)/shard_map/all_to_all | solution.py:44
  98.5 14.1 %collective-permute-start.25 = (bf16[8,128,256]{2,1,0:T(8,128)(2,1)S(1)}, bf16[8,128,256]{2,1,0:T(8,128)(2,1)S(1)}, u32[]{:S(2)}, u32[]{:S(2)}) collective-permute-start(bf16[8,128,256]{2,1,0:T(8,128)(2,1)S(1)} %add_convert_fusion.1), channel_id=1, source_target_pairs={{0,1},{1,0},{2,3},{3,2},{4,5},{5,4},{6,7},{7,6},{8,9},{9,8},{10,11... | collective-permute-start | bytes 1572872 | tf_op jit(solution)/shard_map/ppermute | solution.py:313
  100.3 6.5 %collective-permute-start.22 = (bf16[256,256]{1,0:T(8,128)(2,1)}, bf16[256,256]{1,0:T(8,128)(2,1)}, u32[]{:S(2)}, u32[]{:S(2)}) collective-permute-start(bf16[256,256]{1,0:T(8,128)(2,1)} %get-tuple-element.94), channel_id=1, source_target_pairs={{12,0},{14,2},{0,4},{2,6},{4,8},{6,10},{8,12},{10,14},{28,16},{30,... | collective-permute-start | bytes 393224 | tf_op jit(solution)/shard_map/ppermute | solution.py:34
  101.0 8.0 %collective-permute-start.23 = (bf16[256,256]{1,0:T(8,128)(2,1)}, bf16[256,256]{1,0:T(8,128)(2,1)}, u32[]{:S(2)}, u32[]{:S(2)}) collective-permute-start(bf16[256,256]{1,0:T(8,128)(2,1)} %get-tuple-element.95), channel_id=1, source_target_pairs={{8,0},{10,2},{12,4},{14,6},{0,8},{2,10},{4,12},{6,14},{24,16},{26,... | collective-permute-start | bytes 393224 | tf_op jit(solution)/shard_map/ppermute | solution.py:34
  104.3 5.3 %collective-permute-start.24 = (bf16[256,256]{1,0:T(8,128)(2,1)}, bf16[256,256]{1,0:T(8,128)(2,1)}, u32[]{:S(2)}, u32[]{:S(2)}) collective-permute-start(bf16[256,256]{1,0:T(8,128)(2,1)} %get-tuple-element.96), channel_id=1, source_target_pairs={{4,0},{6,2},{8,4},{10,6},{12,8},{14,10},{0,12},{2,14},{20,16},{22,... | collective-permute-start | bytes 393224 | tf_op jit(solution)/shard_map/ppermute | solution.py:34
  112.6 5.0 %collective-permute-start.26 = (bf16[256,256]{1,0:T(8,128)(2,1)S(1)}, bf16[256,256]{1,0:T(8,128)(2,1)S(1)}, u32[]{:S(2)}, u32[]{:S(2)}) collective-permute-start(bf16[256,256]{1,0:T(8,128)(2,1)S(1)} %add_convert_fusion.2), channel_id=1, source_target_pairs={{64,0},{66,2},{68,4},{70,6},{72,8},{74,10},{76,12},{78,14},{80,16}... | collective-permute-start | bytes 393224 | tf_op jit(solution)/shard_map/ppermute | solution.py:34

commit v4 on v3

--- a/solution.py
+++ b/solution.py
@@ -53,20 +53,26 @@
 def owner_at(here, part, step, lane):
     x, y, z, _ = here
     if part == 0:
-        return (x * YS + lane) * ZS + (z + step) % ZS
+        return (x * YS + (y + lane) % YS) * ZS + (z + step) % ZS
     return ((1 - x) * YS + (y + step) % YS) * ZS + (z + lane) % ZS
 
 
-def tile_kernel(pieces, outs, *refs):
+def tile_kernel(pieces, outs, last, *refs):
     size = len(pieces)
     device_ref, near_ref, far_ref, near_live, far_live, own_ratings, own_masks = refs[:7]
     far_ratings, far_masks = refs[7:9]
     item_rows = refs[9 : 9 + size]
     user_rows, user_cols, user_before = refs[9 + size : 12 + size]
     item_out = refs[12 + size : 12 + size + len(outs)]
-    user_grad = refs[12 + size + len(outs)]
+    after = 12 + size + len(outs)
+    if last:
+        user_near, user_far = refs[after : after + 2]
+        user_grad = refs[-1]
+    else:
+        user_grad = refs[after]
+    after += 1 + last
     owners_ref, rows_ref, grads_ref, ratings, masks, tile_sems, row_sems, out_sems = refs[
-        13 + size + len(outs) :
+        after : after + 8
     ]
     here = place(device_ref[0])
     core = here[3]
@@ -89,10 +95,14 @@
 
     row_copies, at = [], 0
     for a, (part, step, first, lanes) in enumerate(pieces):
-        row_copies.append(
-            pltpu.make_async_copy(item_rows[a], rows_ref.at[pl.ds(at, lanes)], row_sems.at[a])
-        )
-        row_copies[-1].start()
+        for lane in range(lanes):
+            source = (here[1] + lane) % YS if part == 0 else lane
+            row_copies.append(
+                pltpu.make_async_copy(
+                    item_rows[a].at[source], rows_ref.at[at + lane], row_sems.at[at + lane]
+                )
+            )
+            row_copies[-1].start()
         for lane in range(lanes):
             owners_ref[at + lane] = owner_at(here, part, step, first + lane)
             for copy in tile_copies(at + lane):
@@ -105,7 +115,7 @@
     if user_before is None:
         user_grad[...] = jnp.zeros_like(user_grad)
     else:
-        row_copies.append(pltpu.make_async_copy(user_before, user_grad, row_sems.at[size]))
+        row_copies.append(pltpu.make_async_copy(user_before, user_grad, row_sems.at[total]))
         row_copies[-1].start()
     for copy in row_copies:
         copy.wait()
@@ -176,11 +186,14 @@
         return carry
 
     lax.fori_loop(0, total // PAIR, some, 0)
+    if last:
+        user_near[...] = user_grad[pl.ds(0, blocks)]
+        user_far[...] = user_grad[pl.ds(blocks, blocks)].astype(user_far.dtype)
     for copy in out_copies:
         copy.wait()
 
 
-def tile_terms(pieces, outs, device, indices, own_tiles, far_tiles, item_rows, user_rows, user_cols, user_before):
+def tile_terms(pieces, outs, device, indices, own_tiles, far_tiles, item_rows, user_rows, user_cols, user_before, last):
     _, rows, columns = item_rows[0].shape
     blocks = user_rows.shape[0]
     total = sum(piece[3] for piece in pieces)
@@ -190,18 +203,22 @@
     anywhere = pl.BlockSpec(memory_space=pl.ANY)
 
     first = user_before is None
+    users = [jax.ShapeDtypeStruct((blocks, TILE, columns), jnp.float32)]
+    if last:
+        half = (blocks // 2, TILE, columns)
+        users = [jax.ShapeDtypeStruct(half, jnp.float32), jax.ShapeDtypeStruct(half, jnp.bfloat16)]
 
     def kernel(*refs):
         cut = 11 + len(pieces)
-        tile_kernel(pieces, outs, *refs[:cut], *((None,) if first else ()), *refs[cut:])
+        tile_kernel(pieces, outs, last, *refs[:cut], *((None,) if first else ()), *refs[cut:])
 
     result = pl.pallas_call(
         kernel,
         out_shape=[jax.ShapeDtypeStruct((RING, columns, rows), jnp.bfloat16)] * len(outs)
-        + [jax.ShapeDtypeStruct((blocks, TILE, columns), jnp.float32)],
+        + users,
         in_specs=[smem] * 5 + [hbm] * 4 + [anywhere] * len(pieces) + [vmem] * 2
         + [anywhere] * (not first),
-        out_specs=[anywhere] * len(outs) + [vmem],
+        out_specs=[anywhere] * len(outs) + [vmem] * len(users),
         scratch_shapes=[
             pltpu.SMEM((total,), jnp.int32),
             pltpu.VMEM((total, rows, columns), jnp.bfloat16),
@@ -209,15 +226,16 @@
             pltpu.VMEM((total, 2 * SLOTS, TILE, TILE), jnp.bfloat16),
             pltpu.VMEM((total, 2 * SLOTS, TILE, TILE), jnp.bfloat16),
             pltpu.SemaphoreType.DMA((total, 4)),
-            pltpu.SemaphoreType.DMA((len(pieces) + 1,)),
+            pltpu.SemaphoreType.DMA((total + 1,)),
             pltpu.SemaphoreType.DMA((len(outs),)),
-        ],
-        compiler_params=pltpu.CompilerParams(vmem_limit_bytes=32 << 20),
+        ]
+        + [pltpu.VMEM((blocks, TILE, columns), jnp.float32)] * last,
+        compiler_params=pltpu.CompilerParams(vmem_limit_bytes=(total + 12) << 20),
         cost_estimate=pl.CostEstimate(
             flops=total * (3 << 28), bytes_accessed=total << 20, transcendentals=0
         ),
     )(device, *indices, *own_tiles, *far_tiles, *item_rows, user_rows, user_cols, *(() if first else (user_before,)))
-    return result[: len(outs)], result[len(outs)]
+    return result[: len(outs)], result[len(outs) :]
 
 
 def in_hbm(array):
@@ -270,7 +288,7 @@
     ahead = [fetch(rows[0], z=1), fetch(rows[1], y=1)]
     behind = [fetch(rows[0], z=-1), fetch(rows[1], y=-1)]
 
-    def terms(pieces, outs, item_rows, user_before):
+    def terms(pieces, outs, item_rows, user_before, last=False):
         return tile_terms(
             pieces,
             outs,
@@ -282,47 +300,49 @@
             user_rows,
             user_cols,
             user_before,
+            last,
         )
 
-    here_terms, user_first = terms(
+    here_terms, (user_first,) = terms(
         ((0, 0, 0, RING), (1, 0, 0, RING)), ((0, 0), (1, 0)), rows, None
     )
     rows, ahead, behind, here_terms, user_first = lax.optimization_barrier(
         (rows, ahead, behind, here_terms, user_first)
     )
     across = [fetch(rows[0], z=2), fetch(rows[1], y=2)]
-    near_terms, user_second = terms(
+    near_terms, (user_second,) = terms(
         ((0, 1, 0, RING), (1, 1, 0, RING), (0, 3, 0, RING), (1, 3, 0, RING)),
         ((0, 1), (1, 1), (0, 3), (1, 3)),
         [ahead[0], ahead[1], behind[0], behind[1]],
         user_first,
     )
-    across_terms, user_grad = terms(
-        ((0, 2, 0, RING), (1, 2, 0, RING)), ((0, 2), (1, 2)), across, user_second
+    across_terms, (user_near, user_far) = terms(
+        ((0, 2, 0, RING), (1, 2, 0, RING)), ((0, 2), (1, 2)), across, user_second, True
     )
     arrived = [
         [fetch(near_terms[0], z=-1), fetch(near_terms[2], z=1)],
         [fetch(near_terms[1], y=-1), fetch(near_terms[3], y=1)],
     ]
-    arrived, across_terms = lax.optimization_barrier((arrived, across_terms))
-
-    far_grad = fetch(user_grad[blocks:].astype(low), core=1)
-    half = (user_grad[:blocks] + far_grad.astype(jnp.float32)).astype(low)
-    own_last, far_last = fetch(across_terms[0], z=2), fetch(across_terms[1], y=2)
-    half, own_last, far_last = lax.optimization_barrier((half, own_last, far_last))
+    far_grad = fetch(user_far, core=1)
+    arrived, across_terms, far_grad = lax.optimization_barrier((arrived, across_terms, far_grad))
+    half = (user_near + far_grad.astype(jnp.float32)).astype(low)
+    arrived[0].append(fetch(across_terms[0], z=2))
+    arrived[1].append(fetch(across_terms[1], y=2))
     other = lax.ppermute(half, "rep", [(0, 1), (1, 0)])
-    user_sum = added(half, other)
-    own_sum = added(here_terms[0], *arrived[0], own_last).astype(low)
-    far_sum = [
-        added(here_terms[1][k], *[a[k] for a in arrived[1]], far_last[k]).astype(low)
-        for k in range(RING)
-    ]
-    own_sum, far_sum = lax.optimization_barrier((own_sum, far_sum))
+
+    def lines(part):
+        return [
+            added(here_terms[part][k], *[a[k] for a in arrived[part]]).astype(low)
+            for k in range(RING)
+        ]
+
+    far_sum, own_sum = lines(1), lines(0)
     cross_sum = added(far_sum[0], *[fetch(far_sum[d], z=-d) for d in range(1, RING)]).astype(low)
-    cross_sum, other = lax.optimization_barrier((cross_sum, other))
+    own_sum, other = lax.optimization_barrier((own_sum, other))
     user_sum = added(half, other)
     item_sum = added(
-        jnp.sum(exchange_along_y(own_sum).astype(jnp.float32), 0),
+        own_sum[0],
+        *[fetch(own_sum[d], y=-d) for d in range(1, RING)],
         fetch(cross_sum, x=1),
     ).T
     new_users = adagrad(user_factors, user_accum, user_sum.reshape(user_factors.shape), num_slabs)

time: 118 us -> 116 us (0.983); the launches traced: 119 us -> 114 us
  waiting for transfers between devices: 39.7 us -> 29.2 us
  local copies, waits for them, and re-layouts: 2.81 us -> 5.33 us
  starting transfers between devices: 40.4 us -> 42.2 us
    ppermute x26 -> x29, waiting for transfers between devices: 33.7 us -> 24.9 us  [fetch(): return lax.ppermute(block, 'blk', route)]
    ppermute x26 -> x29, starting transfers between devices: 30.6 us -> 35.4 us  [fetch(): return lax.ppermute(block, 'blk', route)]
    all_to_all x2 -> x1, starting transfers between devices: 7.93 us -> 4.46 us  [exchange_along_y(): lax.all_to_all(blocks, 'blk', 0, 0, axis_index_groups=lines, tiled=True)]
    unnamed x11 -> x27, local copies, waits for them, and re-layouts: 1.12 us -> 3.71 us
    add x1 -> x2, other arithmetic: 0.96 us -> 3.21 us  [added(): return sum((term.astype(jnp.float32) for term in terms))]
    ppermute x1, waiting for transfers between devices: 1.8 us -> 0.01 us  [body(): other = lax.ppermute(half, 'rep', [(0, 1), (1, 0)])]
    sub x2, other arithmetic: 2.64 us -> 1.42 us  [adagrad(): return param - learn_rate * step_grad / jnp.sqrt(total)]
    all_to_all x2 -> x1, waiting for transfers between devices: 4.25 us -> 4.25 us  [exchange_along_y(): lax.all_to_all(blocks, 'blk', 0, 0, axis_index_groups=lines, tiled=True)]
  transfers between devices with their start and end apart: 29 -> 31, of which waited for: 16 -> 13; matrix products, arithmetic and copies ran while one was open for 6% -> 10% of each run, Pallas kernels for 21% -> 23%
where the time goes in v4:
time: 116 us; the launch traced here: 114 us
  starting transfers between devices  42.2 us (36%)
  waiting for transfers between devices  29.2 us (25%)
  Pallas kernels  26.6 us (23%)
  other arithmetic  10.2 us (9%)
  local copies, waits for them, and re-layouts  5.33 us (5%)
    ppermute x29, starting transfers between devices, fetch(): return lax.ppermute(block, 'blk', route)  35.4 us
    pallas_call x3, Pallas kernels, tile_terms(): pl.pallas_call(kernel, out_shape=[jax.ShapeDtypeStruct((RING, columns, ro...  26.6 us
    ppermute x29, waiting for transfers between devices, fetch(): return lax.ppermute(block, 'blk', route)  24.9 us
    all_to_all x1, starting transfers between devices, exchange_along_y(): lax.all_to_all(blocks, 'blk', 0, 0, axis_index_groups=lines, tiled=True)  4.46 us
    all_to_all x1, waiting for transfers between devices, exchange_along_y(): lax.all_to_all(blocks, 'blk', 0, 0, axis_index_groups=lines, tiled=True)  4.25 us
    unnamed x27, local copies, waits for them, and re-layouts  3.71 us
    add x2, other arithmetic, added(): return sum((term.astype(jnp.float32) for term in terms))  3.21 us
  transfers between devices with their start and end apart: 31, of which 13 were waited for; matrix products, arithmetic and copies ran while one was open for 10% of the time, Pallas kernels for 23%

profile of v4, /device:TPU:2, one launch (start us, length us, event | category | flops | bytes accessed | tf_op | source)
XLA Modules:
  0.0 114.3 jit_solution(16332373434736602591)
XLA Ops:
  0.6 1.3 %convert_element_type.185 = bf16[1024,256]{1,0:T(8,128)(2,1)S(1)} convert(f32[1024,256]{1,0:T(8,128)} %param.9) | non-fusion elementwise | flops 262144 | bytes 1572864 | tf_op jit(solution)/shard_map/convert_element_type | solution.py:268
  2.3 1.0 convert_element_type.184
  3.3 0.5 collective-permute-start
  3.8 0.7 fusion.11.refs_1_
  5.1 1.0 collective-permute-done.2.refs_4_
  6.1 3.2 %collective-permute-done = bf16[256,256]{1,0:T(8,128)(2,1)S(1)} collective-permute-done((bf16[256,256]{1,0:T(8,128)(2,1)S(1)}, bf16[256,256]{1,0:T(8,128)(2,1)S(1)}, u32[]{:S(2)}, u32[]{:S(2)}) %collective-permute-start) | collective-permute-done | bytes 131104 | tf_op jit(solution)/shard_map/ppermute | solution.py:34
  9.3 0.5 collective-permute-start.8
  9.8 0.8 broadcast_in_dim.9
  10.6 4.5 %all-to-all-start = ((bf16[4,256,256]{2,1,0:T(8,128)(2,1)}), bf16[4,256,256]{2,1,0:T(8,128)(2,1)S(1)}, u32[]{:S(2)}, u32[]{:S(2)}) async-start(bf16[4,256,256]{2,1,0:T(8,128)(2,1)} %broadcast_in_dim.9), calls=%async_computation | async-start | bytes 1048576 | tf_op jit(solution)/shard_map/all_to_all | solution.py:44
  15.1 4.0 %collective-permute-start.4 = (bf16[256,256]{1,0:T(8,128)(2,1)S(1)}, bf16[256,256]{1,0:T(8,128)(2,1)S(1)}, u32[]{:S(2)}, u32[]{:S(2)}) collective-permute-start(bf16[256,256]{1,0:T(8,128)(2,1)S(1)} %collective-permute-done), channel_id=1, source_target_pairs={{4,0},{6,2},{8,4},{10,6},{12,8},{14,10},{0,12},{2,14},{20,16},{22,... | collective-permute-start | bytes 393224 | tf_op jit(solution)/shard_map/ppermute | solution.py:34
  19.1 1.3 %collective-permute-start.6 = (bf16[256,256]{1,0:T(8,128)(2,1)S(1)}, bf16[256,256]{1,0:T(8,128)(2,1)S(1)}, u32[]{:S(2)}, u32[]{:S(2)}) collective-permute-start(bf16[256,256]{1,0:T(8,128)(2,1)S(1)} %collective-permute-done), channel_id=1, source_target_pairs={{12,0},{14,2},{0,4},{2,6},{4,8},{6,10},{8,12},{10,14},{28,16},{30,... | collective-permute-start | bytes 393224 | tf_op jit(solution)/shard_map/ppermute | solution.py:34
  20.4 4.3 %all-to-all-done.refs_9_ = bf16[4,256,256]{2,1,0:T(8,128)(2,1)S(1)} async-done(((bf16[4,256,256]{2,1,0:T(8,128)(2,1)}), bf16[4,256,256]{2,1,0:T(8,128)(2,1)S(1)}, u32[]{:S(2)}, u32[]{:S(2)}) %all-to-all-start) | async-done | bytes 524320 | tf_op jit(solution)/shard_map/all_to_all | solution.py:44
  24.7 2.2 %collective-permute-done.5 = bf16[256,256]{1,0:T(8,128)(2,1)S(1)} collective-permute-done((bf16[256,256]{1,0:T(8,128)(2,1)S(1)}, bf16[256,256]{1,0:T(8,128)(2,1)S(1)}, u32[]{:S(2)}, u32[]{:S(2)}) %collective-permute-start.5) | collective-permute-done | bytes 131104 | tf_op jit(solution)/shard_map/ppermute | solution.py:34
  26.9 1.1 collective-permute-done.6
  28.0 3.0 %collective-permute-start.10 = (bf16[4,256,256]{2,1,0:T(8,128)(2,1)S(1)}, bf16[4,256,256]{2,1,0:T(8,128)(2,1)}, u32[]{:S(2)}, u32[]{:S(2)}) collective-permute-start(bf16[4,256,256]{2,1,0:T(8,128)(2,1)S(1)} %pad_maximum_fusion.1.refs_10_), channel_id=1, source_target_pairs={{16,0},{18,2},{20,4},{22,6},{24,8},{26,10},{28,12},{30,14},{32,16}... | collective-permute-start | bytes 1572872 | tf_op jit(solution)/shard_map/ppermute | solution.py:34
  31.1 3.2 %collective-permute-start.9 = (bf16[4,256,256]{2,1,0:T(8,128)(2,1)S(1)}, bf16[4,256,256]{2,1,0:T(8,128)(2,1)}, u32[]{:S(2)}, u32[]{:S(2)}) collective-permute-start(bf16[4,256,256]{2,1,0:T(8,128)(2,1)S(1)} %all-to-all-done.refs_9_), channel_id=1, source_target_pairs={{4,0},{6,2},{8,4},{10,6},{12,8},{14,10},{0,12},{2,14},{20,16},{22,... | collective-permute-start | bytes 1572872 | tf_op jit(solution)/shard_map/ppermute | solution.py:34
  34.3 0.5 copy.20.refs_11_.refs_13_
  34.8 6.5 %shard_map.104 = (bf16[4,256,256]{2,1,0:T(8,128)(2,1)S(1)}, bf16[4,256,256]{2,1,0:T(8,128)(2,1)S(1)}, f32[16,128,256]{2,1,0:T(8,128)S(1)}) custom-call(s32[1]{0:T(128)} %bitcast.refs_0_, s32[1,256]{1,0:T(1,128)S(1)} %fusion.11.refs_1_, s32[1,256]{1,0:T(1,128)S(1)} %collective-permute-done.1.refs_2_, s32[1,64]{1,0:T(1,128)S(1)} %copy-done.4, ...), custom_call_target="tpu_custom_call" | custom-call | flops 6442450944 | bytes 8388608 | tf_op jit(solution)/shard_map/pallas_call | solution.py:215
  41.4 0.8 copy-done
  42.2 0.8 copy-done.2
  43.0 2.5 %collective-permute-done.12.refs_12_ = bf16[4,256,256]{2,1,0:T(8,128)(2,1)} collective-permute-done((bf16[4,256,256]{2,1,0:T(8,128)(2,1)S(1)}, bf16[4,256,256]{2,1,0:T(8,128)(2,1)}, u32[]{:S(2)}, u32[]{:S(2)}) %collective-permute-start.12) | collective-permute-done | bytes 524320 | tf_op jit(solution)/shard_map/ppermute | solution.py:34
  45.6 1.6 %collective-permute-start.13 = (bf16[4,256,256]{2,1,0:T(8,128)(2,1)S(1)}, bf16[4,256,256]{2,1,0:T(8,128)(2,1)S(1)}, u32[]{:S(2)}, u32[]{:S(2)}) collective-permute-start(bf16[4,256,256]{2,1,0:T(8,128)(2,1)S(1)} %all-to-all-done.refs_9_), channel_id=1, source_target_pairs={{8,0},{10,2},{12,4},{14,6},{0,8},{2,10},{4,12},{6,14},{24,16},{26,... | collective-permute-start | bytes 1572872 | tf_op jit(solution)/shard_map/ppermute | solution.py:34
  47.2 3.0 %collective-permute-start.14 = (bf16[4,256,256]{2,1,0:T(8,128)(2,1)S(1)}, bf16[4,256,256]{2,1,0:T(8,128)(2,1)S(1)}, u32[]{:S(2)}, u32[]{:S(2)}) collective-permute-start(bf16[4,256,256]{2,1,0:T(8,128)(2,1)S(1)} %pad_maximum_fusion.1.refs_10_), channel_id=1, source_target_pairs={{32,0},{34,2},{36,4},{38,6},{40,8},{42,10},{44,12},{46,14},{48,16}... | collective-permute-start | bytes 1572872 | tf_op jit(solution)/shard_map/ppermute | solution.py:34
  50.3 12.9 %shard_map.105 = (bf16[4,256,256]{2,1,0:T(8,128)(2,1)S(1)}, bf16[4,256,256]{2,1,0:T(8,128)(2,1)S(1)}, bf16[4,256,256]{2,1,0:T(8,128)(2,1)S(1)}, bf16[4,256,256]{2,1,0:T(8,128)(2,1)S(1)}, f32[16,128,256]{2,1,0:T(8,128)S(1)}) custom-call(s32[1]{0:T(128)} %bitcast.refs_0_, s32[1,256]{1,0:T(1,128)S(1)} %fusion.11.refs_1_, ...), custom_call_target="tpu_custom_call" | custom-call | flops 12884901888 | bytes 16777216 | tf_op jit(solution)/shard_map/pallas_call | solution.py:215
  63.2 1.5 %collective-permute-start.15 = (bf16[4,256,256]{2,1,0:T(8,128)(2,1)S(1)}, bf16[4,256,256]{2,1,0:T(8,128)(2,1)S(1)}, u32[]{:S(2)}, u32[]{:S(2)}) collective-permute-start(bf16[4,256,256]{2,1,0:T(8,128)(2,1)S(1)} %get-tuple-element.73), channel_id=1, source_target_pairs={{12,0},{14,2},{0,4},{2,6},{4,8},{6,10},{8,12},{10,14},{28,16},{30,... | collective-permute-start | bytes 1572872 | tf_op jit(solution)/shard_map/ppermute | solution.py:34
  64.7 1.8 %collective-permute-start.16 = (bf16[4,256,256]{2,1,0:T(8,128)(2,1)S(1)}, bf16[4,256,256]{2,1,0:T(8,128)(2,1)S(1)}, u32[]{:S(2)}, u32[]{:S(2)}) collective-permute-start(bf16[4,256,256]{2,1,0:T(8,128)(2,1)S(1)} %get-tuple-element.74), channel_id=1, source_target_pairs={{4,0},{6,2},{8,4},{10,6},{12,8},{14,10},{0,12},{2,14},{20,16},{22,... | collective-permute-start | bytes 1572872 | tf_op jit(solution)/shard_map/ppermute | solution.py:34
  67.0 2.8 %collective-permute-start.18 = (bf16[4,256,256]{2,1,0:T(8,128)(2,1)S(1)}, bf16[4,256,256]{2,1,0:T(8,128)(2,1)S(1)}, u32[]{:S(2)}, u32[]{:S(2)}) collective-permute-start(bf16[4,256,256]{2,1,0:T(8,128)(2,1)S(1)} %get-tuple-element.76), channel_id=1, source_target_pairs={{16,0},{18,2},{20,4},{22,6},{24,8},{26,10},{28,12},{30,14},{32,16}... | collective-permute-start | bytes 1572872 | tf_op jit(solution)/shard_map/ppermute | solution.py:34
  69.7 7.1 %shard_map.106 = (bf16[4,256,256]{2,1,0:T(8,128)(2,1)}, bf16[4,256,256]{2,1,0:T(8,128)(2,1)}, f32[8,128,256]{2,1,0:T(8,128)S(1)}, bf16[8,128,256]{2,1,0:T(8,128)(2,1)S(1)}) custom-call(s32[1]{0:T(128)} %bitcast.refs_0_, s32[1,256]{1,0:T(1,128)S(1)} %fusion.11.refs_1_, s32[1,256]{1,0:T(1,128)S(1)} %collective-permute-done.1.refs_2_, s32[1,64]{1,0:T(1,128)S(1)} %copy-done.4, ...), custom_call_target="tpu_custom_call" | custom-call | flops 6442450944 | bytes 8388608 | tf_op jit(solution)/shard_map/pallas_call | solution.py:215
  77.0 0.8 collective-permute-done.15
  78.1 2.4 %collective-permute-done.17 = bf16[4,256,256]{2,1,0:T(8,128)(2,1)S(1)} collective-permute-done((bf16[4,256,256]{2,1,0:T(8,128)(2,1)S(1)}, bf16[4,256,256]{2,1,0:T(8,128)(2,1)S(1)}, u32[]{:S(2)}, u32[]{:S(2)}) %collective-permute-start.17) | collective-permute-done | bytes 524320 | tf_op jit(solution)/shard_map/ppermute | solution.py:34
  80.5 1.5 %collective-permute-start.25 = (bf16[4,256,256]{2,1,0:T(8,128)(2,1)}, bf16[4,256,256]{2,1,0:T(8,128)(2,1)}, u32[]{:S(2)}, u32[]{:S(2)}) collective-permute-start(bf16[4,256,256]{2,1,0:T(8,128)(2,1)} %get-tuple-element.93), channel_id=1, source_target_pairs={{32,0},{34,2},{36,4},{38,6},{40,8},{42,10},{44,12},{46,14},{48,16}... | collective-permute-start | bytes 1572872 | tf_op jit(solution)/shard_map/ppermute | solution.py:34
  81.9 1.0 collective-permute-start.20
  83.1 2.3 %collective-permute-start.21 = (bf16[8,128,256]{2,1,0:T(8,128)(2,1)S(1)}, bf16[8,128,256]{2,1,0:T(8,128)(2,1)}, u32[]{:S(2)}, u32[]{:S(2)}) collective-permute-start(bf16[8,128,256]{2,1,0:T(8,128)(2,1)S(1)} %add_convert_fusion), channel_id=1, source_target_pairs={{0,1},{1,0},{2,3},{3,2},{4,5},{5,4},{6,7},{7,6},{8,9},{9,8},{10,11... | collective-permute-start | bytes 1572872 | tf_op jit(solution)/shard_map/ppermute | solution.py:331
  85.5 1.1 copy.24
  86.6 8.1 %collective-permute-done.25 = bf16[4,256,256]{2,1,0:T(8,128)(2,1)} collective-permute-done((bf16[4,256,256]{2,1,0:T(8,128)(2,1)}, bf16[4,256,256]{2,1,0:T(8,128)(2,1)}, u32[]{:S(2)}, u32[]{:S(2)}) %collective-permute-start.25) | collective-permute-done | bytes 524320 | tf_op jit(solution)/shard_map/ppermute | solution.py:34
  94.7 1.5 %fusion.8 = (bf16[256,256]{1,0:T(8,128)(2,1)S(1)}, bf16[256,256]{1,0:T(8,128)(2,1)S(1)}, bf16[256,256]{1,0:T(8,128)(2,1)S(1)}) fusion(bf16[4,256,256]{2,1,0:T(8,128)(2,1)} %collective-permute-done.25, bf16[4,256,256]{2,1,0:T(8,128)(2,1)} %copy-done.11, bf16[4,256,256]{2,1,0:T(8,128)(2,1)} %copy-done.10, bf16[4,256,256]{2,1,0:T(8,128)(2,1)S(1)} %copy-done.3), kind=kLoop, calls=%fused_computation.25 | loop fusion | flops 1572864 | bytes 1966080 | tf_op jit(solution)/shard_map/add | solution.py:246
  96.2 0.6 collective-permute-start.26
  96.8 1.0 collective-permute-start.27
  97.8 2.2 %collective-permute-start.28 = (bf16[256,256]{1,0:T(8,128)(2,1)S(1)}, bf16[256,256]{1,0:T(8,128)(2,1)S(1)}, u32[]{:S(2)}, u32[]{:S(2)}) collective-permute-start(bf16[256,256]{1,0:T(8,128)(2,1)S(1)} %get-tuple-element.99), channel_id=1, source_target_pairs={{4,0},{6,2},{8,4},{10,6},{12,8},{14,10},{0,12},{2,14},{20,16},{22,... | collective-permute-start | bytes 393224 | tf_op jit(solution)/shard_map/ppermute | solution.py:34
  100.0 1.7 %fusion.6 = (bf16[256,256]{1,0:T(8,128)(2,1)S(1)}, bf16[256,256]{1,0:T(8,128)(2,1)S(1)}, bf16[256,256]{1,0:T(8,128)(2,1)S(1)}, bf16[256,256]{1,0:T(8,128)(2,1)S(1)}) fusion(bf16[4,256,256]{2,1,0:T(8,128)(2,1)} %collective-permute-done.20, bf16[4,256,256]{2,1,0:T(8,128)(2,1)} %copy-done.9, bf16[4,256,256]{2,1,0:T(8,128)(2,1)} %copy-done.8, ...), kind=kLoop, calls=%fused_computation.23 | loop fusion | flops 2097152 | bytes 2621440 | tf_op jit(solution)/shard_map/add | solution.py:246
  101.7 0.7 collective-permute-start.22
  102.4 3.4 %collective-permute-start.23 = (bf16[256,256]{1,0:T(8,128)(2,1)S(1)}, bf16[256,256]{1,0:T(8,128)(2,1)S(1)}, u32[]{:S(2)}, u32[]{:S(2)}) collective-permute-start(bf16[256,256]{1,0:T(8,128)(2,1)S(1)} %get-tuple-element.88), channel_id=1, source_target_pairs={{32,0},{34,2},{36,4},{38,6},{40,8},{42,10},{44,12},{46,14},{48,16}... | collective-permute-start | bytes 393224 | tf_op jit(solution)/shard_map/ppermute | solution.py:34
  105.8 1.2 %add_multiply_fusion = f32[8,128,256]{2,1,0:T(8,128)S(1)} fusion(bf16[8,128,256]{2,1,0:T(8,128)(2,1)} %collective-permute-done.21, bf16[8,128,256]{2,1,0:T(8,128)(2,1)S(1)} %add_convert_fusion), kind=kLoop, calls=%fused_computation.3 | loop fusion | flops 1048576 | bytes 2097152 | tf_op jit(solution)/shard_map/div | solution.py:48
  107.1 1.2 %fusion.2 = bf16[256,256]{1,0:T(8,128)(2,1)S(1)} fusion(bf16[256,256]{1,0:T(8,128)(2,1)S(1)} %collective-permute-done.28, bf16[256,256]{1,0:T(8,128)(2,1)S(1)} %collective-permute-done.27, bf16[256,256]{1,0:T(8,128)(2,1)S(1)} %collective-permute-done.26, bf16[4,256,256]{2,1,0:T(8,128)(2,1)} %collective-permute-done.25, bf16[4,256,256]{2,1,0:T(8,128)(2,1)} %copy-done.11, ...), kind=kLoop, calls=%fused_computation.9 | loop fusion | flops 1048576 | bytes 1048576 | tf_op jit(solution)/shard_map/convert_element_type | solution.py:340
  108.7 1.2 %multiply_subtract_fusion = f32[1024,256]{1,0:T(8,128)} fusion(f32[1024,256]{1,0:T(8,128)S(1)} %copy-done.5, f32[1024,256]{1,0:T(8,128)S(1)} %copy-done.7, f32[8,128,256]{2,1,0:T(8,128)S(1)} %add_multiply_fusion), kind=kLoop, calls=%fused_computation.2 | loop fusion | flops 1835008 | bytes 4194304 | tf_op jit(solution)/shard_map/sub | solution.py:50
  110.2 1.9 %collective-permute-done.24 = bf16[256,256]{1,0:T(8,128)(2,1)S(1)} collective-permute-done((bf16[256,256]{1,0:T(8,128)(2,1)S(1)}, bf16[256,256]{1,0:T(8,128)(2,1)S(1)}, u32[]{:S(2)}, u32[]{:S(2)}) %collective-permute-start.24) | collective-permute-done | bytes 131104 | tf_op jit(solution)/shard_map/ppermute | solution.py:34
  112.1 1.3 %collective-permute-done.29 = bf16[256,256]{1,0:T(8,128)(2,1)S(1)} collective-permute-done((bf16[256,256]{1,0:T(8,128)(2,1)S(1)}, bf16[256,256]{1,0:T(8,128)(2,1)S(1)}, u32[]{:S(2)}, u32[]{:S(2)}) %collective-permute-start.29) | collective-permute-done | bytes 131104 | tf_op jit(solution)/shard_map/ppermute | solution.py:34
  113.5 0.8 copy.26
  (59 shorter events, 3.2 us)
Async XLA Ops:
  0.6 34.2 %copy-start.4 = (s32[1,64]{1,0:T(1,128)S(1)}, s32[1,64]{1,0:T(1,128)}, u32[]{:S(2)}) copy-start(s32[1,64]{1,0:T(1,128)} %refs_3_.5) | copy-start | bytes 772
  2.2 7.0 %collective-permute-start.3 = (bf16[8,128,256]{1,2,0:T(8,128)(2,1)S(1)}, bf16[8,128,256]{1,2,0:T(8,128)(2,1)S(1)}, u32[]{:S(2)}, u32[]{:S(2)}) collective-permute-start(bf16[8,128,256]{1,2,0:T(8,128)(2,1)S(1)} %copy.18), channel_id=1, source_target_pairs={{2,0},{0,2},{6,4},{4,6},{10,8},{8,10},{14,12},{12,14},{18,16},{16,... | collective-permute-start | bytes 1572872 | tf_op jit(solution)/shard_map/ppermute | solution.py:34
  3.3 6.0 %collective-permute-start = (bf16[256,256]{1,0:T(8,128)(2,1)S(1)}, bf16[256,256]{1,0:T(8,128)(2,1)S(1)}, u32[]{:S(2)}, u32[]{:S(2)}) collective-permute-start(bf16[256,256]{1,0:T(8,128)(2,1)S(1)} %convert_element_type.184), channel_id=1, source_target_pairs={{64,0},{66,2},{68,4},{70,6},{72,8},{74,10},{76,12},{78,14},{80,16}... | collective-permute-start | bytes 393224 | tf_op jit(solution)/shard_map/ppermute | solution.py:34
  4.5 1.5 %collective-permute-start.1 = (s32[1,256]{1,0:T(1,128)S(1)}, s32[1,256]{1,0:T(1,128)S(1)}, u32[]{:S(2)}, u32[]{:S(2)}) collective-permute-start(s32[1,256]{1,0:T(1,128)S(1)} %fusion.11.refs_1_), channel_id=1, source_target_pairs={{2,0},{0,2},{6,4},{4,6},{10,8},{8,10},{14,12},{12,14},{18,16},{16,... | collective-permute-start | bytes 3080 | tf_op jit(solution)/shard_map/ppermute | solution.py:34
  4.8 1.3 %collective-permute-start.2 = (s32[1,64]{1,0:T(1,128)}, s32[1,64]{1,0:T(1,128)S(1)}, u32[]{:S(2)}, u32[]{:S(2)}) collective-permute-start(s32[1,64]{1,0:T(1,128)} %refs_3_.5), channel_id=1, source_target_pairs={{2,0},{0,2},{6,4},{4,6},{10,8},{8,10},{14,12},{12,14},{18,16},{16,... | collective-permute-start | bytes 776 | tf_op jit(solution)/shard_map/ppermute | solution.py:34
  9.2 18.7 %collective-permute-start.7 = (bf16[32,2,4,128,128]{4,3,2,1,0:T(8,128)(2,1)}, bf16[32,2,4,128,128]{4,3,2,1,0:T(8,128)(2,1)}, u32[]{:S(2)}, u32[]{:S(2)}) collective-permute-start(bf16[32,2,4,128,128]{4,3,2,1,0:T(8,128)(2,1)} %bitcast.39), channel_id=1, source_target_pairs={{2,0},{0,2},{6,4},{4,6},{10,8},{8,10},{14,12},{12,14},{18,16},{16,... | collective-permute-start | bytes 25165832 | tf_op jit(solution)/shard_map/ppermute | solution.py:34
  9.3 25.6 %collective-permute-start.8 = (bf16[32,2,4,128,128]{4,3,2,1,0:T(8,128)(2,1)}, bf16[32,2,4,128,128]{4,3,2,1,0:T(8,128)(2,1)}, u32[]{:S(2)}, u32[]{:S(2)}) collective-permute-start(bf16[32,2,4,128,128]{4,3,2,1,0:T(8,128)(2,1)} %bitcast.43), channel_id=1, source_target_pairs={{2,0},{0,2},{6,4},{4,6},{10,8},{8,10},{14,12},{12,14},{18,16},{16,... | collective-permute-start | bytes 25165832 | tf_op jit(solution)/shard_map/ppermute | solution.py:34
  10.6 14.1 %all-to-all-start = ((bf16[4,256,256]{2,1,0:T(8,128)(2,1)}), bf16[4,256,256]{2,1,0:T(8,128)(2,1)S(1)}, u32[]{:S(2)}, u32[]{:S(2)}) async-start(bf16[4,256,256]{2,1,0:T(8,128)(2,1)} %broadcast_in_dim.9), calls=%async_computation | async-start | bytes 1048576 | tf_op jit(solution)/shard_map/all_to_all | solution.py:44
  15.1 9.6 %collective-permute-start.4 = (bf16[256,256]{1,0:T(8,128)(2,1)S(1)}, bf16[256,256]{1,0:T(8,128)(2,1)S(1)}, u32[]{:S(2)}, u32[]{:S(2)}) collective-permute-start(bf16[256,256]{1,0:T(8,128)(2,1)S(1)} %collective-permute-done), channel_id=1, source_target_pairs={{4,0},{6,2},{8,4},{10,6},{12,8},{14,10},{0,12},{2,14},{20,16},{22,... | collective-permute-start | bytes 393224 | tf_op jit(solution)/shard_map/ppermute | solution.py:34
  19.1 7.8 %collective-permute-start.5 = (bf16[256,256]{1,0:T(8,128)(2,1)S(1)}, bf16[256,256]{1,0:T(8,128)(2,1)S(1)}, u32[]{:S(2)}, u32[]{:S(2)}) collective-permute-start(bf16[256,256]{1,0:T(8,128)(2,1)S(1)} %collective-permute-done), channel_id=1, source_target_pairs={{8,0},{10,2},{12,4},{14,6},{0,8},{2,10},{4,12},{6,14},{24,16},{26,... | collective-permute-start | bytes 393224 | tf_op jit(solution)/shard_map/ppermute | solution.py:34
  19.1 8.9 %collective-permute-start.6 = (bf16[256,256]{1,0:T(8,128)(2,1)S(1)}, bf16[256,256]{1,0:T(8,128)(2,1)S(1)}, u32[]{:S(2)}, u32[]{:S(2)}) collective-permute-start(bf16[256,256]{1,0:T(8,128)(2,1)S(1)} %collective-permute-done), channel_id=1, source_target_pairs={{12,0},{14,2},{0,4},{2,6},{4,8},{6,10},{8,12},{10,14},{28,16},{30,... | collective-permute-start | bytes 393224 | tf_op jit(solution)/shard_map/ppermute | solution.py:34
  28.0 15.0 %collective-permute-start.10 = (bf16[4,256,256]{2,1,0:T(8,128)(2,1)S(1)}, bf16[4,256,256]{2,1,0:T(8,128)(2,1)}, u32[]{:S(2)}, u32[]{:S(2)}) collective-permute-start(bf16[4,256,256]{2,1,0:T(8,128)(2,1)S(1)} %pad_maximum_fusion.1.refs_10_), channel_id=1, source_target_pairs={{16,0},{18,2},{20,4},{22,6},{24,8},{26,10},{28,12},{30,14},{32,16}... | collective-permute-start | bytes 1572872 | tf_op jit(solution)/shard_map/ppermute | solution.py:34
  31.1 14.5 %collective-permute-start.12 = (bf16[4,256,256]{2,1,0:T(8,128)(2,1)S(1)}, bf16[4,256,256]{2,1,0:T(8,128)(2,1)}, u32[]{:S(2)}, u32[]{:S(2)}) collective-permute-start(bf16[4,256,256]{2,1,0:T(8,128)(2,1)S(1)} %pad_maximum_fusion.1.refs_10_), channel_id=1, source_target_pairs={{48,0},{50,2},{52,4},{54,6},{56,8},{58,10},{60,12},{62,14},{0,16},... | collective-permute-start | bytes 1572872 | tf_op jit(solution)/shard_map/ppermute | solution.py:34
  31.1 14.5 %collective-permute-start.11 = (bf16[4,256,256]{2,1,0:T(8,128)(2,1)S(1)}, bf16[4,256,256]{2,1,0:T(8,128)(2,1)}, u32[]{:S(2)}, u32[]{:S(2)}) collective-permute-start(bf16[4,256,256]{2,1,0:T(8,128)(2,1)S(1)} %all-to-all-done.refs_9_), channel_id=1, source_target_pairs={{12,0},{14,2},{0,4},{2,6},{4,8},{6,10},{8,12},{10,14},{28,16},{30,... | collective-permute-start | bytes 1572872 | tf_op jit(solution)/shard_map/ppermute | solution.py:34
  31.1 14.5 %collective-permute-start.9 = (bf16[4,256,256]{2,1,0:T(8,128)(2,1)S(1)}, bf16[4,256,256]{2,1,0:T(8,128)(2,1)}, u32[]{:S(2)}, u32[]{:S(2)}) collective-permute-start(bf16[4,256,256]{2,1,0:T(8,128)(2,1)S(1)} %all-to-all-done.refs_9_), channel_id=1, source_target_pairs={{4,0},{6,2},{8,4},{10,6},{12,8},{14,10},{0,12},{2,14},{20,16},{22,... | collective-permute-start | bytes 1572872 | tf_op jit(solution)/shard_map/ppermute | solution.py:34
  41.4 0.8 copy-start
  42.2 0.8 copy-start.2
  45.6 21.4 %collective-permute-start.13 = (bf16[4,256,256]{2,1,0:T(8,128)(2,1)S(1)}, bf16[4,256,256]{2,1,0:T(8,128)(2,1)S(1)}, u32[]{:S(2)}, u32[]{:S(2)}) collective-permute-start(bf16[4,256,256]{2,1,0:T(8,128)(2,1)S(1)} %all-to-all-done.refs_9_), channel_id=1, source_target_pairs={{8,0},{10,2},{12,4},{14,6},{0,8},{2,10},{4,12},{6,14},{24,16},{26,... | collective-permute-start | bytes 1572872 | tf_op jit(solution)/shard_map/ppermute | solution.py:34
  47.2 22.5 %collective-permute-start.14 = (bf16[4,256,256]{2,1,0:T(8,128)(2,1)S(1)}, bf16[4,256,256]{2,1,0:T(8,128)(2,1)S(1)}, u32[]{:S(2)}, u32[]{:S(2)}) collective-permute-start(bf16[4,256,256]{2,1,0:T(8,128)(2,1)S(1)} %pad_maximum_fusion.1.refs_10_), channel_id=1, source_target_pairs={{32,0},{34,2},{36,4},{38,6},{40,8},{42,10},{44,12},{46,14},{48,16}... | collective-permute-start | bytes 1572872 | tf_op jit(solution)/shard_map/ppermute | solution.py:34
  63.2 14.6 %collective-permute-start.15 = (bf16[4,256,256]{2,1,0:T(8,128)(2,1)S(1)}, bf16[4,256,256]{2,1,0:T(8,128)(2,1)S(1)}, u32[]{:S(2)}, u32[]{:S(2)}) collective-permute-start(bf16[4,256,256]{2,1,0:T(8,128)(2,1)S(1)} %get-tuple-element.73), channel_id=1, source_target_pairs={{12,0},{14,2},{0,4},{2,6},{4,8},{6,10},{8,12},{10,14},{28,16},{30,... | collective-permute-start | bytes 1572872 | tf_op jit(solution)/shard_map/ppermute | solution.py:34
  64.7 13.4 %collective-permute-start.16 = (bf16[4,256,256]{2,1,0:T(8,128)(2,1)S(1)}, bf16[4,256,256]{2,1,0:T(8,128)(2,1)S(1)}, u32[]{:S(2)}, u32[]{:S(2)}) collective-permute-start(bf16[4,256,256]{2,1,0:T(8,128)(2,1)S(1)} %get-tuple-element.74), channel_id=1, source_target_pairs={{4,0},{6,2},{8,4},{10,6},{12,8},{14,10},{0,12},{2,14},{20,16},{22,... | collective-permute-start | bytes 1572872 | tf_op jit(solution)/shard_map/ppermute | solution.py:34
  66.5 14.0 %collective-permute-start.17 = (bf16[4,256,256]{2,1,0:T(8,128)(2,1)S(1)}, bf16[4,256,256]{2,1,0:T(8,128)(2,1)S(1)}, u32[]{:S(2)}, u32[]{:S(2)}) collective-permute-start(bf16[4,256,256]{2,1,0:T(8,128)(2,1)S(1)} %get-tuple-element.75), channel_id=1, source_target_pairs={{48,0},{50,2},{52,4},{54,6},{56,8},{58,10},{60,12},{62,14},{0,16},... | collective-permute-start | bytes 1572872 | tf_op jit(solution)/shard_map/ppermute | solution.py:34
  67.0 13.5 %collective-permute-start.18 = (bf16[4,256,256]{2,1,0:T(8,128)(2,1)S(1)}, bf16[4,256,256]{2,1,0:T(8,128)(2,1)S(1)}, u32[]{:S(2)}, u32[]{:S(2)}) collective-permute-start(bf16[4,256,256]{2,1,0:T(8,128)(2,1)S(1)} %get-tuple-element.76), channel_id=1, source_target_pairs={{16,0},{18,2},{20,4},{22,6},{24,8},{26,10},{28,12},{30,14},{32,16}... | collective-permute-start | bytes 1572872 | tf_op jit(solution)/shard_map/ppermute | solution.py:34
  69.7 15.6 %copy-start.6 = (f32[256,256]{1,0:T(8,128)S(1)}, f32[256,256]{1,0:T(8,128)}, u32[]{:S(2)}) copy-start(f32[256,256]{1,0:T(8,128)} %param.10) | copy-start | bytes 786436
  69.7 25.0 %copy-start.3 = (bf16[4,256,256]{2,1,0:T(8,128)(2,1)S(1)}, bf16[4,256,256]{2,1,0:T(8,128)(2,1)}, u32[]{:S(2)}) copy-start(bf16[4,256,256]{2,1,0:T(8,128)(2,1)} %copy-done.2) | copy-start | bytes 1572868
  69.7 30.3 %copy-start.1 = (bf16[4,256,256]{2,1,0:T(8,128)(2,1)S(1)}, bf16[4,256,256]{2,1,0:T(8,128)(2,1)}, u32[]{:S(2)}) copy-start(bf16[4,256,256]{2,1,0:T(8,128)(2,1)} %copy-done) | copy-start | bytes 1572868
  76.9 31.8 %copy-start.5 = (f32[1024,256]{1,0:T(8,128)S(1)}, f32[1024,256]{1,0:T(8,128)}, u32[]{:S(2)}) copy-start(f32[1024,256]{1,0:T(8,128)} %param.9) | copy-start | bytes 3145732
  76.9 3.6 %collective-permute-start.19 = (bf16[8,128,256]{2,1,0:T(8,128)(2,1)S(1)}, bf16[8,128,256]{2,1,0:T(8,128)(2,1)S(1)}, u32[]{:S(2)}, u32[]{:S(2)}) collective-permute-start(bf16[8,128,256]{2,1,0:T(8,128)(2,1)S(1)} %get-tuple-element.79), channel_id=1, source_target_pairs={{2,0},{0,2},{6,4},{4,6},{10,8},{8,10},{14,12},{12,14},{18,16},{16,... | collective-permute-start | bytes 1572872 | tf_op jit(solution)/shard_map/ppermute | solution.py:34
  77.8 5.2 %copy-start.8 = (bf16[4,256,256]{2,1,0:T(8,128)(2,1)}, bf16[4,256,256]{2,1,0:T(8,128)(2,1)S(1)}, u32[]{:S(2)}) copy-start(bf16[4,256,256]{2,1,0:T(8,128)(2,1)S(1)} %collective-permute-done.15) | copy-start | bytes 1572868
  78.1 5.0 %copy-start.9 = (bf16[4,256,256]{2,1,0:T(8,128)(2,1)}, bf16[4,256,256]{2,1,0:T(8,128)(2,1)S(1)}, u32[]{:S(2)}) copy-start(bf16[4,256,256]{2,1,0:T(8,128)(2,1)S(1)} %collective-permute-done.16) | copy-start | bytes 1572868
  80.5 2.6 %copy-start.10 = (bf16[4,256,256]{2,1,0:T(8,128)(2,1)}, bf16[4,256,256]{2,1,0:T(8,128)(2,1)S(1)}, u32[]{:S(2)}) copy-start(bf16[4,256,256]{2,1,0:T(8,128)(2,1)S(1)} %collective-permute-done.17) | copy-start | bytes 1572868
  80.5 2.6 %copy-start.11 = (bf16[4,256,256]{2,1,0:T(8,128)(2,1)}, bf16[4,256,256]{2,1,0:T(8,128)(2,1)S(1)}, u32[]{:S(2)}) copy-start(bf16[4,256,256]{2,1,0:T(8,128)(2,1)S(1)} %collective-permute-done.18) | copy-start | bytes 1572868
  80.5 14.2 %collective-permute-start.25 = (bf16[4,256,256]{2,1,0:T(8,128)(2,1)}, bf16[4,256,256]{2,1,0:T(8,128)(2,1)}, u32[]{:S(2)}, u32[]{:S(2)}) collective-permute-start(bf16[4,256,256]{2,1,0:T(8,128)(2,1)} %get-tuple-element.93), channel_id=1, source_target_pairs={{32,0},{34,2},{36,4},{38,6},{40,8},{42,10},{44,12},{46,14},{48,16}... | collective-permute-start | bytes 1572872 | tf_op jit(solution)/shard_map/ppermute | solution.py:34
  81.9 18.1 %collective-permute-start.20 = (bf16[4,256,256]{2,1,0:T(8,128)(2,1)}, bf16[4,256,256]{2,1,0:T(8,128)(2,1)}, u32[]{:S(2)}, u32[]{:S(2)}) collective-permute-start(bf16[4,256,256]{2,1,0:T(8,128)(2,1)} %get-tuple-element.84), channel_id=1, source_target_pairs={{8,0},{10,2},{12,4},{14,6},{0,8},{2,10},{4,12},{6,14},{24,16},{26,... | collective-permute-start | bytes 1572872 | tf_op jit(solution)/shard_map/ppermute | solution.py:34
  83.1 18.6 %collective-permute-start.21 = (bf16[8,128,256]{2,1,0:T(8,128)(2,1)S(1)}, bf16[8,128,256]{2,1,0:T(8,128)(2,1)}, u32[]{:S(2)}, u32[]{:S(2)}) collective-permute-start(bf16[8,128,256]{2,1,0:T(8,128)(2,1)S(1)} %add_convert_fusion), channel_id=1, source_target_pairs={{0,1},{1,0},{2,3},{3,2},{4,5},{5,4},{6,7},{7,6},{8,9},{9,8},{10,11... | collective-permute-start | bytes 1572872 | tf_op jit(solution)/shard_map/ppermute | solution.py:331
  86.6 22.2 %copy-start.7 = (f32[1024,256]{1,0:T(8,128)S(1)}, f32[1024,256]{1,0:T(8,128)}, u32[]{:S(2)}) copy-start(f32[1024,256]{1,0:T(8,128)} %param.11) | copy-start | bytes 3145732
  96.2 10.8 %collective-permute-start.26 = (bf16[256,256]{1,0:T(8,128)(2,1)S(1)}, bf16[256,256]{1,0:T(8,128)(2,1)S(1)}, u32[]{:S(2)}, u32[]{:S(2)}) collective-permute-start(bf16[256,256]{1,0:T(8,128)(2,1)S(1)} %get-tuple-element.98), channel_id=1, source_target_pairs={{12,0},{14,2},{0,4},{2,6},{4,8},{6,10},{8,12},{10,14},{28,16},{30,... | collective-permute-start | bytes 393224 | tf_op jit(solution)/shard_map/ppermute | solution.py:34
  96.8 10.3 %collective-permute-start.27 = (bf16[256,256]{1,0:T(8,128)(2,1)S(1)}, bf16[256,256]{1,0:T(8,128)(2,1)S(1)}, u32[]{:S(2)}, u32[]{:S(2)}) collective-permute-start(bf16[256,256]{1,0:T(8,128)(2,1)S(1)} %get-tuple-element.100), channel_id=1, source_target_pairs={{8,0},{10,2},{12,4},{14,6},{0,8},{2,10},{4,12},{6,14},{24,16},{26,... | collective-permute-start | bytes 393224 | tf_op jit(solution)/shard_map/ppermute | solution.py:34
  97.8 9.3 %collective-permute-start.28 = (bf16[256,256]{1,0:T(8,128)(2,1)S(1)}, bf16[256,256]{1,0:T(8,128)(2,1)S(1)}, u32[]{:S(2)}, u32[]{:S(2)}) collective-permute-start(bf16[256,256]{1,0:T(8,128)(2,1)S(1)} %get-tuple-element.99), channel_id=1, source_target_pairs={{4,0},{6,2},{8,4},{10,6},{12,8},{14,10},{0,12},{2,14},{20,16},{22,... | collective-permute-start | bytes 393224 | tf_op jit(solution)/shard_map/ppermute | solution.py:34
  101.7 8.3 %collective-permute-start.22 = (bf16[256,256]{1,0:T(8,128)(2,1)S(1)}, bf16[256,256]{1,0:T(8,128)(2,1)S(1)}, u32[]{:S(2)}, u32[]{:S(2)}) collective-permute-start(bf16[256,256]{1,0:T(8,128)(2,1)S(1)} %get-tuple-element.87), channel_id=1, source_target_pairs={{48,0},{50,2},{52,4},{54,6},{56,8},{58,10},{60,12},{62,14},{0,16},... | collective-permute-start | bytes 393224 | tf_op jit(solution)/shard_map/ppermute | solution.py:34
  102.4 7.8 %collective-permute-start.23 = (bf16[256,256]{1,0:T(8,128)(2,1)S(1)}, bf16[256,256]{1,0:T(8,128)(2,1)S(1)}, u32[]{:S(2)}, u32[]{:S(2)}) collective-permute-start(bf16[256,256]{1,0:T(8,128)(2,1)S(1)} %get-tuple-element.88), channel_id=1, source_target_pairs={{32,0},{34,2},{36,4},{38,6},{40,8},{42,10},{44,12},{46,14},{48,16}... | collective-permute-start | bytes 393224 | tf_op jit(solution)/shard_map/ppermute | solution.py:34
  107.0 5.0 %collective-permute-start.24 = (bf16[256,256]{1,0:T(8,128)(2,1)S(1)}, bf16[256,256]{1,0:T(8,128)(2,1)S(1)}, u32[]{:S(2)}, u32[]{:S(2)}) collective-permute-start(bf16[256,256]{1,0:T(8,128)(2,1)S(1)} %get-tuple-element.89), channel_id=1, source_target_pairs={{16,0},{18,2},{20,4},{22,6},{24,8},{26,10},{28,12},{30,14},{32,16}... | collective-permute-start | bytes 393224 | tf_op jit(solution)/shard_map/ppermute | solution.py:34
  108.3 5.0 %collective-permute-start.29 = (bf16[256,256]{1,0:T(8,128)(2,1)S(1)}, bf16[256,256]{1,0:T(8,128)(2,1)S(1)}, u32[]{:S(2)}, u32[]{:S(2)}) collective-permute-start(bf16[256,256]{1,0:T(8,128)(2,1)S(1)} %fusion.2), channel_id=1, source_target_pairs={{64,0},{66,2},{68,4},{70,6},{72,8},{74,10},{76,12},{78,14},{80,16}... | collective-permute-start | bytes 393224 | tf_op jit(solution)/shard_map/ppermute | solution.py:34

commit v5 on v4

--- a/solution.py
+++ b/solution.py
@@ -94,6 +94,9 @@
         ]
 
     row_copies, at = [], 0
+    if user_before is not None:
+        row_copies.append(pltpu.make_async_copy(user_before, user_grad, row_sems.at[total]))
+        row_copies[-1].start()
     for a, (part, step, first, lanes) in enumerate(pieces):
         for lane in range(lanes):
             source = (here[1] + lane) % YS if part == 0 else lane
@@ -114,9 +117,6 @@
     ]
     if user_before is None:
         user_grad[...] = jnp.zeros_like(user_grad)
-    else:
-        row_copies.append(pltpu.make_async_copy(user_before, user_grad, row_sems.at[total]))
-        row_copies[-1].start()
     for copy in row_copies:
         copy.wait()
 
@@ -265,11 +265,12 @@
 
     near = tile_users * 2 + tile_items % 2
     far, far_live = fetch(near, core=1), fetch(tile_counts, core=1)
-    user_low = user_factors.astype(low).reshape(-1, TILE, columns)
+    item_low = item_factors.astype(low)
+    cross = fetch(item_low, x=1)
+    item_low, user_given = lax.optimization_barrier((item_low, user_factors))
+    user_low = user_given.astype(low).reshape(-1, TILE, columns)
     blocks = user_low.shape[0]
     far_rows = fetch(user_low, core=1)
-    item_low = item_factors.astype(low)
-    cross = fetch(item_low, x=1)
     shape = (owners, CORES, SLOTS, TILE, TILE)
     own_tiles = [ratings.reshape(shape), masks.reshape(shape)]
     first, second, cross, far, far_live, far_rows = lax.optimization_barrier(
@@ -280,9 +281,7 @@
 
     own_line = exchange_along_y(jnp.broadcast_to(item_low, (YS,) + item_low.shape))
     far_line = [cross] + [fetch(cross, z=d) for d in range(1, RING)]
-    own_line, far_line, user_rows, far_tiles[0] = lax.optimization_barrier(
-        (own_line, far_line, user_rows, far_tiles[0])
-    )
+    own_line, far_line[1], far_line[2] = lax.optimization_barrier((own_line, far_line[1], far_line[2]))
     user_cols = user_rows.swapaxes(1, 2)
     rows = [own_line, jnp.stack(far_line)]
     ahead = [fetch(rows[0], z=1), fetch(rows[1], y=1)]

time: 116 us -> 114 us (0.983)
  starting transfers between devices: 42.2 us -> 39.8 us
  waiting for transfers between devices: 29.2 us -> 27.2 us
  other arithmetic: 10.2 us -> 12.1 us
  local copies, waits for them, and re-layouts: 5.33 us -> 6.94 us
    all_to_all x1, waiting for transfers between devices: 4.25 us -> 1.75 us  [exchange_along_y(): lax.all_to_all(blocks, 'blk', 0, 0, axis_index_groups=lines, tiled=True)]
    ppermute x29, starting transfers between devices: 35.4 us -> 33.5 us  [fetch(): return lax.ppermute(block, 'blk', route)]
    concatenate x0 -> x1, local copies, waits for them, and re-layouts: none -> 1.48 us  [body(): user_rows = jnp.concatenate([user_low, far_rows], 0)]
    unnamed x27 -> x29, local copies, waits for them, and re-layouts: 3.71 us -> 4.35 us
  transfers between devices with their start and end apart: 31 -> 31, of which waited for: 13 -> 12; matrix products, arithmetic and copies ran while one was open for 10% -> 13% of each run, Pallas kernels for 23% -> 23%
where the time goes in v5:
time: 114 us; the launch traced here: 113 us
  starting transfers between devices  39.8 us (35%)
  waiting for transfers between devices  27.2 us (24%)
  Pallas kernels  26.5 us (23%)
  other arithmetic  12.1 us (11%)
  local copies, waits for them, and re-layouts  6.94 us (6%)
    ppermute x29, starting transfers between devices, fetch(): return lax.ppermute(block, 'blk', route)  33.5 us
    pallas_call x3, Pallas kernels, tile_terms(): pl.pallas_call(kernel, out_shape=[jax.ShapeDtypeStruct((RING, columns, ro...  26.5 us
    ppermute x29, waiting for transfers between devices, fetch(): return lax.ppermute(block, 'blk', route)  25.5 us
    all_to_all x1, starting transfers between devices, exchange_along_y(): lax.all_to_all(blocks, 'blk', 0, 0, axis_index_groups=lines, tiled=True)  4.46 us
    unnamed x29, local copies, waits for them, and re-layouts  4.35 us
    add x2, other arithmetic, added(): return sum((term.astype(jnp.float32) for term in terms))  3.05 us
  transfers between devices with their start and end apart: 31, of which 12 were waited for; matrix products, arithmetic and copies ran while one was open for 13% of the time, Pallas kernels for 23%

profile of v5, /device:TPU:2, one launch (start us, length us, event | category | flops | bytes accessed | tf_op | source)
XLA Modules:
  0.0 113.5 jit_solution(7249889701908596)
XLA Ops:
  0.6 1.0 convert_element_type.184
  1.6 1.3 %convert_element_type.185 = bf16[1024,256]{1,0:T(8,128)(2,1)S(1)} convert(f32[1024,256]{1,0:T(8,128)} %param.9) | non-fusion elementwise | flops 262144 | bytes 1572864 | tf_op jit(solution)/shard_map/convert_element_type | solution.py:271
  3.3 0.5 collective-permute-start
  3.8 0.7 fusion.11.refs_1_
  5.1 1.0 collective-permute-done.2.refs_4_
  6.0 3.1 %collective-permute-done = bf16[256,256]{1,0:T(8,128)(2,1)S(1)} collective-permute-done((bf16[256,256]{1,0:T(8,128)(2,1)S(1)}, bf16[256,256]{1,0:T(8,128)(2,1)S(1)}, u32[]{:S(2)}, u32[]{:S(2)}) %collective-permute-start) | collective-permute-done | bytes 131104 | tf_op jit(solution)/shard_map/ppermute | solution.py:34
  9.7 0.8 broadcast_in_dim.9
  10.5 4.5 %all-to-all-start = ((bf16[4,256,256]{2,1,0:T(8,128)(2,1)}), bf16[4,256,256]{2,1,0:T(8,128)(2,1)S(1)}, u32[]{:S(2)}, u32[]{:S(2)}) async-start(bf16[4,256,256]{2,1,0:T(8,128)(2,1)} %broadcast_in_dim.9), calls=%async_computation | async-start | bytes 1048576 | tf_op jit(solution)/shard_map/all_to_all | solution.py:44
  15.0 4.0 %collective-permute-start.6 = (bf16[256,256]{1,0:T(8,128)(2,1)S(1)}, bf16[256,256]{1,0:T(8,128)(2,1)S(1)}, u32[]{:S(2)}, u32[]{:S(2)}) collective-permute-start(bf16[256,256]{1,0:T(8,128)(2,1)S(1)} %collective-permute-done), channel_id=1, source_target_pairs={{4,0},{6,2},{8,4},{10,6},{12,8},{14,10},{0,12},{2,14},{20,16},{22,... | collective-permute-start | bytes 393224 | tf_op jit(solution)/shard_map/ppermute | solution.py:34
  19.0 1.3 %collective-permute-start.8 = (bf16[256,256]{1,0:T(8,128)(2,1)S(1)}, bf16[256,256]{1,0:T(8,128)(2,1)}, u32[]{:S(2)}, u32[]{:S(2)}) collective-permute-start(bf16[256,256]{1,0:T(8,128)(2,1)S(1)} %collective-permute-done), channel_id=1, source_target_pairs={{12,0},{14,2},{0,4},{2,6},{4,8},{6,10},{8,12},{10,14},{28,16},{30,... | collective-permute-start | bytes 393224 | tf_op jit(solution)/shard_map/ppermute | solution.py:34
  20.3 1.1 fusion.13
  21.4 1.5 %copy.20.refs_11_.refs_13_ = bf16[16,128,256]{2,1,0:T(8,128)(2,1)S(1)} copy(bf16[16,128,256]{1,2,0:T(8,128)(2,1)} %get-tuple-element.102) | data formatting | bytes 2097152 | tf_op jit(solution)/shard_map/concatenate | solution.py:280
  22.9 1.8 %all-to-all-done.refs_9_ = bf16[4,256,256]{2,1,0:T(8,128)(2,1)S(1)} async-done(((bf16[4,256,256]{2,1,0:T(8,128)(2,1)}), bf16[4,256,256]{2,1,0:T(8,128)(2,1)S(1)}, u32[]{:S(2)}, u32[]{:S(2)}) %all-to-all-start) | async-done | bytes 524320 | tf_op jit(solution)/shard_map/all_to_all | solution.py:44
  24.6 2.2 %collective-permute-done.7 = bf16[256,256]{1,0:T(8,128)(2,1)S(1)} collective-permute-done((bf16[256,256]{1,0:T(8,128)(2,1)S(1)}, bf16[256,256]{1,0:T(8,128)(2,1)S(1)}, u32[]{:S(2)}, u32[]{:S(2)}) %collective-permute-start.7) | collective-permute-done | bytes 131104 | tf_op jit(solution)/shard_map/ppermute | solution.py:34
  26.8 1.2 %collective-permute-done.8 = bf16[256,256]{1,0:T(8,128)(2,1)} collective-permute-done((bf16[256,256]{1,0:T(8,128)(2,1)S(1)}, bf16[256,256]{1,0:T(8,128)(2,1)}, u32[]{:S(2)}, u32[]{:S(2)}) %collective-permute-start.8) | collective-permute-done | bytes 131104 | tf_op jit(solution)/shard_map/ppermute | solution.py:34
  28.0 1.0 pad_maximum_fusion.1.refs_10_
  29.0 3.0 %collective-permute-start.10 = (bf16[4,256,256]{2,1,0:T(8,128)(2,1)S(1)}, bf16[4,256,256]{2,1,0:T(8,128)(2,1)S(1)}, u32[]{:S(2)}, u32[]{:S(2)}) collective-permute-start(bf16[4,256,256]{2,1,0:T(8,128)(2,1)S(1)} %pad_maximum_fusion.1.refs_10_), channel_id=1, source_target_pairs={{16,0},{18,2},{20,4},{22,6},{24,8},{26,10},{28,12},{30,14},{32,16}... | collective-permute-start | bytes 1572872 | tf_op jit(solution)/shard_map/ppermute | solution.py:34
  32.0 3.2 %collective-permute-start.9 = (bf16[4,256,256]{2,1,0:T(8,128)(2,1)S(1)}, bf16[4,256,256]{2,1,0:T(8,128)(2,1)S(1)}, u32[]{:S(2)}, u32[]{:S(2)}) collective-permute-start(bf16[4,256,256]{2,1,0:T(8,128)(2,1)S(1)} %all-to-all-done.refs_9_), channel_id=1, source_target_pairs={{4,0},{6,2},{8,4},{10,6},{12,8},{14,10},{0,12},{2,14},{20,16},{22,... | collective-permute-start | bytes 1572872 | tf_op jit(solution)/shard_map/ppermute | solution.py:34
  35.3 6.6 %shard_map.104 = (bf16[4,256,256]{2,1,0:T(8,128)(2,1)S(1)}, bf16[4,256,256]{2,1,0:T(8,128)(2,1)S(1)}, f32[16,128,256]{2,1,0:T(8,128)S(1)}) custom-call(s32[1]{0:T(128)} %bitcast.refs_0_, s32[1,256]{1,0:T(1,128)S(1)} %fusion.11.refs_1_, s32[1,256]{1,0:T(1,128)S(1)} %collective-permute-done.1.refs_2_, s32[1,64]{1,0:T(1,128)S(1)} %copy-done.2, ...), custom_call_target="tpu_custom_call" | custom-call | flops 6442450944 | bytes 8388608 | tf_op jit(solution)/shard_map/pallas_call | solution.py:215
  41.9 0.8 copy-done
  43.0 3.4 %collective-permute-done.12.refs_12_ = bf16[4,256,256]{2,1,0:T(8,128)(2,1)S(1)} collective-permute-done((bf16[4,256,256]{2,1,0:T(8,128)(2,1)S(1)}, bf16[4,256,256]{2,1,0:T(8,128)(2,1)S(1)}, u32[]{:S(2)}, u32[]{:S(2)}) %collective-permute-start.12) | collective-permute-done | bytes 524320 | tf_op jit(solution)/shard_map/ppermute | solution.py:34
  46.4 1.5 %collective-permute-start.13 = (bf16[4,256,256]{2,1,0:T(8,128)(2,1)S(1)}, bf16[4,256,256]{2,1,0:T(8,128)(2,1)S(1)}, u32[]{:S(2)}, u32[]{:S(2)}) collective-permute-start(bf16[4,256,256]{2,1,0:T(8,128)(2,1)S(1)} %all-to-all-done.refs_9_), channel_id=1, source_target_pairs={{8,0},{10,2},{12,4},{14,6},{0,8},{2,10},{4,12},{6,14},{24,16},{26,... | collective-permute-start | bytes 1572872 | tf_op jit(solution)/shard_map/ppermute | solution.py:34
  47.9 2.0 %collective-permute-start.14 = (bf16[4,256,256]{2,1,0:T(8,128)(2,1)S(1)}, bf16[4,256,256]{2,1,0:T(8,128)(2,1)S(1)}, u32[]{:S(2)}, u32[]{:S(2)}) collective-permute-start(bf16[4,256,256]{2,1,0:T(8,128)(2,1)S(1)} %pad_maximum_fusion.1.refs_10_), channel_id=1, source_target_pairs={{32,0},{34,2},{36,4},{38,6},{40,8},{42,10},{44,12},{46,14},{48,16}... | collective-permute-start | bytes 1572872 | tf_op jit(solution)/shard_map/ppermute | solution.py:34
  49.9 12.3 %shard_map.105 = (bf16[4,256,256]{2,1,0:T(8,128)(2,1)S(1)}, bf16[4,256,256]{2,1,0:T(8,128)(2,1)S(1)}, bf16[4,256,256]{2,1,0:T(8,128)(2,1)S(1)}, bf16[4,256,256]{2,1,0:T(8,128)(2,1)S(1)}, f32[16,128,256]{2,1,0:T(8,128)S(1)}) custom-call(s32[1]{0:T(128)} %bitcast.refs_0_, s32[1,256]{1,0:T(1,128)S(1)} %fusion.11.refs_1_, ...), custom_call_target="tpu_custom_call" | custom-call | flops 12884901888 | bytes 16777216 | tf_op jit(solution)/shard_map/pallas_call | solution.py:215
  62.3 2.6 %collective-permute-start.15 = (bf16[4,256,256]{2,1,0:T(8,128)(2,1)S(1)}, bf16[4,256,256]{2,1,0:T(8,128)(2,1)S(1)}, u32[]{:S(2)}, u32[]{:S(2)}) collective-permute-start(bf16[4,256,256]{2,1,0:T(8,128)(2,1)S(1)} %get-tuple-element.69), channel_id=1, source_target_pairs={{12,0},{14,2},{0,4},{2,6},{4,8},{6,10},{8,12},{10,14},{28,16},{30,... | collective-permute-start | bytes 1572872 | tf_op jit(solution)/shard_map/ppermute | solution.py:34
  64.9 0.7 collective-permute-start.16
  65.6 1.8 %collective-permute-start.17 = (bf16[4,256,256]{2,1,0:T(8,128)(2,1)S(1)}, bf16[4,256,256]{2,1,0:T(8,128)(2,1)S(1)}, u32[]{:S(2)}, u32[]{:S(2)}) collective-permute-start(bf16[4,256,256]{2,1,0:T(8,128)(2,1)S(1)} %get-tuple-element.71), channel_id=1, source_target_pairs={{48,0},{50,2},{52,4},{54,6},{56,8},{58,10},{60,12},{62,14},{0,16},... | collective-permute-start | bytes 1572872 | tf_op jit(solution)/shard_map/ppermute | solution.py:34
  67.3 1.5 %collective-permute-start.18 = (bf16[4,256,256]{2,1,0:T(8,128)(2,1)S(1)}, bf16[4,256,256]{2,1,0:T(8,128)(2,1)S(1)}, u32[]{:S(2)}, u32[]{:S(2)}) collective-permute-start(bf16[4,256,256]{2,1,0:T(8,128)(2,1)S(1)} %get-tuple-element.72), channel_id=1, source_target_pairs={{16,0},{18,2},{20,4},{22,6},{24,8},{26,10},{28,12},{30,14},{32,16}... | collective-permute-start | bytes 1572872 | tf_op jit(solution)/shard_map/ppermute | solution.py:34
  68.8 7.6 %shard_map.106 = (bf16[4,256,256]{2,1,0:T(8,128)(2,1)}, bf16[4,256,256]{2,1,0:T(8,128)(2,1)}, f32[8,128,256]{2,1,0:T(8,128)S(1)}, bf16[8,128,256]{2,1,0:T(8,128)(2,1)S(1)}) custom-call(s32[1]{0:T(128)} %bitcast.refs_0_, s32[1,256]{1,0:T(1,128)S(1)} %fusion.11.refs_1_, s32[1,256]{1,0:T(1,128)S(1)} %collective-permute-done.1.refs_2_, s32[1,64]{1,0:T(1,128)S(1)} %copy-done.2, ...), custom_call_target="tpu_custom_call" | custom-call | flops 6442450944 | bytes 8388608 | tf_op jit(solution)/shard_map/pallas_call | solution.py:215
  76.6 2.7 %collective-permute-done.17 = bf16[4,256,256]{2,1,0:T(8,128)(2,1)S(1)} collective-permute-done((bf16[4,256,256]{2,1,0:T(8,128)(2,1)S(1)}, bf16[4,256,256]{2,1,0:T(8,128)(2,1)S(1)}, u32[]{:S(2)}, u32[]{:S(2)}) %collective-permute-start.17) | collective-permute-done | bytes 524320 | tf_op jit(solution)/shard_map/ppermute | solution.py:34
  79.2 1.7 %collective-permute-start.25 = (bf16[4,256,256]{2,1,0:T(8,128)(2,1)}, bf16[4,256,256]{2,1,0:T(8,128)(2,1)}, u32[]{:S(2)}, u32[]{:S(2)}) collective-permute-start(bf16[4,256,256]{2,1,0:T(8,128)(2,1)} %get-tuple-element.89), channel_id=1, source_target_pairs={{32,0},{34,2},{36,4},{38,6},{40,8},{42,10},{44,12},{46,14},{48,16}... | collective-permute-start | bytes 1572872 | tf_op jit(solution)/shard_map/ppermute | solution.py:34
  81.1 1.9 %collective-permute-start.21 = (bf16[8,128,256]{2,1,0:T(8,128)(2,1)S(1)}, bf16[8,128,256]{2,1,0:T(8,128)(2,1)}, u32[]{:S(2)}, u32[]{:S(2)}) collective-permute-start(bf16[8,128,256]{2,1,0:T(8,128)(2,1)S(1)} %add_convert_fusion), channel_id=1, source_target_pairs={{0,1},{1,0},{2,3},{3,2},{4,5},{5,4},{6,7},{7,6},{8,9},{9,8},{10,11... | collective-permute-start | bytes 1572872 | tf_op jit(solution)/shard_map/ppermute | solution.py:330
  83.0 0.8 copy.25
  83.9 1.8 %copy.24 = f32[256,256]{0,1:T(8,128)} copy(f32[256,256]{1,0:T(8,128)} %param.12) | data formatting | bytes 524288 | tf_op args[3]
  85.7 8.5 %collective-permute-done.25 = bf16[4,256,256]{2,1,0:T(8,128)(2,1)} collective-permute-done((bf16[4,256,256]{2,1,0:T(8,128)(2,1)}, bf16[4,256,256]{2,1,0:T(8,128)(2,1)}, u32[]{:S(2)}, u32[]{:S(2)}) %collective-permute-start.25) | collective-permute-done | bytes 524320 | tf_op jit(solution)/shard_map/ppermute | solution.py:34
  94.2 1.5 %fusion.8 = (bf16[256,256]{1,0:T(8,128)(2,1)S(1)}, bf16[256,256]{1,0:T(8,128)(2,1)S(1)}, bf16[256,256]{1,0:T(8,128)(2,1)S(1)}) fusion(bf16[4,256,256]{2,1,0:T(8,128)(2,1)} %collective-permute-done.25, bf16[4,256,256]{2,1,0:T(8,128)(2,1)} %copy-done.12, bf16[4,256,256]{2,1,0:T(8,128)(2,1)} %copy-done.11, bf16[4,256,256]{2,1,0:T(8,128)(2,1)S(1)} %copy-done.1), kind=kLoop, calls=%fused_computation.25 | loop fusion | flops 1572864 | bytes 1966080 | tf_op jit(solution)/shard_map/add | solution.py:246
  95.7 1.3 %collective-permute-start.26 = (bf16[256,256]{1,0:T(8,128)(2,1)S(1)}, bf16[256,256]{1,0:T(8,128)(2,1)S(1)}, u32[]{:S(2)}, u32[]{:S(2)}) collective-permute-start(bf16[256,256]{1,0:T(8,128)(2,1)S(1)} %get-tuple-element.94), channel_id=1, source_target_pairs={{12,0},{14,2},{0,4},{2,6},{4,8},{6,10},{8,12},{10,14},{28,16},{30,... | collective-permute-start | bytes 393224 | tf_op jit(solution)/shard_map/ppermute | solution.py:34
  97.4 2.5 %collective-permute-start.28 = (bf16[256,256]{1,0:T(8,128)(2,1)S(1)}, bf16[256,256]{1,0:T(8,128)(2,1)S(1)}, u32[]{:S(2)}, u32[]{:S(2)}) collective-permute-start(bf16[256,256]{1,0:T(8,128)(2,1)S(1)} %get-tuple-element.95), channel_id=1, source_target_pairs={{4,0},{6,2},{8,4},{10,6},{12,8},{14,10},{0,12},{2,14},{20,16},{22,... | collective-permute-start | bytes 393224 | tf_op jit(solution)/shard_map/ppermute | solution.py:34
  100.0 1.5 %fusion.6 = (bf16[256,256]{1,0:T(8,128)(2,1)S(1)}, bf16[256,256]{1,0:T(8,128)(2,1)S(1)}, bf16[256,256]{1,0:T(8,128)(2,1)S(1)}, bf16[256,256]{1,0:T(8,128)(2,1)S(1)}) fusion(bf16[4,256,256]{2,1,0:T(8,128)(2,1)S(1)} %collective-permute-done.20, bf16[4,256,256]{2,1,0:T(8,128)(2,1)} %copy-done.10, bf16[4,256,256]{2,1,0:T(8,128)(2,1)} %copy-done.9, ...), kind=kLoop, calls=%fused_computation.23 | loop fusion | flops 2097152 | bytes 2621440 | tf_op jit(solution)/shard_map/add | solution.py:246
  101.9 1.5 %collective-permute-start.23 = (bf16[256,256]{1,0:T(8,128)(2,1)S(1)}, bf16[256,256]{1,0:T(8,128)(2,1)S(1)}, u32[]{:S(2)}, u32[]{:S(2)}) collective-permute-start(bf16[256,256]{1,0:T(8,128)(2,1)S(1)} %get-tuple-element.84), channel_id=1, source_target_pairs={{32,0},{34,2},{36,4},{38,6},{40,8},{42,10},{44,12},{46,14},{48,16}... | collective-permute-start | bytes 393224 | tf_op jit(solution)/shard_map/ppermute | solution.py:34
  103.4 1.3 %add_multiply_fusion = f32[8,128,256]{2,1,0:T(8,128)S(1)} fusion(bf16[8,128,256]{2,1,0:T(8,128)(2,1)} %collective-permute-done.21, bf16[8,128,256]{2,1,0:T(8,128)(2,1)} %copy-done.4), kind=kLoop, calls=%fused_computation.3 | loop fusion | flops 1048576 | bytes 2097152 | tf_op jit(solution)/shard_map/div | solution.py:48
  104.8 1.5 %collective-permute-start.24 = (bf16[256,256]{1,0:T(8,128)(2,1)S(1)}, bf16[256,256]{1,0:T(8,128)(2,1)S(1)}, u32[]{:S(2)}, u32[]{:S(2)}) collective-permute-start(bf16[256,256]{1,0:T(8,128)(2,1)S(1)} %get-tuple-element.85), channel_id=1, source_target_pairs={{16,0},{18,2},{20,4},{22,6},{24,8},{26,10},{28,12},{30,14},{32,16}... | collective-permute-start | bytes 393224 | tf_op jit(solution)/shard_map/ppermute | solution.py:34
  106.3 1.2 %fusion.2 = bf16[256,256]{1,0:T(8,128)(2,1)S(1)} fusion(bf16[256,256]{1,0:T(8,128)(2,1)S(1)} %collective-permute-done.28, bf16[256,256]{1,0:T(8,128)(2,1)S(1)} %collective-permute-done.27, bf16[256,256]{1,0:T(8,128)(2,1)S(1)} %collective-permute-done.26, bf16[4,256,256]{2,1,0:T(8,128)(2,1)} %collective-permute-done.25, bf16[4,256,256]{2,1,0:T(8,128)(2,1)} %copy-done.12, ...), kind=kLoop, calls=%fused_computation.9 | loop fusion | flops 1048576 | bytes 1048576 | tf_op jit(solution)/shard_map/convert_element_type | solution.py:339
  107.4 0.8 collective-permute-start.29
  108.2 1.2 %multiply_subtract_fusion = f32[1024,256]{1,0:T(8,128)} fusion(f32[1024,256]{1,0:T(8,128)S(1)} %copy-done.3, f32[1024,256]{1,0:T(8,128)S(1)} %copy-done.8, f32[8,128,256]{2,1,0:T(8,128)S(1)} %add_multiply_fusion), kind=kLoop, calls=%fused_computation.2 | loop fusion | flops 1835008 | bytes 4194304 | tf_op jit(solution)/shard_map/sub | solution.py:50
  109.6 0.6 collective-permute-done.24
  110.2 2.3 %collective-permute-done.29 = bf16[256,256]{1,0:T(8,128)(2,1)S(1)} collective-permute-done((bf16[256,256]{1,0:T(8,128)(2,1)S(1)}, bf16[256,256]{1,0:T(8,128)(2,1)S(1)}, u32[]{:S(2)}, u32[]{:S(2)}) %collective-permute-start.29) | collective-permute-done | bytes 131104 | tf_op jit(solution)/shard_map/ppermute | solution.py:34
  112.6 0.8 copy.26
  (61 shorter events, 3.3 us)
Async XLA Ops:
  0.6 34.6 %copy-start.2 = (s32[1,64]{1,0:T(1,128)S(1)}, s32[1,64]{1,0:T(1,128)}, u32[]{:S(2)}) copy-start(s32[1,64]{1,0:T(1,128)} %refs_3_.5) | copy-start | bytes 772
  3.2 6.0 %collective-permute-start.3 = (bf16[8,128,256]{1,2,0:T(8,128)(2,1)S(1)}, bf16[8,128,256]{1,2,0:T(8,128)(2,1)S(1)}, u32[]{:S(2)}, u32[]{:S(2)}) collective-permute-start(bf16[8,128,256]{1,2,0:T(8,128)(2,1)S(1)} %copy.18), channel_id=1, source_target_pairs={{2,0},{0,2},{6,4},{4,6},{10,8},{8,10},{14,12},{12,14},{18,16},{16,... | collective-permute-start | bytes 1572872 | tf_op jit(solution)/shard_map/ppermute | solution.py:34
  3.3 5.9 %collective-permute-start = (bf16[256,256]{1,0:T(8,128)(2,1)S(1)}, bf16[256,256]{1,0:T(8,128)(2,1)S(1)}, u32[]{:S(2)}, u32[]{:S(2)}) collective-permute-start(bf16[256,256]{1,0:T(8,128)(2,1)S(1)} %convert_element_type.184), channel_id=1, source_target_pairs={{64,0},{66,2},{68,4},{70,6},{72,8},{74,10},{76,12},{78,14},{80,16}... | collective-permute-start | bytes 393224 | tf_op jit(solution)/shard_map/ppermute | solution.py:34
  4.5 1.5 %collective-permute-start.1 = (s32[1,256]{1,0:T(1,128)S(1)}, s32[1,256]{1,0:T(1,128)S(1)}, u32[]{:S(2)}, u32[]{:S(2)}) collective-permute-start(s32[1,256]{1,0:T(1,128)S(1)} %fusion.11.refs_1_), channel_id=1, source_target_pairs={{2,0},{0,2},{6,4},{4,6},{10,8},{8,10},{14,12},{12,14},{18,16},{16,... | collective-permute-start | bytes 3080 | tf_op jit(solution)/shard_map/ppermute | solution.py:34
  4.7 1.3 %collective-permute-start.2 = (s32[1,64]{1,0:T(1,128)}, s32[1,64]{1,0:T(1,128)S(1)}, u32[]{:S(2)}, u32[]{:S(2)}) collective-permute-start(s32[1,64]{1,0:T(1,128)} %refs_3_.5), channel_id=1, source_target_pairs={{2,0},{0,2},{6,4},{4,6},{10,8},{8,10},{14,12},{12,14},{18,16},{16,... | collective-permute-start | bytes 776 | tf_op jit(solution)/shard_map/ppermute | solution.py:34
  9.2 22.8 %collective-permute-start.4 = (bf16[32,2,4,128,128]{4,3,2,1,0:T(8,128)(2,1)}, bf16[32,2,4,128,128]{4,3,2,1,0:T(8,128)(2,1)}, u32[]{:S(2)}, u32[]{:S(2)}) collective-permute-start(bf16[32,2,4,128,128]{4,3,2,1,0:T(8,128)(2,1)} %bitcast.37), channel_id=1, source_target_pairs={{2,0},{0,2},{6,4},{4,6},{10,8},{8,10},{14,12},{12,14},{18,16},{16,... | collective-permute-start | bytes 25165832 | tf_op jit(solution)/shard_map/ppermute | solution.py:34
  9.2 26.1 %collective-permute-start.5 = (bf16[32,2,4,128,128]{4,3,2,1,0:T(8,128)(2,1)}, bf16[32,2,4,128,128]{4,3,2,1,0:T(8,128)(2,1)}, u32[]{:S(2)}, u32[]{:S(2)}) collective-permute-start(bf16[32,2,4,128,128]{4,3,2,1,0:T(8,128)(2,1)} %bitcast.41), channel_id=1, source_target_pairs={{2,0},{0,2},{6,4},{4,6},{10,8},{8,10},{14,12},{12,14},{18,16},{16,... | collective-permute-start | bytes 25165832 | tf_op jit(solution)/shard_map/ppermute | solution.py:34
  10.5 14.1 %all-to-all-start = ((bf16[4,256,256]{2,1,0:T(8,128)(2,1)}), bf16[4,256,256]{2,1,0:T(8,128)(2,1)S(1)}, u32[]{:S(2)}, u32[]{:S(2)}) async-start(bf16[4,256,256]{2,1,0:T(8,128)(2,1)} %broadcast_in_dim.9), calls=%async_computation | async-start | bytes 1048576 | tf_op jit(solution)/shard_map/all_to_all | solution.py:44
  15.0 9.6 %collective-permute-start.6 = (bf16[256,256]{1,0:T(8,128)(2,1)S(1)}, bf16[256,256]{1,0:T(8,128)(2,1)S(1)}, u32[]{:S(2)}, u32[]{:S(2)}) collective-permute-start(bf16[256,256]{1,0:T(8,128)(2,1)S(1)} %collective-permute-done), channel_id=1, source_target_pairs={{4,0},{6,2},{8,4},{10,6},{12,8},{14,10},{0,12},{2,14},{20,16},{22,... | collective-permute-start | bytes 393224 | tf_op jit(solution)/shard_map/ppermute | solution.py:34
  19.0 7.8 %collective-permute-start.7 = (bf16[256,256]{1,0:T(8,128)(2,1)S(1)}, bf16[256,256]{1,0:T(8,128)(2,1)S(1)}, u32[]{:S(2)}, u32[]{:S(2)}) collective-permute-start(bf16[256,256]{1,0:T(8,128)(2,1)S(1)} %collective-permute-done), channel_id=1, source_target_pairs={{8,0},{10,2},{12,4},{14,6},{0,8},{2,10},{4,12},{6,14},{24,16},{26,... | collective-permute-start | bytes 393224 | tf_op jit(solution)/shard_map/ppermute | solution.py:34
  19.0 9.0 %collective-permute-start.8 = (bf16[256,256]{1,0:T(8,128)(2,1)S(1)}, bf16[256,256]{1,0:T(8,128)(2,1)}, u32[]{:S(2)}, u32[]{:S(2)}) collective-permute-start(bf16[256,256]{1,0:T(8,128)(2,1)S(1)} %collective-permute-done), channel_id=1, source_target_pairs={{12,0},{14,2},{0,4},{2,6},{4,8},{6,10},{8,12},{10,14},{28,16},{30,... | collective-permute-start | bytes 393224 | tf_op jit(solution)/shard_map/ppermute | solution.py:34
  29.0 14.0 %collective-permute-start.10 = (bf16[4,256,256]{2,1,0:T(8,128)(2,1)S(1)}, bf16[4,256,256]{2,1,0:T(8,128)(2,1)S(1)}, u32[]{:S(2)}, u32[]{:S(2)}) collective-permute-start(bf16[4,256,256]{2,1,0:T(8,128)(2,1)S(1)} %pad_maximum_fusion.1.refs_10_), channel_id=1, source_target_pairs={{16,0},{18,2},{20,4},{22,6},{24,8},{26,10},{28,12},{30,14},{32,16}... | collective-permute-start | bytes 1572872 | tf_op jit(solution)/shard_map/ppermute | solution.py:34
  32.0 14.4 %collective-permute-start.12 = (bf16[4,256,256]{2,1,0:T(8,128)(2,1)S(1)}, bf16[4,256,256]{2,1,0:T(8,128)(2,1)S(1)}, u32[]{:S(2)}, u32[]{:S(2)}) collective-permute-start(bf16[4,256,256]{2,1,0:T(8,128)(2,1)S(1)} %pad_maximum_fusion.1.refs_10_), channel_id=1, source_target_pairs={{48,0},{50,2},{52,4},{54,6},{56,8},{58,10},{60,12},{62,14},{0,16},... | collective-permute-start | bytes 1572872 | tf_op jit(solution)/shard_map/ppermute | solution.py:34
  32.0 14.4 %collective-permute-start.11 = (bf16[4,256,256]{2,1,0:T(8,128)(2,1)S(1)}, bf16[4,256,256]{2,1,0:T(8,128)(2,1)S(1)}, u32[]{:S(2)}, u32[]{:S(2)}) collective-permute-start(bf16[4,256,256]{2,1,0:T(8,128)(2,1)S(1)} %all-to-all-done.refs_9_), channel_id=1, source_target_pairs={{12,0},{14,2},{0,4},{2,6},{4,8},{6,10},{8,12},{10,14},{28,16},{30,... | collective-permute-start | bytes 1572872 | tf_op jit(solution)/shard_map/ppermute | solution.py:34
  32.0 14.4 %collective-permute-start.9 = (bf16[4,256,256]{2,1,0:T(8,128)(2,1)S(1)}, bf16[4,256,256]{2,1,0:T(8,128)(2,1)S(1)}, u32[]{:S(2)}, u32[]{:S(2)}) collective-permute-start(bf16[4,256,256]{2,1,0:T(8,128)(2,1)S(1)} %all-to-all-done.refs_9_), channel_id=1, source_target_pairs={{4,0},{6,2},{8,4},{10,6},{12,8},{14,10},{0,12},{2,14},{20,16},{22,... | collective-permute-start | bytes 1572872 | tf_op jit(solution)/shard_map/ppermute | solution.py:34
  41.9 0.8 copy-start
  46.4 20.9 %collective-permute-start.13 = (bf16[4,256,256]{2,1,0:T(8,128)(2,1)S(1)}, bf16[4,256,256]{2,1,0:T(8,128)(2,1)S(1)}, u32[]{:S(2)}, u32[]{:S(2)}) collective-permute-start(bf16[4,256,256]{2,1,0:T(8,128)(2,1)S(1)} %all-to-all-done.refs_9_), channel_id=1, source_target_pairs={{8,0},{10,2},{12,4},{14,6},{0,8},{2,10},{4,12},{6,14},{24,16},{26,... | collective-permute-start | bytes 1572872 | tf_op jit(solution)/shard_map/ppermute | solution.py:34
  47.9 20.9 %collective-permute-start.14 = (bf16[4,256,256]{2,1,0:T(8,128)(2,1)S(1)}, bf16[4,256,256]{2,1,0:T(8,128)(2,1)S(1)}, u32[]{:S(2)}, u32[]{:S(2)}) collective-permute-start(bf16[4,256,256]{2,1,0:T(8,128)(2,1)S(1)} %pad_maximum_fusion.1.refs_10_), channel_id=1, source_target_pairs={{32,0},{34,2},{36,4},{38,6},{40,8},{42,10},{44,12},{46,14},{48,16}... | collective-permute-start | bytes 1572872 | tf_op jit(solution)/shard_map/ppermute | solution.py:34
  62.3 14.3 %collective-permute-start.15 = (bf16[4,256,256]{2,1,0:T(8,128)(2,1)S(1)}, bf16[4,256,256]{2,1,0:T(8,128)(2,1)S(1)}, u32[]{:S(2)}, u32[]{:S(2)}) collective-permute-start(bf16[4,256,256]{2,1,0:T(8,128)(2,1)S(1)} %get-tuple-element.69), channel_id=1, source_target_pairs={{12,0},{14,2},{0,4},{2,6},{4,8},{6,10},{8,12},{10,14},{28,16},{30,... | collective-permute-start | bytes 1572872 | tf_op jit(solution)/shard_map/ppermute | solution.py:34
  64.9 11.7 %collective-permute-start.16 = (bf16[4,256,256]{2,1,0:T(8,128)(2,1)S(1)}, bf16[4,256,256]{2,1,0:T(8,128)(2,1)S(1)}, u32[]{:S(2)}, u32[]{:S(2)}) collective-permute-start(bf16[4,256,256]{2,1,0:T(8,128)(2,1)S(1)} %get-tuple-element.70), channel_id=1, source_target_pairs={{4,0},{6,2},{8,4},{10,6},{12,8},{14,10},{0,12},{2,14},{20,16},{22,... | collective-permute-start | bytes 1572872 | tf_op jit(solution)/shard_map/ppermute | solution.py:34
  65.6 13.6 %collective-permute-start.17 = (bf16[4,256,256]{2,1,0:T(8,128)(2,1)S(1)}, bf16[4,256,256]{2,1,0:T(8,128)(2,1)S(1)}, u32[]{:S(2)}, u32[]{:S(2)}) collective-permute-start(bf16[4,256,256]{2,1,0:T(8,128)(2,1)S(1)} %get-tuple-element.71), channel_id=1, source_target_pairs={{48,0},{50,2},{52,4},{54,6},{56,8},{58,10},{60,12},{62,14},{0,16},... | collective-permute-start | bytes 1572872 | tf_op jit(solution)/shard_map/ppermute | solution.py:34
  67.3 11.9 %collective-permute-start.18 = (bf16[4,256,256]{2,1,0:T(8,128)(2,1)S(1)}, bf16[4,256,256]{2,1,0:T(8,128)(2,1)S(1)}, u32[]{:S(2)}, u32[]{:S(2)}) collective-permute-start(bf16[4,256,256]{2,1,0:T(8,128)(2,1)S(1)} %get-tuple-element.72), channel_id=1, source_target_pairs={{16,0},{18,2},{20,4},{22,6},{24,8},{26,10},{28,12},{30,14},{32,16}... | collective-permute-start | bytes 1572872 | tf_op jit(solution)/shard_map/ppermute | solution.py:34
  68.8 14.2 %copy-start.5 = (f32[256,256]{1,0:T(8,128)S(1)}, f32[256,256]{1,0:T(8,128)}, u32[]{:S(2)}) copy-start(f32[256,256]{1,0:T(8,128)} %param.10) | copy-start | bytes 786436
  68.8 25.4 %copy-start.1 = (bf16[4,256,256]{2,1,0:T(8,128)(2,1)S(1)}, bf16[4,256,256]{2,1,0:T(8,128)(2,1)}, u32[]{:S(2)}) copy-start(bf16[4,256,256]{2,1,0:T(8,128)(2,1)} %copy-done) | copy-start | bytes 1572868
  76.4 31.8 %copy-start.3 = (f32[1024,256]{1,0:T(8,128)S(1)}, f32[1024,256]{1,0:T(8,128)}, u32[]{:S(2)}) copy-start(f32[1024,256]{1,0:T(8,128)} %param.9) | copy-start | bytes 3145732
  76.4 2.8 %collective-permute-start.19 = (bf16[8,128,256]{2,1,0:T(8,128)(2,1)S(1)}, bf16[8,128,256]{2,1,0:T(8,128)(2,1)S(1)}, u32[]{:S(2)}, u32[]{:S(2)}) collective-permute-start(bf16[8,128,256]{2,1,0:T(8,128)(2,1)S(1)} %get-tuple-element.75), channel_id=1, source_target_pairs={{2,0},{0,2},{6,4},{4,6},{10,8},{8,10},{14,12},{12,14},{18,16},{16,... | collective-permute-start | bytes 1572872 | tf_op jit(solution)/shard_map/ppermute | solution.py:34
  76.5 4.5 %copy-start.9 = (bf16[4,256,256]{2,1,0:T(8,128)(2,1)}, bf16[4,256,256]{2,1,0:T(8,128)(2,1)S(1)}, u32[]{:S(2)}) copy-start(bf16[4,256,256]{2,1,0:T(8,128)(2,1)S(1)} %collective-permute-done.15) | copy-start | bytes 1572868
  76.5 4.5 %copy-start.10 = (bf16[4,256,256]{2,1,0:T(8,128)(2,1)}, bf16[4,256,256]{2,1,0:T(8,128)(2,1)S(1)}, u32[]{:S(2)}) copy-start(bf16[4,256,256]{2,1,0:T(8,128)(2,1)S(1)} %collective-permute-done.16) | copy-start | bytes 1572868
  79.2 1.9 %copy-start.11 = (bf16[4,256,256]{2,1,0:T(8,128)(2,1)}, bf16[4,256,256]{2,1,0:T(8,128)(2,1)S(1)}, u32[]{:S(2)}) copy-start(bf16[4,256,256]{2,1,0:T(8,128)(2,1)S(1)} %collective-permute-done.17) | copy-start | bytes 1572868
  79.2 1.9 %copy-start.12 = (bf16[4,256,256]{2,1,0:T(8,128)(2,1)}, bf16[4,256,256]{2,1,0:T(8,128)(2,1)S(1)}, u32[]{:S(2)}) copy-start(bf16[4,256,256]{2,1,0:T(8,128)(2,1)S(1)} %collective-permute-done.18) | copy-start | bytes 1572868
  79.2 15.0 %collective-permute-start.25 = (bf16[4,256,256]{2,1,0:T(8,128)(2,1)}, bf16[4,256,256]{2,1,0:T(8,128)(2,1)}, u32[]{:S(2)}, u32[]{:S(2)}) collective-permute-start(bf16[4,256,256]{2,1,0:T(8,128)(2,1)} %get-tuple-element.89), channel_id=1, source_target_pairs={{32,0},{34,2},{36,4},{38,6},{40,8},{42,10},{44,12},{46,14},{48,16}... | collective-permute-start | bytes 1572872 | tf_op jit(solution)/shard_map/ppermute | solution.py:34
  80.9 19.0 %collective-permute-start.20 = (bf16[4,256,256]{2,1,0:T(8,128)(2,1)}, bf16[4,256,256]{2,1,0:T(8,128)(2,1)S(1)}, u32[]{:S(2)}, u32[]{:S(2)}) collective-permute-start(bf16[4,256,256]{2,1,0:T(8,128)(2,1)} %get-tuple-element.80), channel_id=1, source_target_pairs={{8,0},{10,2},{12,4},{14,6},{0,8},{2,10},{4,12},{6,14},{24,16},{26,... | collective-permute-start | bytes 1572872 | tf_op jit(solution)/shard_map/ppermute | solution.py:34
  81.1 20.8 %copy-start.4 = (bf16[8,128,256]{2,1,0:T(8,128)(2,1)}, bf16[8,128,256]{2,1,0:T(8,128)(2,1)S(1)}, u32[]{:S(2)}) copy-start(bf16[8,128,256]{2,1,0:T(8,128)(2,1)S(1)} %add_convert_fusion) | copy-start | bytes 1572868
  81.1 20.4 %collective-permute-start.21 = (bf16[8,128,256]{2,1,0:T(8,128)(2,1)S(1)}, bf16[8,128,256]{2,1,0:T(8,128)(2,1)}, u32[]{:S(2)}, u32[]{:S(2)}) collective-permute-start(bf16[8,128,256]{2,1,0:T(8,128)(2,1)S(1)} %add_convert_fusion), channel_id=1, source_target_pairs={{0,1},{1,0},{2,3},{3,2},{4,5},{5,4},{6,7},{7,6},{8,9},{9,8},{10,11... | collective-permute-start | bytes 1572872 | tf_op jit(solution)/shard_map/ppermute | solution.py:330
  83.9 28.6 %copy-start.6 = (f32[256,256]{0,1:T(8,128)S(1)}, f32[256,256]{0,1:T(8,128)}, u32[]{:S(2)}) copy-start(f32[256,256]{0,1:T(8,128)} %copy.25) | copy-start | bytes 786436
  85.7 22.5 %copy-start.8 = (f32[1024,256]{1,0:T(8,128)S(1)}, f32[1024,256]{1,0:T(8,128)}, u32[]{:S(2)}) copy-start(f32[1024,256]{1,0:T(8,128)} %param.11) | copy-start | bytes 3145732
  85.7 26.8 %copy-start.7 = (f32[256,256]{0,1:T(8,128)S(1)}, f32[256,256]{0,1:T(8,128)}, u32[]{:S(2)}) copy-start(f32[256,256]{0,1:T(8,128)} %copy.24) | copy-start | bytes 786436
  95.7 9.1 %collective-permute-start.26 = (bf16[256,256]{1,0:T(8,128)(2,1)S(1)}, bf16[256,256]{1,0:T(8,128)(2,1)S(1)}, u32[]{:S(2)}, u32[]{:S(2)}) collective-permute-start(bf16[256,256]{1,0:T(8,128)(2,1)S(1)} %get-tuple-element.94), channel_id=1, source_target_pairs={{12,0},{14,2},{0,4},{2,6},{4,8},{6,10},{8,12},{10,14},{28,16},{30,... | collective-permute-start | bytes 393224 | tf_op jit(solution)/shard_map/ppermute | solution.py:34
  97.0 9.2 %collective-permute-start.27 = (bf16[256,256]{1,0:T(8,128)(2,1)S(1)}, bf16[256,256]{1,0:T(8,128)(2,1)S(1)}, u32[]{:S(2)}, u32[]{:S(2)}) collective-permute-start(bf16[256,256]{1,0:T(8,128)(2,1)S(1)} %get-tuple-element.96), channel_id=1, source_target_pairs={{8,0},{10,2},{12,4},{14,6},{0,8},{2,10},{4,12},{6,14},{24,16},{26,... | collective-permute-start | bytes 393224 | tf_op jit(solution)/shard_map/ppermute | solution.py:34
  97.4 8.8 %collective-permute-start.28 = (bf16[256,256]{1,0:T(8,128)(2,1)S(1)}, bf16[256,256]{1,0:T(8,128)(2,1)S(1)}, u32[]{:S(2)}, u32[]{:S(2)}) collective-permute-start(bf16[256,256]{1,0:T(8,128)(2,1)S(1)} %get-tuple-element.95), channel_id=1, source_target_pairs={{4,0},{6,2},{8,4},{10,6},{12,8},{14,10},{0,12},{2,14},{20,16},{22,... | collective-permute-start | bytes 393224 | tf_op jit(solution)/shard_map/ppermute | solution.py:34
  101.5 8.1 %collective-permute-start.22 = (bf16[256,256]{1,0:T(8,128)(2,1)S(1)}, bf16[256,256]{1,0:T(8,128)(2,1)S(1)}, u32[]{:S(2)}, u32[]{:S(2)}) collective-permute-start(bf16[256,256]{1,0:T(8,128)(2,1)S(1)} %get-tuple-element.83), channel_id=1, source_target_pairs={{48,0},{50,2},{52,4},{54,6},{56,8},{58,10},{60,12},{62,14},{0,16},... | collective-permute-start | bytes 393224 | tf_op jit(solution)/shard_map/ppermute | solution.py:34
  101.9 7.7 %collective-permute-start.23 = (bf16[256,256]{1,0:T(8,128)(2,1)S(1)}, bf16[256,256]{1,0:T(8,128)(2,1)S(1)}, u32[]{:S(2)}, u32[]{:S(2)}) collective-permute-start(bf16[256,256]{1,0:T(8,128)(2,1)S(1)} %get-tuple-element.84), channel_id=1, source_target_pairs={{32,0},{34,2},{36,4},{38,6},{40,8},{42,10},{44,12},{46,14},{48,16}... | collective-permute-start | bytes 393224 | tf_op jit(solution)/shard_map/ppermute | solution.py:34
  104.8 5.4 %collective-permute-start.24 = (bf16[256,256]{1,0:T(8,128)(2,1)S(1)}, bf16[256,256]{1,0:T(8,128)(2,1)S(1)}, u32[]{:S(2)}, u32[]{:S(2)}) collective-permute-start(bf16[256,256]{1,0:T(8,128)(2,1)S(1)} %get-tuple-element.85), channel_id=1, source_target_pairs={{16,0},{18,2},{20,4},{22,6},{24,8},{26,10},{28,12},{30,14},{32,16}... | collective-permute-start | bytes 393224 | tf_op jit(solution)/shard_map/ppermute | solution.py:34
  107.4 5.0 %collective-permute-start.29 = (bf16[256,256]{1,0:T(8,128)(2,1)S(1)}, bf16[256,256]{1,0:T(8,128)(2,1)S(1)}, u32[]{:S(2)}, u32[]{:S(2)}) collective-permute-start(bf16[256,256]{1,0:T(8,128)(2,1)S(1)} %fusion.2), channel_id=1, source_target_pairs={{64,0},{66,2},{68,4},{70,6},{72,8},{74,10},{76,12},{78,14},{80,16}... | collective-permute-start | bytes 393224 | tf_op jit(solution)/shard_map/ppermute | solution.py:34
